TPU v7x, 256 devices: a whole 4x4x8 slice. The times are simulated.
256 devices in a mesh: gx: 16 (over x, y), gy: 16 (over z, core).
Axes of the slice: x: 4, y: 4, z: 8, core: 2. Of those that a mesh axis runs over, the one named last changes fastest.
Arguments:
- level_set: float32 [512, 1024, 128], P('gx', 'gy'), may hold values from -6 to 6
- stress_jump: float32 [512, 1024, 128], P('gx', 'gy'), may hold values from -6 to 6
- materials: int32 [512, 1024, 128], P('gx', 'gy'), may hold values from 0 to 2
Outputs:
- new_level: float32 [512, 1024, 128], P('gx', 'gy')
- normal_speed: float32 [512, 1024, 128], P('gx', 'gy')
Inputs may be any that keep to these rules, and one draw needn't show every extreme that they name: `materials`: 0 marks magnet, 1 iron, 2 air.
All inputs are finite; a program needn't handle non-finite values. Where the computation divides by a largest or mean magnitude, that divisor is 1e-20 or more.
Results may differ from a plain program's by a relative error of at most 0.0003.
Values sent between devices are 32-bit elements; how exact they have to be, the bound alone decides.
No kernel may reach another device: no remote copies, remote signals or barrier semaphores. Data moves between devices by JAX's collectives and lax.ppermute only.
A program may use at most 64 MiB of HBM per device.

v0:
```python
import jax
import jax.numpy as jnp
from jax import lax
from jax.sharding import PartitionSpec as P

SWEEPS = 4
REINIT = 2


screening = 0.1
spectral_mid = screening + 6.0
spectral_half = 6.0
courant = 0.25
pseudo_step = 0.25
weno_floor = 1e-06


def with_halo(x, sides, width):
    for axis, dim in sides:
        size, length = (lax.axis_size(axis), x.shape[dim])
        up = [(i, (i + 1) % size) for i in range(size)]
        down = [(j, i) for i, j in up]
        last = lax.slice_in_dim(x, length - width, length, axis=dim)
        initial = lax.slice_in_dim(x, 0, width, axis=dim)
        before = lax.ppermute(last, axis, up)
        after = lax.ppermute(initial, axis, down)
        x = jnp.concatenate([before, x, after], axis=dim)
    return x


def material_weight(materials):
    return jnp.where(materials == 0, 1.0, jnp.where(materials == 1, 0.6, 0.0)).astype(jnp.float32)


def periodic_pad(field, along, margin):
    extent = field.shape[along]
    leading = lax.slice_in_dim(field, extent - margin, extent, axis=along)
    trailing = lax.slice_in_dim(field, 0, margin, axis=along)
    return jnp.concatenate([leading, field, trailing], axis=along)


def square_of(value):
    return value * value


def weno_side(stencil_a, stencil_b, stencil_c, stencil_d, stencil_e):
    smooth_a = 13.0 / 12.0 * square_of(stencil_a - 2.0 * stencil_b + stencil_c) + 0.25 * square_of(
        stencil_a - 4.0 * stencil_b + 3.0 * stencil_c
    )
    smooth_b = 13.0 / 12.0 * square_of(stencil_b - 2.0 * stencil_c + stencil_d) + 0.25 * square_of(
        stencil_b - stencil_d
    )
    smooth_c = 13.0 / 12.0 * square_of(stencil_c - 2.0 * stencil_d + stencil_e) + 0.25 * square_of(
        3.0 * stencil_c - 4.0 * stencil_d + stencil_e
    )
    weight_a = 0.1 / square_of(weno_floor + smooth_a)
    weight_b = 0.6 / square_of(weno_floor + smooth_b)
    weight_c = 0.3 / square_of(weno_floor + smooth_c)
    weight_sum = weight_a + weight_b + weight_c
    combined = weight_a * (stencil_a / 3.0 - 7.0 * stencil_b / 6.0 + 11.0 * stencil_c / 6.0)
    combined = combined + weight_b * (-stencil_b / 6.0 + 5.0 * stencil_c / 6.0 + stencil_d / 3.0)
    combined = combined + weight_c * (stencil_c / 3.0 + 5.0 * stencil_d / 6.0 - stencil_e / 6.0)
    return combined / weight_sum


def weno_pair(padded, along, extent):
    length = padded.shape[along]
    differences = lax.slice_in_dim(padded, 1, length, axis=along) - lax.slice_in_dim(
        padded, 0, length - 1, axis=along
    )
    pieces = [lax.slice_in_dim(differences, k, k + extent, axis=along) for k in range(6)]
    left_side = weno_side(pieces[0], pieces[1], pieces[2], pieces[3], pieces[4])
    right_side = weno_side(pieces[5], pieces[4], pieces[3], pieces[2], pieces[1])
    return (left_side, right_side)


def godunov_square(left_side, right_side, positive):
    upper = jnp.maximum(
        square_of(jnp.maximum(left_side, 0.0)), square_of(jnp.minimum(right_side, 0.0))
    )
    lower = jnp.maximum(
        square_of(jnp.minimum(left_side, 0.0)), square_of(jnp.maximum(right_side, 0.0))
    )
    return jnp.where(positive, upper, lower)


def apply_valid(padded):
    centre = padded[1:-1, 1:-1]
    beside = padded[2:, 1:-1] + padded[:-2, 1:-1]
    beside = beside + padded[1:-1, 2:] + padded[1:-1, :-2]
    beside = beside + jnp.roll(centre, 1, 2) + jnp.roll(centre, -1, 2)
    return spectral_mid * centre - beside


def rate_inner(padded, velocity):
    inner_x = padded.shape[0] - 6
    inner_y = padded.shape[1] - 6
    positive = velocity > 0
    left_side, right_side = weno_pair(padded[:, 3:-3], 0, inner_x)
    total = godunov_square(left_side, right_side, positive)
    left_side, right_side = weno_pair(padded[3:-3, :], 1, inner_y)
    total = total + godunov_square(left_side, right_side, positive)
    middle = padded[3:-3, 3:-3]
    left_side, right_side = weno_pair(periodic_pad(middle, 2, 3), 2, middle.shape[2])
    total = total + godunov_square(left_side, right_side, positive)
    return -velocity * jnp.sqrt(total)


def section_rate(level, velocity):
    padded = with_halo(level, (("gx", 0), ("gy", 1)), 3)
    return rate_inner(padded, velocity)


def sweep_valid(padded, sign_field):
    positive = sign_field > 0
    centre = padded[1:-1, 1:-1]
    total = godunov_square(centre - padded[:-2, 1:-1], padded[2:, 1:-1] - centre, positive)
    total = total + godunov_square(centre - padded[1:-1, :-2], padded[1:-1, 2:] - centre, positive)
    total = total + godunov_square(
        centre - jnp.roll(centre, 1, 2), jnp.roll(centre, -1, 2) - centre, positive
    )
    return centre - pseudo_step * sign_field * (jnp.sqrt(total) - 1.0)


def local(level_set, stress_jump, materials):
    source = material_weight(materials) * stress_jump
    ratio_now = spectral_half / spectral_mid
    iterate = jnp.zeros_like(source)
    residue = source
    search = source / spectral_mid
    for k in range(SWEEPS):
        applied = apply_valid(with_halo(search, (("gx", 0), ("gy", 1)), 1))
        iterate = iterate + search
        residue = residue - applied
        ratio_next = 1.0 / (2.0 * spectral_mid / spectral_half - ratio_now)
        search = ratio_next * ratio_now * search + 2.0 * ratio_next / spectral_half * residue
        ratio_now = ratio_next
    normal_speed = iterate + search
    peak_speed = lax.pmax(jnp.max(jnp.abs(normal_speed)), ("gx", "gy"))
    time_step = courant / (peak_speed + 1e-06)
    section_one = level_set + time_step * section_rate(level_set, normal_speed)
    advected = 0.5 * level_set + 0.5 * (
        section_one + time_step * section_rate(section_one, normal_speed)
    )
    sign_field = advected / jnp.sqrt(advected * advected + 1.0)
    current = advected
    for k in range(REINIT):
        current = sweep_valid(with_halo(current, (("gx", 0), ("gy", 1)), 1), sign_field)
    return (current, normal_speed)


def solution(mesh):
    in_specs = (P("gx", "gy", None), P("gx", "gy", None), P("gx", "gy", None))
    out_specs = (P("gx", "gy", None), P("gx", "gy", None))
    return jax.shard_map(local, mesh=mesh, in_specs=in_specs, out_specs=out_specs, check_vma=False)
```

profile of v0, /device:TPU:1, one launch (start us, length us, event | category | flops | bytes accessed | tf_op | source)
XLA Modules:
  0.0 222.4 jit_solution(8057829715410574709)
XLA Ops:
  0.6 1.9 broadcast_multiply_fusion
  2.5 5.8 %collective-permute-start = (f32[1,64,128]{2,1,0:T(8,128)S(1)}, f32[1,64,128]{2,1,0:T(8,128)S(1)}, u32[]{:S(2)}, u32[]{:S(2)}) collective-permute-start(f32[1,64,128]{2,1,0:T(8,128)S(1)} %get-tuple-element.63), channel_id=1, source_target_pairs={{16,0},{32,16},{48,32},{64,48},{80,64},{96,80},{112,96},{128,112},... | collective-permute-start | bytes 98312 | tf_op jit(solution)/shard_map/ppermute | solution.py:26
  8.5 4.9 %collective-permute-start.17 = (f32[3,64,128]{2,1,0:T(8,128)S(1)}, f32[3,64,128]{2,1,0:T(8,128)S(1)}, u32[]{:S(2)}, u32[]{:S(2)}) collective-permute-start(f32[3,64,128]{2,1,0:T(8,128)S(1)} %get-tuple-element.68), channel_id=1, source_target_pairs={{16,0},{32,16},{48,32},{64,48},{80,64},{96,80},{112,96},{128,112},... | collective-permute-start | bytes 294920 | tf_op jit(solution)/shard_map/ppermute | solution.py:26
  14.7 2.0 slice_subtract_fusion.1
  21.6 2.2 collective-permute-done.3
  28.0 4.7 %collective-permute-done.5 = f32[1,64,128]{2,1,0:T(8,128)S(1)} collective-permute-done((f32[1,64,128]{2,1,0:T(8,128)S(1)}, f32[1,64,128]{2,1,0:T(8,128)S(1)}, u32[]{:S(2)}, u32[]{:S(2)}) %collective-permute-start.5) | collective-permute-done | bytes 32800 | tf_op jit(solution)/shard_map/ppermute | solution.py:25
  32.7 5.1 %collective-permute-start.6 = (f32[34,1,128]{2,1,0:T(1,128)S(1)}, f32[34,1,128]{2,1,0:T(1,128)S(1)}, u32[]{:S(2)}, u32[]{:S(2)}) collective-permute-start(f32[34,1,128]{2,1,0:T(1,128)S(1)} %get-tuple-element.24), channel_id=1, source_target_pairs={{1,0},{2,1},{3,2},{4,3},{5,4},{6,5},{7,6},{8,7},{9,8},{10,9},{11,1... | collective-permute-start | bytes 52232 | tf_op jit(solution)/shard_map/ppermute | solution.py:26
  43.2 3.3 %collective-permute-done.9 = f32[1,64,128]{2,1,0:T(8,128)S(1)} collective-permute-done((f32[1,64,128]{2,1,0:T(8,128)S(1)}, f32[1,64,128]{2,1,0:T(8,128)S(1)}, u32[]{:S(2)}, u32[]{:S(2)}) %collective-permute-start.9) | collective-permute-done | bytes 32800 | tf_op jit(solution)/shard_map/ppermute | solution.py:25
  46.5 4.4 %collective-permute-start.10 = (f32[34,1,128]{2,1,0:T(1,128)S(1)}, f32[34,1,128]{2,1,0:T(1,128)S(1)}, u32[]{:S(2)}, u32[]{:S(2)}) collective-permute-start(f32[34,1,128]{2,1,0:T(1,128)S(1)} %get-tuple-element.22), channel_id=1, source_target_pairs={{1,0},{2,1},{3,2},{4,3},{5,4},{6,5},{7,6},{8,7},{9,8},{10,9},{11,1... | collective-permute-start | bytes 52232 | tf_op jit(solution)/shard_map/ppermute | solution.py:26
  56.7 3.4 %collective-permute-done.13 = f32[1,64,128]{2,1,0:T(8,128)S(1)} collective-permute-done((f32[1,64,128]{2,1,0:T(8,128)S(1)}, f32[1,64,128]{2,1,0:T(8,128)S(1)}, u32[]{:S(2)}, u32[]{:S(2)}) %collective-permute-start.13) | collective-permute-done | bytes 32800 | tf_op jit(solution)/shard_map/ppermute | solution.py:25
  60.1 4.4 %collective-permute-start.14 = (f32[34,1,128]{2,1,0:T(1,128)S(1)}, f32[34,1,128]{2,1,0:T(1,128)S(1)}, u32[]{:S(2)}, u32[]{:S(2)}) collective-permute-start(f32[34,1,128]{2,1,0:T(1,128)S(1)} %get-tuple-element.20), channel_id=1, source_target_pairs={{1,0},{2,1},{3,2},{4,3},{5,4},{6,5},{7,6},{8,7},{9,8},{10,9},{11,1... | collective-permute-start | bytes 52232 | tf_op jit(solution)/shard_map/ppermute | solution.py:26
  65.7 3.8 %abs_reduce_fusion = (f32[]{:T(128)}, f32[32,64,128]{2,1,0:T(8,128)}) fusion(f32[32,64,128]{2,1,0:T(8,128)S(1)} %get-tuple-element.5, f32[32,64,1]{2,1,0:T(8,128)S(1)} %get-tuple-element.47, f32[32,64,127]{2,1,0:T(8,128)S(1)} %get-tuple-element.49, f32[32,64,127]{2,1,0:T(8,128)S(1)} %get-tuple-element.48, f32[32,64,1]{2,1,0:T(8,128)S(1)} %get-tuple-element.46, ...), kind=kLoop, calls=%fused_computation.106 | loop fusion | flops 7340031 | bytes 8488964 | tf_op jit(solution)/shard_map/reduce_max | solution.py:139
  69.5 74.6 %pmax.7 = f32[]{:T(128)} all-reduce(f32[]{:T(128)} %get-tuple-element.2), channel_id=1, replica_groups=mesh['gx'=16,'gy'=16] {'gx','gy'}, use_global_device_ids=true, to_apply=%region_1.2 | all-reduce | flops 1 | bytes 8 | tf_op jit(solution)/shard_map/pmax | solution.py:139
  144.8 18.0 %multiply_add_fusion = f32[32,64,128]{2,1,0:T(8,128)S(1)} fusion(f32[32,64,128]{2,1,0:T(8,128)S(1)} %copy-done, f32[32,64,133]{2,1,0:T(8,128)} %slice_subtract_fusion.1, f32[32,69,128]{2,1,0:T(8,128)S(1)} %slice_subtract_fusion.5, f32[37,64,128]{2,1,0:T(8,128)S(1)} %slice_subtract_fusion.3, f32[32,64,128]{2,1,0:T(8,128)} %get-tuple-element.3, f32[]{:T(128)S(6)} %div.436), kind=kLoop, calls=%fused_computation.105 | loop fusion | flops 108003328 | bytes 22020100 | tf_op jit(solution)/shard_map/add | solution.py:141
  163.6 4.4 %collective-permute-start.21 = (f32[3,64,128]{2,1,0:T(8,128)S(1)}, f32[3,64,128]{2,1,0:T(8,128)S(1)}, u32[]{:S(2)}, u32[]{:S(2)}) collective-permute-start(f32[3,64,128]{2,1,0:T(8,128)S(1)} %get-tuple-element.41), channel_id=1, source_target_pairs={{16,0},{32,16},{48,32},{64,48},{80,64},{96,80},{112,96},{128,112},... | collective-permute-start | bytes 294920 | tf_op jit(solution)/shard_map/ppermute | solution.py:26
  170.0 2.5 %collective-permute-start.22 = (f32[38,3,128]{2,1,0:T(4,128)S(1)}, f32[38,3,128]{2,1,0:T(4,128)S(1)}, u32[]{:S(2)}, u32[]{:S(2)}) collective-permute-start(f32[38,3,128]{2,1,0:T(4,128)S(1)} %get-tuple-element.12), channel_id=1, source_target_pairs={{0,1},{1,2},{2,3},{3,4},{4,5},{5,6},{6,7},{7,8},{8,9},{9,10},{10,1... | collective-permute-start | bytes 175112 | tf_op jit(solution)/shard_map/ppermute | solution.py:25
  174.0 2.5 %collective-permute-done.23 = f32[38,3,128]{2,1,0:T(4,128)S(1)} collective-permute-done((f32[38,3,128]{2,1,0:T(4,128)S(1)}, f32[38,3,128]{2,1,0:T(4,128)S(1)}, u32[]{:S(2)}, u32[]{:S(2)}) %collective-permute-start.23) | collective-permute-done | bytes 58400 | tf_op jit(solution)/shard_map/ppermute | solution.py:26
  177.9 15.6 %add_multiply_fusion = f32[32,64,128]{2,1,0:T(8,128)S(1)} fusion(f32[32,64,128]{2,1,0:T(8,128)S(1)} %copy-done, f32[32,64,128]{2,1,0:T(8,128)S(1)} %multiply_add_fusion, f32[32,64,133]{2,1,0:T(8,128)S(1)} %slice_subtract_fusion, f32[32,69,128]{2,1,0:T(8,128)S(1)} %slice_subtract_fusion.4, f32[37,64,128]{2,1,0:T(8,128)S(1)} %slice_subtract_fusion.2, ...), kind=kLoop, calls=%fused_computation.104 | loop fusion | flops 108527616 | bytes 23068676 | tf_op jit(solution)/shard_map/add | solution.py:142
  193.6 5.1 %collective-permute-start.25 = (f32[1,64,128]{2,1,0:T(8,128)S(1)}, f32[1,64,128]{2,1,0:T(8,128)S(1)}, u32[]{:S(2)}, u32[]{:S(2)}) collective-permute-start(f32[1,64,128]{2,1,0:T(8,128)S(1)} %get-tuple-element.35), channel_id=1, source_target_pairs={{16,0},{32,16},{48,32},{64,48},{80,64},{96,80},{112,96},{128,112},... | collective-permute-start | bytes 98312 | tf_op jit(solution)/shard_map/ppermute | solution.py:26
  201.9 2.0 collective-permute-done.27
  203.9 3.5 %multiply_subtract_fusion.1 = f32[32,64,128]{2,1,0:T(8,128)S(1)} fusion(f32[32,64,128]{2,1,0:T(8,128)S(1)} %add_multiply_fusion, f32[32,64,1]{2,1,0:T(8,128)S(1)} %get-tuple-element.37, f32[32,64,127]{2,1,0:T(8,128)S(1)} %get-tuple-element.39, f32[32,64,127]{2,1,0:T(8,128)S(1)} %get-tuple-element.38, f32[32,64,1]{2,1,0:T(8,128)S(1)} %get-tuple-element.36, ...), kind=kLoop, calls=%fused_computation.102 | loop fusion | flops 15466496 | bytes 4294656 | tf_op jit(solution)/shard_map/sub | solution.py:122
  207.5 5.5 %collective-permute-start.29 = (f32[1,64,128]{2,1,0:T(8,128)S(1)}, f32[1,64,128]{2,1,0:T(8,128)S(1)}, u32[]{:S(2)}, u32[]{:S(2)}) collective-permute-start(f32[1,64,128]{2,1,0:T(8,128)S(1)} %get-tuple-element.29), channel_id=1, source_target_pairs={{16,0},{32,16},{48,32},{64,48},{80,64},{96,80},{112,96},{128,112},... | collective-permute-start | bytes 98312 | tf_op jit(solution)/shard_map/ppermute | solution.py:26
  215.0 1.8 collective-permute-start.31
  218.1 4.3 %multiply_subtract_fusion = f32[32,64,128]{2,1,0:T(8,128)} fusion(f32[32,64,128]{2,1,0:T(8,128)S(1)} %multiply_subtract_fusion.1, f32[32,64,1]{2,1,0:T(8,128)S(1)} %get-tuple-element.31, f32[32,64,127]{2,1,0:T(8,128)S(1)} %get-tuple-element.33, f32[32,64,127]{2,1,0:T(8,128)S(1)} %get-tuple-element.32, f32[32,64,1]{2,1,0:T(8,128)S(1)} %get-tuple-element.30, ...), kind=kLoop, calls=%fused_computation.101 | loop fusion | flops 15466496 | bytes 5343232 | tf_op jit(solution)/shard_map/sub | solution.py:122
  (98 shorter events, 35.1 us)
Async XLA Ops:
  2.5 14.5 %collective-permute-start = (f32[1,64,128]{2,1,0:T(8,128)S(1)}, f32[1,64,128]{2,1,0:T(8,128)S(1)}, u32[]{:S(2)}, u32[]{:S(2)}) collective-permute-start(f32[1,64,128]{2,1,0:T(8,128)S(1)} %get-tuple-element.63), channel_id=1, source_target_pairs={{16,0},{32,16},{48,32},{64,48},{80,64},{96,80},{112,96},{128,112},... | collective-permute-start | bytes 98312 | tf_op jit(solution)/shard_map/ppermute | solution.py:26
  8.4 8.7 %collective-permute-start.1 = (f32[1,64,128]{2,1,0:T(8,128)S(1)}, f32[1,64,128]{2,1,0:T(8,128)S(1)}, u32[]{:S(2)}, u32[]{:S(2)}) collective-permute-start(f32[1,64,128]{2,1,0:T(8,128)S(1)} %get-tuple-element.62), channel_id=1, source_target_pairs={{0,16},{16,32},{32,48},{48,64},{64,80},{80,96},{96,112},{112,128},... | collective-permute-start | bytes 98312 | tf_op jit(solution)/shard_map/ppermute | solution.py:25
  8.4 29.5 %collective-permute-start.16 = (f32[3,64,128]{2,1,0:T(8,128)S(1)}, f32[3,64,128]{2,1,0:T(8,128)S(1)}, u32[]{:S(2)}, u32[]{:S(2)}) collective-permute-start(f32[3,64,128]{2,1,0:T(8,128)S(1)} %get-tuple-element.69), channel_id=1, source_target_pairs={{0,16},{16,32},{32,48},{48,64},{64,80},{80,96},{96,112},{112,128},... | collective-permute-start | bytes 294920 | tf_op jit(solution)/shard_map/ppermute | solution.py:25
  8.5 29.5 %collective-permute-start.17 = (f32[3,64,128]{2,1,0:T(8,128)S(1)}, f32[3,64,128]{2,1,0:T(8,128)S(1)}, u32[]{:S(2)}, u32[]{:S(2)}) collective-permute-start(f32[3,64,128]{2,1,0:T(8,128)S(1)} %get-tuple-element.68), channel_id=1, source_target_pairs={{16,0},{32,16},{48,32},{64,48},{80,64},{96,80},{112,96},{128,112},... | collective-permute-start | bytes 294920 | tf_op jit(solution)/shard_map/ppermute | solution.py:26
  17.1 4.5 %collective-permute-start.2 = (f32[34,1,128]{2,1,0:T(1,128)S(1)}, f32[34,1,128]{2,1,0:T(1,128)S(1)}, u32[]{:S(2)}, u32[]{:S(2)}) collective-permute-start(f32[34,1,128]{2,1,0:T(1,128)S(1)} %get-tuple-element.26), channel_id=1, source_target_pairs={{1,0},{2,1},{3,2},{4,3},{5,4},{6,5},{7,6},{8,7},{9,8},{10,9},{11,1... | collective-permute-start | bytes 52232 | tf_op jit(solution)/shard_map/ppermute | solution.py:26
  18.6 5.1 %collective-permute-start.3 = (f32[34,1,128]{2,1,0:T(1,128)S(1)}, f32[34,1,128]{2,1,0:T(1,128)S(1)}, u32[]{:S(2)}, u32[]{:S(2)}) collective-permute-start(f32[34,1,128]{2,1,0:T(1,128)S(1)} %get-tuple-element.27), channel_id=1, source_target_pairs={{0,1},{1,2},{2,3},{3,4},{4,5},{5,6},{6,7},{7,8},{8,9},{9,10},{10,1... | collective-permute-start | bytes 52232 | tf_op jit(solution)/shard_map/ppermute | solution.py:25
  26.6 6.1 %collective-permute-start.5 = (f32[1,64,128]{2,1,0:T(8,128)S(1)}, f32[1,64,128]{2,1,0:T(8,128)S(1)}, u32[]{:S(2)}, u32[]{:S(2)}) collective-permute-start(f32[1,64,128]{2,1,0:T(8,128)S(1)} %get-tuple-element.56), channel_id=1, source_target_pairs={{0,16},{16,32},{32,48},{48,64},{64,80},{80,96},{96,112},{112,128},... | collective-permute-start | bytes 98312 | tf_op jit(solution)/shard_map/ppermute | solution.py:25
  32.7 6.0 %collective-permute-start.6 = (f32[34,1,128]{2,1,0:T(1,128)S(1)}, f32[34,1,128]{2,1,0:T(1,128)S(1)}, u32[]{:S(2)}, u32[]{:S(2)}) collective-permute-start(f32[34,1,128]{2,1,0:T(1,128)S(1)} %get-tuple-element.24), channel_id=1, source_target_pairs={{1,0},{2,1},{3,2},{4,3},{5,4},{6,5},{7,6},{8,7},{9,8},{10,9},{11,1... | collective-permute-start | bytes 52232 | tf_op jit(solution)/shard_map/ppermute | solution.py:26
  38.2 17.2 %collective-permute-start.18 = (f32[38,3,128]{2,1,0:T(4,128)S(1)}, f32[38,3,128]{2,1,0:T(4,128)S(1)}, u32[]{:S(2)}, u32[]{:S(2)}) collective-permute-start(f32[38,3,128]{2,1,0:T(4,128)S(1)} %get-tuple-element.14), channel_id=1, source_target_pairs={{0,1},{1,2},{2,3},{3,4},{4,5},{5,6},{6,7},{7,8},{8,9},{9,10},{10,1... | collective-permute-start | bytes 175112 | tf_op jit(solution)/shard_map/ppermute | solution.py:25
  38.2 17.2 %collective-permute-start.19 = (f32[38,3,128]{2,1,0:T(4,128)S(1)}, f32[38,3,128]{2,1,0:T(4,128)S(1)}, u32[]{:S(2)}, u32[]{:S(2)}) collective-permute-start(f32[38,3,128]{2,1,0:T(4,128)S(1)} %get-tuple-element.15), channel_id=1, source_target_pairs={{1,0},{2,1},{3,2},{4,3},{5,4},{6,5},{7,6},{8,7},{9,8},{10,9},{11,1... | collective-permute-start | bytes 175112 | tf_op jit(solution)/shard_map/ppermute | solution.py:26
  40.1 6.3 %collective-permute-start.9 = (f32[1,64,128]{2,1,0:T(8,128)S(1)}, f32[1,64,128]{2,1,0:T(8,128)S(1)}, u32[]{:S(2)}, u32[]{:S(2)}) collective-permute-start(f32[1,64,128]{2,1,0:T(8,128)S(1)} %get-tuple-element.50), channel_id=1, source_target_pairs={{0,16},{16,32},{32,48},{48,64},{64,80},{80,96},{96,112},{112,128},... | collective-permute-start | bytes 98312 | tf_op jit(solution)/shard_map/ppermute | solution.py:25
  46.5 5.2 %collective-permute-start.10 = (f32[34,1,128]{2,1,0:T(1,128)S(1)}, f32[34,1,128]{2,1,0:T(1,128)S(1)}, u32[]{:S(2)}, u32[]{:S(2)}) collective-permute-start(f32[34,1,128]{2,1,0:T(1,128)S(1)} %get-tuple-element.22), channel_id=1, source_target_pairs={{1,0},{2,1},{3,2},{4,3},{5,4},{6,5},{7,6},{8,7},{9,8},{10,9},{11,1... | collective-permute-start | bytes 52232 | tf_op jit(solution)/shard_map/ppermute | solution.py:26
  53.9 6.2 %collective-permute-start.13 = (f32[1,64,128]{2,1,0:T(8,128)S(1)}, f32[1,64,128]{2,1,0:T(8,128)S(1)}, u32[]{:S(2)}, u32[]{:S(2)}) collective-permute-start(f32[1,64,128]{2,1,0:T(8,128)S(1)} %get-tuple-element.44), channel_id=1, source_target_pairs={{0,16},{16,32},{32,48},{48,64},{64,80},{80,96},{96,112},{112,128},... | collective-permute-start | bytes 98312 | tf_op jit(solution)/shard_map/ppermute | solution.py:25
  60.1 5.2 %collective-permute-start.14 = (f32[34,1,128]{2,1,0:T(1,128)S(1)}, f32[34,1,128]{2,1,0:T(1,128)S(1)}, u32[]{:S(2)}, u32[]{:S(2)}) collective-permute-start(f32[34,1,128]{2,1,0:T(1,128)S(1)} %get-tuple-element.20), channel_id=1, source_target_pairs={{1,0},{2,1},{3,2},{4,3},{5,4},{6,5},{7,6},{8,7},{9,8},{10,9},{11,1... | collective-permute-start | bytes 52232 | tf_op jit(solution)/shard_map/ppermute | solution.py:26
  163.1 6.9 %collective-permute-start.20 = (f32[3,64,128]{2,1,0:T(8,128)S(1)}, f32[3,64,128]{2,1,0:T(8,128)S(1)}, u32[]{:S(2)}, u32[]{:S(2)}) collective-permute-start(f32[3,64,128]{2,1,0:T(8,128)S(1)} %get-tuple-element.40), channel_id=1, source_target_pairs={{0,16},{16,32},{32,48},{48,64},{64,80},{80,96},{96,112},{112,128},... | collective-permute-start | bytes 294920 | tf_op jit(solution)/shard_map/ppermute | solution.py:25
  163.6 6.4 %collective-permute-start.21 = (f32[3,64,128]{2,1,0:T(8,128)S(1)}, f32[3,64,128]{2,1,0:T(8,128)S(1)}, u32[]{:S(2)}, u32[]{:S(2)}) collective-permute-start(f32[3,64,128]{2,1,0:T(8,128)S(1)} %get-tuple-element.41), channel_id=1, source_target_pairs={{16,0},{32,16},{48,32},{64,48},{80,64},{96,80},{112,96},{128,112},... | collective-permute-start | bytes 294920 | tf_op jit(solution)/shard_map/ppermute | solution.py:26
  170.0 3.9 %collective-permute-start.22 = (f32[38,3,128]{2,1,0:T(4,128)S(1)}, f32[38,3,128]{2,1,0:T(4,128)S(1)}, u32[]{:S(2)}, u32[]{:S(2)}) collective-permute-start(f32[38,3,128]{2,1,0:T(4,128)S(1)} %get-tuple-element.12), channel_id=1, source_target_pairs={{0,1},{1,2},{2,3},{3,4},{4,5},{5,6},{6,7},{7,8},{8,9},{9,10},{10,1... | collective-permute-start | bytes 175112 | tf_op jit(solution)/shard_map/ppermute | solution.py:25
  172.5 4.0 %collective-permute-start.23 = (f32[38,3,128]{2,1,0:T(4,128)S(1)}, f32[38,3,128]{2,1,0:T(4,128)S(1)}, u32[]{:S(2)}, u32[]{:S(2)}) collective-permute-start(f32[38,3,128]{2,1,0:T(4,128)S(1)} %get-tuple-element.13), channel_id=1, source_target_pairs={{1,0},{2,1},{3,2},{4,3},{5,4},{6,5},{7,6},{8,7},{9,8},{10,9},{11,1... | collective-permute-start | bytes 175112 | tf_op jit(solution)/shard_map/ppermute | solution.py:26
  193.5 6.4 %collective-permute-start.24 = (f32[1,64,128]{2,1,0:T(8,128)S(1)}, f32[1,64,128]{2,1,0:T(8,128)S(1)}, u32[]{:S(2)}, u32[]{:S(2)}) collective-permute-start(f32[1,64,128]{2,1,0:T(8,128)S(1)} %get-tuple-element.34), channel_id=1, source_target_pairs={{0,16},{16,32},{32,48},{48,64},{64,80},{80,96},{96,112},{112,128},... | collective-permute-start | bytes 98312 | tf_op jit(solution)/shard_map/ppermute | solution.py:25
  193.6 6.4 %collective-permute-start.25 = (f32[1,64,128]{2,1,0:T(8,128)S(1)}, f32[1,64,128]{2,1,0:T(8,128)S(1)}, u32[]{:S(2)}, u32[]{:S(2)}) collective-permute-start(f32[1,64,128]{2,1,0:T(8,128)S(1)} %get-tuple-element.35), channel_id=1, source_target_pairs={{16,0},{32,16},{48,32},{64,48},{80,64},{96,80},{112,96},{128,112},... | collective-permute-start | bytes 98312 | tf_op jit(solution)/shard_map/ppermute | solution.py:26
  200.7 3.2 %collective-permute-start.27 = (f32[34,1,128]{2,1,0:T(1,128)S(1)}, f32[34,1,128]{2,1,0:T(1,128)S(1)}, u32[]{:S(2)}, u32[]{:S(2)}) collective-permute-start(f32[34,1,128]{2,1,0:T(1,128)S(1)} %get-tuple-element.19), channel_id=1, source_target_pairs={{1,0},{2,1},{3,2},{4,3},{5,4},{6,5},{7,6},{8,7},{9,8},{10,9},{11,1... | collective-permute-start | bytes 52232 | tf_op jit(solution)/shard_map/ppermute | solution.py:26
  207.4 6.5 %collective-permute-start.28 = (f32[1,64,128]{2,1,0:T(8,128)S(1)}, f32[1,64,128]{2,1,0:T(8,128)S(1)}, u32[]{:S(2)}, u32[]{:S(2)}) collective-permute-start(f32[1,64,128]{2,1,0:T(8,128)S(1)} %get-tuple-element.28), channel_id=1, source_target_pairs={{0,16},{16,32},{32,48},{48,64},{64,80},{80,96},{96,112},{112,128},... | collective-permute-start | bytes 98312 | tf_op jit(solution)/shard_map/ppermute | solution.py:25
  207.5 6.5 %collective-permute-start.29 = (f32[1,64,128]{2,1,0:T(8,128)S(1)}, f32[1,64,128]{2,1,0:T(8,128)S(1)}, u32[]{:S(2)}, u32[]{:S(2)}) collective-permute-start(f32[1,64,128]{2,1,0:T(8,128)S(1)} %get-tuple-element.29), channel_id=1, source_target_pairs={{16,0},{32,16},{48,32},{64,48},{80,64},{96,80},{112,96},{128,112},... | collective-permute-start | bytes 98312 | tf_op jit(solution)/shard_map/ppermute | solution.py:26
  214.1 3.3 %collective-permute-start.30 = (f32[34,1,128]{2,1,0:T(1,128)S(1)}, f32[34,1,128]{2,1,0:T(1,128)S(1)}, u32[]{:S(2)}, u32[]{:S(2)}) collective-permute-start(f32[34,1,128]{2,1,0:T(1,128)S(1)} %get-tuple-element.16), channel_id=1, source_target_pairs={{0,1},{1,2},{2,3},{3,4},{4,5},{5,6},{6,7},{7,8},{8,9},{9,10},{10,1... | collective-permute-start | bytes 52232 | tf_op jit(solution)/shard_map/ppermute | solution.py:25
  (10 other events, 26.5 us)
where the time goes:
time: 225 us; the launch traced here: 222 us
  blocking collectives  74.6 us (33%)
  other arithmetic  55.3 us (25%)
  starting transfers between devices  55.1 us (24%)
  waiting for transfers between devices  29.1 us (13%)
  local copies, waits for them, and re-layouts  6.51 us (3%)
    pmax x1, blocking collectives, local(): peak_speed = lax.pmax(jnp.max(jnp.abs(normal_speed)), ('gx', 'gy'))  74.6 us
    ppermute x16, starting transfers between devices, with_halo(): after = lax.ppermute(initial, axis, down)  45.6 us
    ppermute x16, waiting for transfers between devices, with_halo(): before = lax.ppermute(last, axis, up)  18.3 us
    add x1, other arithmetic, local(): section_one = level_set + time_step * section_rate(level_set, normal_speed)  18 us
    add x1, other arithmetic, local(): 0.5 * level_set  15.6 us
    ppermute x16, waiting for transfers between devices, with_halo(): after = lax.ppermute(initial, axis, down)  10.8 us
    ppermute x16, starting transfers between devices, with_halo(): before = lax.ppermute(last, axis, up)  9.44 us
    sub x2, other arithmetic, sweep_valid(): return centre - pseudo_step * sign_field * (jnp.sqrt(total) - 1.0)  7.8 us
  transfers between devices with their start and end apart: 32, of which 23 were waited for; matrix products, arithmetic and copies ran while one was open for 6% of the time, Pallas kernels for 0%

commit v1 on v0

v1 whole, which is shorter than its diff:
```python
import jax
import jax.numpy as jnp
import numpy as np
from jax import lax
from jax.experimental import pallas as pl
from jax.experimental.pallas import tpu as pltpu
from jax.sharding import PartitionSpec as P

SWEEPS = 4
REINIT = 2

screening = 0.1
spectral_mid = screening + 6.0
spectral_half = 6.0
courant = 0.25
pseudo_step = 0.25
weno_floor = 1e-06

OWN = 16
ROWS = 96
SRC = 9
LEV = 8
SPD = 5


def velocity_polynomial():
    times = np.array([0.0, 1.0])
    add = np.polynomial.polynomial.polyadd
    mul = np.polynomial.polynomial.polymul
    operator = add([spectral_mid], -times)
    ratio_now = spectral_half / spectral_mid
    iterate, residue, search = np.array([0.0]), np.array([1.0]), np.array([1.0 / spectral_mid])
    for _ in range(SWEEPS):
        applied = mul(operator, search)
        iterate = add(iterate, search)
        residue = add(residue, -applied)
        ratio_next = 1.0 / (2.0 * spectral_mid / spectral_half - ratio_now)
        search = add(ratio_next * ratio_now * search, 2.0 * ratio_next / spectral_half * residue)
        ratio_now = ratio_next
    return [float(c) for c in add(iterate, search)]


def along_lanes(value, k):
    return pltpu.roll(value, (-k) % value.shape[1], axis=1)


def inverse(x):
    r = pl.reciprocal(x, approx=True)
    return r * (2.0 - x * r)


def smooth_terms(second, second_next, third, scaled, scaled_next):
    twice = third + third
    middle = (third * twice + (1.5 * weno_floor)) + scaled * second_next
    return middle + scaled_next * twice, middle, middle - scaled * twice


def side_ratios(u1, u2, u3, jump_near, jump_far):
    p12 = jnp.square(u1 * u2)
    p13 = jnp.square(u1 * u3)
    p23 = jnp.square(u2 * u3)
    a = p12 * jump_near
    b = p23 * jump_far
    both = a + b
    both = both + both
    base = 3.0 * p13 + 0.5 * (p12 + p23)
    return (both + a) * inverse(base + p12), (both + b) * inverse(base + p23)


def weno_line(f, count):
    values, first, second, third, scaled, terms, jump, ratios = ({} for _ in range(8))

    def need(table, j, make):
        if j not in table:
            table[j] = make(j)
        return table[j]

    def val(j):
        return need(values, j, f)

    def d1(j):
        return need(first, j, lambda k: val(k + 1) - val(k))

    def d2(j):
        return need(second, j, lambda k: d1(k) - d1(k - 1))

    def d3(j):
        return need(third, j, lambda k: d2(k + 1) - d2(k))

    def sc(j):
        return need(scaled, j, lambda k: 1.5 * d2(k))

    def u(j):
        return need(terms, j, lambda k: smooth_terms(d2(k), d2(k + 1), d3(k), sc(k), sc(k + 1)))

    def g(j):
        return need(jump, j, lambda k: d3(k + 1) - d3(k))

    def r(c):
        return need(
            ratios, c, lambda k: side_ratios(u(k - 2)[0], u(k - 1)[1], u(k)[2], g(k - 1), g(k - 2))
        )

    for i in range(count):
        wide = 6.0 * (d1(i) + d1(i - 1))
        left = (wide - (d3(i - 1) + d3(i - 1))) - r(i)[0]
        right = ((d3(i) + d3(i)) - wide) - r(i + 1)[1]
        yield i, left, right


def weno_lanes(f):
    ahead = along_lanes(f, 1) - f
    behind = along_lanes(ahead, -1)
    second = ahead - behind
    second_next = along_lanes(second, 1)
    third = second_next - second
    u1, u2, u3 = smooth_terms(second, second_next, third, 1.5 * second, 1.5 * second_next)
    third_back = along_lanes(third, -1)
    near = third - third_back
    far = along_lanes(near, -1)
    ratio_left, ratio_right = side_ratios(
        along_lanes(u1, -2), along_lanes(u2, -1), u3, near, far
    )
    wide = 6.0 * (ahead + behind)
    left = (wide - (third_back + third_back)) - ratio_left
    right = ((third + third) - wide) - along_lanes(ratio_right, 1)
    return left, right


def upwind_square(left, right, sign):
    return jnp.square(jnp.maximum(jnp.maximum(sign * left, sign * right), 0.0))


def sign_of(value):
    return jnp.where(value > 0, 1.0, -1.0)


def strided(ref, x, start, step):
    return ref[x, pl.ds(start, 8, stride=step), :]


def weno_rates(field, fx, speed, sx, acc, planes, start, step, emit):
    def along_x(t, _):
        row = start + t

        def f(j):
            return strided(field, fx + j, row, step)

        for i, left, right in weno_line(f, planes):
            sign = sign_of(strided(speed, sx + i, row, step))
            acc[i, t] = upwind_square(left, right, sign)
        return _

    lax.fori_loop(0, step, along_x, 0)

    def along_yz(x, _):
        lines = {}

        def f(j):
            if j not in lines:
                lines[j] = strided(field, fx + x, start + j, step)
            return lines[j]

        for t, left, right in weno_line(f, step):
            velocity = strided(speed, sx + x, start + t, step)
            sign = sign_of(velocity)
            total = acc[x, t] + upwind_square(left, right, sign)
            left, right = weno_lanes(f(t))
            total = total + upwind_square(left, right, sign)
            emit(x, t, velocity * (jnp.sqrt(total) * (-1.0 / 12.0)))
        return _

    lax.fori_loop(0, planes, along_yz, 0)


def reinit_sweep(field, fx, origin, ox, planes, start, step, emit):
    def body(x, _):
        lines = {}

        def f(j):
            if j not in lines:
                lines[j] = strided(field, fx + x, start + j, step)
            return lines[j]

        for t in range(step):
            row = start + t
            centre = f(t)
            base = strided(origin, ox + x, row, step)
            sign_field = base / jnp.sqrt(base * base + 1.0)
            sign = sign_of(sign_field)
            total = upwind_square(
                centre - strided(field, fx + x - 1, row, step),
                centre - strided(field, fx + x + 1, row, step),
                sign,
            )
            total = total + upwind_square(centre - f(t - 1), centre - f(t + 1), sign)
            total = total + upwind_square(
                centre - along_lanes(centre, -1), centre - along_lanes(centre, 1), sign
            )
            emit(x, t, centre - pseudo_step * sign_field * (jnp.sqrt(total) - 1.0))
        return _

    lax.fori_loop(0, planes, body, 0)


def pack_x(level, stress, materials, source, low, high):
    nx, ny, _ = level.shape

    def weigh(x, _):
        label = materials[x]
        weight = jnp.where(label == 0, 1.0, jnp.where(label == 1, 0.6, 0.0)).astype(jnp.float32)
        source[x] = weight * stress[x]
        return _

    lax.fori_loop(0, nx, weigh, 0)
    for k in range(SRC):
        low[pl.ds(k * ny, ny), :] = source[k]
        high[pl.ds(k * ny, ny), :] = source[nx - SRC + k]
    for k in range(LEV):
        low[pl.ds((SRC + k) * ny, ny), :] = level[k]
        high[pl.ds((SRC + k) * ny, ny), :] = level[nx - LEV + k]


def pack_y(level, source, before, after, low, high):
    nx, ny, _ = level.shape
    wide = nx + 2 * SRC
    tall = nx + 2 * LEV
    extra = tall * 8 + wide * 8

    def put_level(k, piece_low, piece_high):
        low[pl.ds(k * 8, 8), :] = piece_low
        high[pl.ds(k * 8, 8), :] = piece_high

    def put_source(k, piece_low, row_low, piece_high, row_high):
        low[pl.ds((tall + k) * 8, 8), :] = piece_low
        high[pl.ds((tall + k) * 8, 8), :] = piece_high
        low[pl.ds(extra + k, 1), :] = row_low
        high[pl.ds(extra + k, 1), :] = row_high

    for k in range(nx):
        put_level(LEV + k, level[k, 0:8], level[k, ny - 8 : ny])
        put_source(
            SRC + k,
            source[k, 0:8],
            source[k, 8:9],
            source[k, ny - 8 : ny],
            source[k, ny - 9 : ny - 8],
        )
    for ref, at in ((before, 0), (after, 1)):
        for k in range(SRC):
            b = k * ny
            put_source(
                k + at * (SRC + nx),
                ref[b : b + 8],
                ref[b + 8 : b + 9],
                ref[b + ny - 8 : b + ny],
                ref[b + ny - 9 : b + ny - 8],
            )
        for k in range(LEV):
            b = (SRC + k) * ny
            put_level(k + at * (LEV + nx), ref[b : b + 8], ref[b + ny - 8 : b + ny])
    low[pl.ds(extra + wide, 8 - wide % 8), :] = jnp.zeros((8 - wide % 8, 128), jnp.float32)
    high[pl.ds(extra + wide, 8 - wide % 8), :] = jnp.zeros((8 - wide % 8, 128), jnp.float32)


def extend(level, source, before, after, below, above, level_out, source_out):
    nx, ny, _ = level.shape
    wide = nx + 2 * SRC
    tall = nx + 2 * LEV
    extra = tall * 8 + wide * 8
    top = OWN + ny
    for k in range(nx):
        level_out[LEV + k, OWN:top] = level[k]
        source_out[SRC + k, OWN:top] = source[k]
    for ref, at in ((before, 0), (after, 1)):
        for k in range(SRC):
            source_out[k + at * (SRC + nx), OWN:top] = ref[k * ny : (k + 1) * ny]
        for k in range(LEV):
            b = (SRC + k) * ny
            level_out[k + at * (LEV + nx), OWN:top] = ref[b : b + ny]
    for k in range(tall):
        level_out[k, OWN - 8 : OWN] = below[k * 8 : k * 8 + 8]
        level_out[k, top : top + 8] = above[k * 8 : k * 8 + 8]
    for k in range(wide):
        b = (tall + k) * 8
        source_out[k, OWN - 8 : OWN] = below[b : b + 8]
        source_out[k, top : top + 8] = above[b : b + 8]
        source_out[k, OWN - 9 : OWN - 8] = below[extra + k : extra + k + 1]
        source_out[k, top + 8 : top + 9] = above[extra + k : extra + k + 1]


def velocity(
    level, source, before, after, below, above, level_out, speed, own_speed, peaks, src, one, two
):
    extend(level, source, before, after, below, above, level_out, src)
    nx, ny, _ = level.shape
    wide = nx + 2 * SRC
    coefficients = velocity_polynomial()
    step = (ny + 2 * (SRC - 1)) // 8
    start = OWN - (SRC - 1)

    def sweep(old, new, shift, lo, hi, last, constant):
        def body(x, _):
            lines = {}

            def f(j):
                if j not in lines:
                    lines[j] = strided(old, x, start + j, step)
                return lines[j]

            for t in range(step):
                centre = f(t)
                beside = strided(old, x - 1, start + t, step) + strided(old, x + 1, start + t, step)
                beside = beside + (f(t - 1) + f(t + 1))
                beside = beside + (along_lanes(centre, 1) + along_lanes(centre, -1))
                if last is not None:
                    beside = last * beside
                own = centre if old is src else strided(src, x, start + t, step)
                new[x - shift, pl.ds(start + t, 8, stride=step), :] = beside + constant * own
            return _

        lax.fori_loop(lo, hi, body, 0)

    sweep(src, one, 0, 1, wide - 1, coefficients[4], coefficients[3])
    sweep(one, two, 0, 2, wide - 2, None, coefficients[2])
    sweep(two, one, 0, 3, wide - 3, None, coefficients[1])
    sweep(one, speed, SRC - SPD, 4, wide - 4, None, coefficients[0])

    def largest(x, carry):
        mine = speed[SPD + x, OWN : OWN + ny]
        own_speed[x] = mine
        return jnp.maximum(carry, jnp.abs(mine))

    top = lax.fori_loop(0, nx, largest, jnp.zeros((ny, 128), jnp.float32))
    peaks[...] = jnp.broadcast_to(jnp.max(top), peaks.shape)


def first_stage(level, speed, rate, acc):
    planes = rate.shape[0]
    step = 10
    start = OWN - SPD

    def emit(x, t, value):
        rate[x, pl.ds(start + t, 8, stride=step), :] = value

    weno_rates(level, LEV - SPD, speed, 0, acc, planes, start, step, emit)


def second_stage(level, speed, rate, peaks, new_level, stage, advected, swept, acc):
    nx, ny, _ = new_level.shape
    peak = jnp.max(peaks[...], axis=0, keepdims=True)
    time_step = courant / (peak + 1e-06)
    step_row = jnp.broadcast_to(time_step, (8, 128))
    step_rows = jnp.broadcast_to(time_step, (ROWS - 8, 128))

    def advance(x, _):
        stage[x, 8:ROWS] = level[x + LEV - SPD, 8:ROWS] + step_rows * rate[x, 8:ROWS]
        return _

    lax.fori_loop(0, stage.shape[0], advance, 0)

    start, step = OWN - 2, 9

    def emit(x, t, value):
        row = start + t
        after = strided(stage, x + SPD - 2, row, step) + step_row * value
        before = strided(level, x + LEV - 2, row, step)
        advected[x, pl.ds(row, 8, stride=step), :] = 0.5 * before + 0.5 * after

    weno_rates(stage, SPD - 2, speed, SPD - 2, acc, nx + 4, start, step, emit)

    def emit_one(x, t, value):
        swept[x, pl.ds(OWN - 1 + t, 8, stride=9), :] = value

    reinit_sweep(advected, 1, advected, 1, nx + 2, OWN - 1, 9, emit_one)

    def emit_two(x, t, value):
        new_level[x, pl.ds(t, 8, stride=ny // 8), :] = value

    reinit_sweep(swept, 1, advected, 2, nx, OWN, ny // 8, emit_two)


VM = pl.BlockSpec(memory_space=pltpu.VMEM)


def call(kernel, outs, scratch, args):
    return pl.pallas_call(
        kernel,
        out_shape=[jax.ShapeDtypeStruct(s, jnp.float32) for s in outs],
        in_specs=[VM] * len(args),
        out_specs=[VM] * len(outs),
        scratch_shapes=[pltpu.VMEM(s, jnp.float32) for s in scratch],
        compiler_params=pltpu.CompilerParams(vmem_limit_bytes=40 * 1024 * 1024),
    )(*args)


def local(level_set, stress_jump, materials):
    nx, ny, nz = level_set.shape
    wide, tall, mid = nx + 2 * SRC, nx + 2 * LEV, nx + 2 * SPD
    size_x, size_y = lax.axis_size("gx"), lax.axis_size("gy")

    def shift(value, axis, size, by):
        return lax.ppermute(value, axis, [(i, (i + by) % size) for i in range(size)])

    message = ((SRC + LEV) * ny, nz)
    source, low, high = call(
        pack_x, [(nx, ny, nz), message, message], [], (level_set, stress_jump, materials)
    )
    after = shift(low, "gx", size_x, -1)
    before = shift(high, "gx", size_x, 1)
    message = (tall * 8 + wide * 8 + (wide + 7) // 8 * 8, nz)
    low, high = call(pack_y, [message, message], [], (level_set, source, before, after))
    above = shift(low, "gy", size_y, -1)
    below = shift(high, "gy", size_y, 1)
    devices = size_x * size_y
    level, speed, normal_speed, peaks = call(
        velocity,
        [(tall, ROWS, nz), (mid, ROWS, nz), (nx, ny, nz), (devices, nz)],
        [(wide, ROWS, nz)] * 3,
        (level_set, source, before, after, below, above),
    )
    peaks = lax.all_to_all(peaks.reshape(devices, 1, nz), ("gx", "gy"), 0, 0)
    peaks = peaks.reshape(devices, nz)
    (rate,) = call(first_stage, [(mid, ROWS, nz)], [(mid, 10, 8, nz)], (level, speed))
    (new_level,) = call(
        second_stage,
        [(nx, ny, nz)],
        [(mid, ROWS, nz), (nx + 4, ROWS, nz), (nx + 2, ROWS, nz), (nx + 4, 9, 8, nz)],
        (level, speed, rate, peaks),
    )
    return (new_level, normal_speed)


def solution(mesh):
    in_specs = (P("gx", "gy", None), P("gx", "gy", None), P("gx", "gy", None))
    out_specs = (P("gx", "gy", None), P("gx", "gy", None))
    return jax.shard_map(local, mesh=mesh, in_specs=in_specs, out_specs=out_specs, check_vma=False)
```

time: 225 us -> 122 us (0.54); the launches traced: 222 us -> 122 us
  blocking collectives: 74.6 us -> 0 us
  Pallas kernels: 0 us -> 67.9 us
  other arithmetic: 55.3 us -> 0 us
  starting transfers between devices: 55.1 us -> 24 us
  waiting for transfers between devices: 29.1 us -> 18.2 us
  local copies, waits for them, and re-layouts: 6.51 us -> 11 us
    pmax x1 -> x0, blocking collectives: 74.6 us -> none  [local(): peak_speed = lax.pmax(jnp.max(jnp.abs(normal_speed)), ('gx', 'gy'))]
    pallas_call x0 -> x5, Pallas kernels: none -> 67.9 us  [call(): pl.pallas_call(kernel, out_shape=[jax.ShapeDtypeStruct(s, jnp.float32) fo...]
    ppermute x32 -> x4, starting transfers between devices: 55.1 us -> 10.7 us  [shift(): lax.ppermute(value, axis, [(i, (i + by) % size) for i in range(size)])]
    add x5 -> x0, other arithmetic: 36.5 us -> none  [the longest x1 18 us: local(): section_one = level_set + time_step * section_rate(level_set, normal_speed)]
    all_to_all x0 -> x1, starting transfers between devices: none -> 13.3 us  [local(): peaks = lax.all_to_all(peaks.reshape(devices, 1, nz), ('gx', 'gy'), 0, 0)]
    ppermute x32 -> x4, waiting for transfers between devices: 29.1 us -> 18.2 us  [shift(): lax.ppermute(value, axis, [(i, (i + by) % size) for i in range(size)])]
    sub x8 -> x0, other arithmetic: 10.8 us -> none  [the longest x2 7.8 us: sweep_valid(): return centre - pseudo_step * sign_field * (jnp.sqrt(total) - 1.0)]
    unnamed x6 -> x16, local copies, waits for them, and re-layouts: 1.21 us -> 11 us
  transfers between devices with their start and end apart: 32 -> 5, of which waited for: 23 -> 3; matrix products, arithmetic and copies ran while one was open for 6% -> 0% of each run, Pallas kernels for 0% -> 18%
where the time goes in v1:
time: 122 us
  Pallas kernels  67.9 us (56%)
  starting transfers between devices  24 us (20%)
  waiting for transfers between devices  18.2 us (15%)
  local copies, waits for them, and re-layouts  11 us (9%)
    pallas_call x5, Pallas kernels, call(): pl.pallas_call(kernel, out_shape=[jax.ShapeDtypeStruct(s, jnp.float32) fo...  67.9 us
    ppermute x4, waiting for transfers between devices, shift(): lax.ppermute(value, axis, [(i, (i + by) % size) for i in range(size)])  18.2 us
    all_to_all x1, starting transfers between devices, local(): peaks = lax.all_to_all(peaks.reshape(devices, 1, nz), ('gx', 'gy'), 0, 0)  13.3 us
    unnamed x16, local copies, waits for them, and re-layouts  11 us
    ppermute x4, starting transfers between devices, shift(): lax.ppermute(value, axis, [(i, (i + by) % size) for i in range(size)])  10.7 us
  transfers between devices with their start and end apart: 5, of which 3 were waited for; matrix products, arithmetic and copies ran while one was open for 0% of the time, Pallas kernels for 18%

profile of v1, /device:TPU:1, one launch (start us, length us, event | category | flops | bytes accessed | tf_op | source)
XLA Modules:
  0.0 121.8 jit_solution(14577530021579575161)
XLA Ops:
  0.6 0.0 copy-start
  0.6 1.2 copy-done
  1.9 1.2 %copy-done.6 = f32[32,64,128]{2,1,0:T(8,128)S(1)} copy-done((f32[32,64,128]{2,1,0:T(8,128)S(1)}, f32[32,64,128]{2,1,0:T(8,128)}, u32[]{:S(2)}) %copy-start.6) | copy-done | bytes 1048600
  3.1 1.2 %copy-done.7 = s32[32,64,128]{2,1,0:T(8,128)S(1)} copy-done((s32[32,64,128]{2,1,0:T(8,128)S(1)}, s32[32,64,128]{2,1,0:T(8,128)}, u32[]{:S(2)}) %copy-start.7) | copy-done | bytes 1048600
  4.3 0.4 shard_map.50
  4.7 2.2 %collective-permute-start = (f32[1088,128]{1,0:T(8,128)S(1)}, f32[1088,128]{1,0:T(8,128)S(1)}, u32[]{:S(2)}, u32[]{:S(2)}) collective-permute-start(f32[1088,128]{1,0:T(8,128)S(1)} %get-tuple-element.12), channel_id=1, source_target_pairs={{0,16},{16,32},{32,48},{48,64},{64,80},{80,96},{96,112},{112,128},... | collective-permute-start | bytes 1671176 | tf_op jit(solution)/shard_map/ppermute | solution.py:403
  6.9 3.7 %collective-permute-start.1 = (f32[1088,128]{1,0:T(8,128)S(1)}, f32[1088,128]{1,0:T(8,128)S(1)}, u32[]{:S(2)}, u32[]{:S(2)}) collective-permute-start(f32[1088,128]{1,0:T(8,128)S(1)} %get-tuple-element.13), channel_id=1, source_target_pairs={{0,240},{16,0},{32,16},{48,32},{64,48},{80,64},{96,80},{112,96},{1... | collective-permute-start | bytes 1671176 | tf_op jit(solution)/shard_map/ppermute | solution.py:403
  10.6 10.3 %collective-permute-done.before = f32[1088,128]{1,0:T(8,128)S(1)} collective-permute-done((f32[1088,128]{1,0:T(8,128)S(1)}, f32[1088,128]{1,0:T(8,128)S(1)}, u32[]{:S(2)}, u32[]{:S(2)}) %collective-permute-start) | collective-permute-done | bytes 557088 | tf_op jit(solution)/shard_map/ppermute | solution.py:403
  20.9 0.0 collective-permute-done.1.after
  20.9 0.1 shard_map.51
  21.0 4.7 %collective-permute-start.2 = (f32[840,128]{1,0:T(8,128)S(1)}, f32[840,128]{1,0:T(8,128)S(1)}, u32[]{:S(2)}, u32[]{:S(2)}) collective-permute-start(f32[840,128]{1,0:T(8,128)S(1)} %get-tuple-element.14), channel_id=1, source_target_pairs={{0,1},{1,2},{2,3},{3,4},{4,5},{5,6},{6,7},{7,8},{8,9},{9,10},{10,1... | collective-permute-start | bytes 1290248 | tf_op jit(solution)/shard_map/ppermute | solution.py:403
  25.7 0.0 collective-permute-start.3
  25.7 5.1 %collective-permute-done.2.below = f32[840,128]{1,0:T(8,128)S(1)} collective-permute-done((f32[840,128]{1,0:T(8,128)S(1)}, f32[840,128]{1,0:T(8,128)S(1)}, u32[]{:S(2)}, u32[]{:S(2)}) %collective-permute-start.2) | collective-permute-done | bytes 430112 | tf_op jit(solution)/shard_map/ppermute | solution.py:403
  30.8 2.8 %collective-permute-done.3.above = f32[840,128]{1,0:T(8,128)S(1)} collective-permute-done((f32[840,128]{1,0:T(8,128)S(1)}, f32[840,128]{1,0:T(8,128)S(1)}, u32[]{:S(2)}, u32[]{:S(2)}) %collective-permute-start.3) | collective-permute-done | bytes 430112 | tf_op jit(solution)/shard_map/ppermute | solution.py:403
  33.6 18.0 %shard_map.52 = (f32[48,96,128]{2,1,0:T(8,128)S(1)}, f32[42,96,128]{2,1,0:T(8,128)S(1)}, f32[32,64,128]{2,1,0:T(8,128)}, f32[256,128]{1,0:T(8,128)}) custom-call(f32[32,64,128]{2,1,0:T(8,128)S(1)} %copy-done, f32[32,64,128]{2,1,0:T(8,128)S(1)} %get-tuple-element.11.source, f32[1088,128]{1,0:T(8,128)S(1)} %collective-permute-done.before, ...), custom_call_target="tpu_custom_call" | custom-call | tf_op jit(solution)/shard_map/pallas_call | solution.py:387
  51.6 1.3 %copy-done.1 = f32[42,96,128]{2,1,0:T(8,128)} copy-done((f32[42,96,128]{2,1,0:T(8,128)}, f32[42,96,128]{2,1,0:T(8,128)S(1)}, u32[]{:S(2)}) %copy-start.1) | copy-done | bytes 2064408
  52.9 13.3 %all-to-all-start = ((f32[256,1,128]{2,1,0:T(1,128)}), f32[256,1,128]{2,1,0:T(1,128)S(1)}, u32[]{:S(2)}, u32[]{:S(2)}) async-start(f32[256,1,128]{2,1,0:T(1,128)} %bitcast.1), calls=%async_computation | async-start | bytes 262144 | tf_op jit(solution)/shard_map/all_to_all | solution.py:422
  66.3 1.6 %copy-done.2 = f32[42,96,128]{2,1,0:T(8,128)S(1)} copy-done((f32[42,96,128]{2,1,0:T(8,128)S(1)}, f32[42,96,128]{2,1,0:T(8,128)}, u32[]{:S(2)}) %copy-start.2) | copy-done | bytes 2064408
  67.8 22.2 %shard_map.53.rate = f32[42,96,128]{2,1,0:T(8,128)S(1)} custom-call(f32[48,96,128]{2,1,0:T(8,128)S(1)} %get-tuple-element.16.level, f32[42,96,128]{2,1,0:T(8,128)S(1)} %copy-done.2), custom_call_target="tpu_custom_call" | custom-call | tf_op jit(solution)/shard_map/pallas_call | solution.py:387
  90.0 1.3 %copy-done.4 = f32[42,96,128]{2,1,0:T(8,128)} copy-done((f32[42,96,128]{2,1,0:T(8,128)}, f32[42,96,128]{2,1,0:T(8,128)S(1)}, u32[]{:S(2)}) %copy-start.4) | copy-done | bytes 2064408
  91.3 0.0 all-to-all-done
  91.3 1.6 %copy-done.3 = f32[42,96,128]{2,1,0:T(8,128)S(1)} copy-done((f32[42,96,128]{2,1,0:T(8,128)S(1)}, f32[42,96,128]{2,1,0:T(8,128)}, u32[]{:S(2)}) %copy-start.3) | copy-done | bytes 2064408
  92.9 1.6 %copy-done.5 = f32[42,96,128]{2,1,0:T(8,128)S(1)} copy-done((f32[42,96,128]{2,1,0:T(8,128)S(1)}, f32[42,96,128]{2,1,0:T(8,128)}, u32[]{:S(2)}) %copy-start.5) | copy-done | bytes 2064408
  94.5 27.3 %shard_map.54 = f32[32,64,128]{2,1,0:T(8,128)} custom-call(f32[48,96,128]{2,1,0:T(8,128)S(1)} %get-tuple-element.16.level, f32[42,96,128]{2,1,0:T(8,128)S(1)} %copy-done.3, f32[42,96,128]{2,1,0:T(8,128)S(1)} %copy-done.5, f32[256,128]{1,0:T(8,128)S(1)} %bitcast.4), custom_call_target="tpu_custom_call" | custom-call | tf_op jit(solution)/shard_map/pallas_call | solution.py:387
  (7 shorter events, 0.0 us)
Async XLA Ops:
  0.6 1.2 %copy-start = (f32[32,64,128]{2,1,0:T(8,128)S(1)}, f32[32,64,128]{2,1,0:T(8,128)}, u32[]{:S(2)}) copy-start(f32[32,64,128]{2,1,0:T(8,128)} %level.5) | copy-start | bytes 3145732
  1.9 1.2 %copy-start.6 = (f32[32,64,128]{2,1,0:T(8,128)S(1)}, f32[32,64,128]{2,1,0:T(8,128)}, u32[]{:S(2)}) copy-start(f32[32,64,128]{2,1,0:T(8,128)} %stress.1) | copy-start | bytes 3145732
  3.1 1.2 %copy-start.7 = (s32[32,64,128]{2,1,0:T(8,128)S(1)}, s32[32,64,128]{2,1,0:T(8,128)}, u32[]{:S(2)}) copy-start(s32[32,64,128]{2,1,0:T(8,128)} %materials.1) | copy-start | bytes 3145732
  4.7 16.2 %collective-permute-start = (f32[1088,128]{1,0:T(8,128)S(1)}, f32[1088,128]{1,0:T(8,128)S(1)}, u32[]{:S(2)}, u32[]{:S(2)}) collective-permute-start(f32[1088,128]{1,0:T(8,128)S(1)} %get-tuple-element.12), channel_id=1, source_target_pairs={{0,16},{16,32},{32,48},{48,64},{64,80},{80,96},{96,112},{112,128},... | collective-permute-start | bytes 1671176 | tf_op jit(solution)/shard_map/ppermute | solution.py:403
  6.9 14.0 %collective-permute-start.1 = (f32[1088,128]{1,0:T(8,128)S(1)}, f32[1088,128]{1,0:T(8,128)S(1)}, u32[]{:S(2)}, u32[]{:S(2)}) collective-permute-start(f32[1088,128]{1,0:T(8,128)S(1)} %get-tuple-element.13), channel_id=1, source_target_pairs={{0,240},{16,0},{32,16},{48,32},{64,48},{80,64},{96,80},{112,96},{1... | collective-permute-start | bytes 1671176 | tf_op jit(solution)/shard_map/ppermute | solution.py:403
  21.0 9.8 %collective-permute-start.2 = (f32[840,128]{1,0:T(8,128)S(1)}, f32[840,128]{1,0:T(8,128)S(1)}, u32[]{:S(2)}, u32[]{:S(2)}) collective-permute-start(f32[840,128]{1,0:T(8,128)S(1)} %get-tuple-element.14), channel_id=1, source_target_pairs={{0,1},{1,2},{2,3},{3,4},{4,5},{5,6},{6,7},{7,8},{8,9},{9,10},{10,1... | collective-permute-start | bytes 1290248 | tf_op jit(solution)/shard_map/ppermute | solution.py:403
  25.7 7.9 %collective-permute-start.3 = (f32[840,128]{1,0:T(8,128)S(1)}, f32[840,128]{1,0:T(8,128)S(1)}, u32[]{:S(2)}, u32[]{:S(2)}) collective-permute-start(f32[840,128]{1,0:T(8,128)S(1)} %get-tuple-element.15), channel_id=1, source_target_pairs={{0,15},{1,0},{2,1},{3,2},{4,3},{5,4},{6,5},{7,6},{8,7},{9,8},{10,9... | collective-permute-start | bytes 1290248 | tf_op jit(solution)/shard_map/ppermute | solution.py:403
  51.6 1.3 %copy-start.1 = (f32[42,96,128]{2,1,0:T(8,128)}, f32[42,96,128]{2,1,0:T(8,128)S(1)}, u32[]{:S(2)}) copy-start(f32[42,96,128]{2,1,0:T(8,128)S(1)} %get-tuple-element.17.speed) | copy-start | bytes 6193156
  52.9 38.4 %all-to-all-start = ((f32[256,1,128]{2,1,0:T(1,128)}), f32[256,1,128]{2,1,0:T(1,128)S(1)}, u32[]{:S(2)}, u32[]{:S(2)}) async-start(f32[256,1,128]{2,1,0:T(1,128)} %bitcast.1), calls=%async_computation | async-start | bytes 262144 | tf_op jit(solution)/shard_map/all_to_all | solution.py:422
  66.2 1.6 %copy-start.2 = (f32[42,96,128]{2,1,0:T(8,128)S(1)}, f32[42,96,128]{2,1,0:T(8,128)}, u32[]{:S(2)}) copy-start(f32[42,96,128]{2,1,0:T(8,128)} %copy-done.1) | copy-start | bytes 6193156
  90.0 1.3 %copy-start.4 = (f32[42,96,128]{2,1,0:T(8,128)}, f32[42,96,128]{2,1,0:T(8,128)S(1)}, u32[]{:S(2)}) copy-start(f32[42,96,128]{2,1,0:T(8,128)S(1)} %shard_map.53.rate) | copy-start | bytes 6193156
  91.3 1.6 %copy-start.3 = (f32[42,96,128]{2,1,0:T(8,128)S(1)}, f32[42,96,128]{2,1,0:T(8,128)}, u32[]{:S(2)}) copy-start(f32[42,96,128]{2,1,0:T(8,128)} %copy-done.1) | copy-start | bytes 6193156
  92.9 1.6 %copy-start.5 = (f32[42,96,128]{2,1,0:T(8,128)S(1)}, f32[42,96,128]{2,1,0:T(8,128)}, u32[]{:S(2)}) copy-start(f32[42,96,128]{2,1,0:T(8,128)} %copy-done.4) | copy-start | bytes 6193156

commit v2 on v1

--- a/solution.py
+++ b/solution.py
@@ -45,8 +45,11 @@
 
 
 def inverse(x):
-    r = pl.reciprocal(x, approx=True)
-    return r * (2.0 - x * r)
+    return pl.reciprocal(x, approx=True)
+
+
+def root(x):
+    return x * lax.rsqrt(jnp.maximum(x, 1.2e-38))
 
 
 def smooth_terms(second, second_next, third, scaled, scaled_next):
@@ -109,21 +112,8 @@
 
 
 def weno_lanes(f):
-    ahead = along_lanes(f, 1) - f
-    behind = along_lanes(ahead, -1)
-    second = ahead - behind
-    second_next = along_lanes(second, 1)
-    third = second_next - second
-    u1, u2, u3 = smooth_terms(second, second_next, third, 1.5 * second, 1.5 * second_next)
-    third_back = along_lanes(third, -1)
-    near = third - third_back
-    far = along_lanes(near, -1)
-    ratio_left, ratio_right = side_ratios(
-        along_lanes(u1, -2), along_lanes(u2, -1), u3, near, far
-    )
-    wide = 6.0 * (ahead + behind)
-    left = (wide - (third_back + third_back)) - ratio_left
-    right = ((third + third) - wide) - along_lanes(ratio_right, 1)
+    shifted = {k: along_lanes(f, k) if k else f for k in range(-3, 4)}
+    ((_, left, right),) = weno_line(lambda j: shifted[j], 1)
     return left, right
 
 
@@ -167,10 +157,10 @@
             total = acc[x, t] + upwind_square(left, right, sign)
             left, right = weno_lanes(f(t))
             total = total + upwind_square(left, right, sign)
-            emit(x, t, velocity * (jnp.sqrt(total) * (-1.0 / 12.0)))
+            emit(x, t, velocity * (root(total) * (-1.0 / 12.0)))
         return _
 
-    lax.fori_loop(0, planes, along_yz, 0)
+    lax.fori_loop(0, planes, along_yz, 0, unroll=2)
 
 
 def reinit_sweep(field, fx, origin, ox, planes, start, step, emit):
@@ -186,7 +176,7 @@
             row = start + t
             centre = f(t)
             base = strided(origin, ox + x, row, step)
-            sign_field = base / jnp.sqrt(base * base + 1.0)
+            sign_field = base * lax.rsqrt(base * base + 1.0)
             sign = sign_of(sign_field)
             total = upwind_square(
                 centre - strided(field, fx + x - 1, row, step),
@@ -197,10 +187,10 @@
             total = total + upwind_square(
                 centre - along_lanes(centre, -1), centre - along_lanes(centre, 1), sign
             )
-            emit(x, t, centre - pseudo_step * sign_field * (jnp.sqrt(total) - 1.0))
+            emit(x, t, centre - pseudo_step * sign_field * (root(total) - 1.0))
         return _
 
-    lax.fori_loop(0, planes, body, 0)
+    lax.fori_loop(0, planes, body, 0, unroll=2)
 
 
 def pack_x(level, stress, materials, source, low, high):
@@ -319,7 +309,7 @@
                 new[x - shift, pl.ds(start + t, 8, stride=step), :] = beside + constant * own
             return _
 
-        lax.fori_loop(lo, hi, body, 0)
+        lax.fori_loop(lo, hi, body, 0, unroll=4)
 
     sweep(src, one, 0, 1, wide - 1, coefficients[4], coefficients[3])
     sweep(one, two, 0, 2, wide - 2, None, coefficients[2])
@@ -383,14 +373,14 @@
 VM = pl.BlockSpec(memory_space=pltpu.VMEM)
 
 
-def call(kernel, outs, scratch, args):
+def call(kernel, outs, scratch, args, megabytes=18):
     return pl.pallas_call(
         kernel,
         out_shape=[jax.ShapeDtypeStruct(s, jnp.float32) for s in outs],
         in_specs=[VM] * len(args),
         out_specs=[VM] * len(outs),
         scratch_shapes=[pltpu.VMEM(s, jnp.float32) for s in scratch],
-        compiler_params=pltpu.CompilerParams(vmem_limit_bytes=40 * 1024 * 1024),
+        compiler_params=pltpu.CompilerParams(vmem_limit_bytes=megabytes * 1024 * 1024),
     )(*args)
 
 
@@ -418,6 +408,7 @@
         [(tall, ROWS, nz), (mid, ROWS, nz), (nx, ny, nz), (devices, nz)],
         [(wide, ROWS, nz)] * 3,
         (level_set, source, before, after, below, above),
+        megabytes=24,
     )
     peaks = lax.all_to_all(peaks.reshape(devices, 1, nz), ("gx", "gy"), 0, 0)
     peaks = peaks.reshape(devices, nz)

time: 122 us -> 92.2 us (0.76)
  Pallas kernels: 67.9 us -> 37.9 us
    pallas_call x5, Pallas kernels: 67.9 us -> 37.9 us  [call(): pl.pallas_call(kernel, out_shape=[jax.ShapeDtypeStruct(s, jnp.float32) fo...]
    unnamed x16 -> x18, local copies, waits for them, and re-layouts: 11 us -> 11 us
  transfers between devices with their start and end apart: 5 -> 5, of which waited for: 3 -> 3; matrix products, arithmetic and copies ran while one was open for 0% -> 0% of each run, Pallas kernels for 18% -> 14%
where the time goes in v2:
time: 92.2 us; the launch traced here: 91.8 us
  Pallas kernels  37.9 us (41%)
  starting transfers between devices  24 us (26%)
  waiting for transfers between devices  18.2 us (20%)
  local copies, waits for them, and re-layouts  11 us (12%)
    pallas_call x5, Pallas kernels, call(): pl.pallas_call(kernel, out_shape=[jax.ShapeDtypeStruct(s, jnp.float32) fo...  37.9 us
    ppermute x4, waiting for transfers between devices, shift(): lax.ppermute(value, axis, [(i, (i + by) % size) for i in range(size)])  18.2 us
    all_to_all x1, starting transfers between devices, local(): peaks = lax.all_to_all(peaks.reshape(devices, 1, nz), ('gx', 'gy'), 0, 0)  13.3 us
    unnamed x18, local copies, waits for them, and re-layouts  11 us
    ppermute x4, starting transfers between devices, shift(): lax.ppermute(value, axis, [(i, (i + by) % size) for i in range(size)])  10.7 us
  transfers between devices with their start and end apart: 5, of which 3 were waited for; matrix products, arithmetic and copies ran while one was open for 0% of the time, Pallas kernels for 14%

profile of v2, /device:TPU:1, one launch (start us, length us, event | category | flops | bytes accessed | tf_op | source)
XLA Modules:
  0.0 91.8 jit_solution(10668973827935460380)
XLA Ops:
  0.6 0.0 copy-start
  0.6 1.2 %copy-done = f32[32,64,128]{2,1,0:T(8,128)S(1)} copy-done((f32[32,64,128]{2,1,0:T(8,128)S(1)}, f32[32,64,128]{2,1,0:T(8,128)}, u32[]{:S(2)}) %copy-start) | copy-done | bytes 1048600
  1.9 1.2 %copy-done.7 = f32[32,64,128]{2,1,0:T(8,128)S(1)} copy-done((f32[32,64,128]{2,1,0:T(8,128)S(1)}, f32[32,64,128]{2,1,0:T(8,128)}, u32[]{:S(2)}) %copy-start.7) | copy-done | bytes 1048600
  3.1 1.2 %copy-done.8 = s32[32,64,128]{2,1,0:T(8,128)S(1)} copy-done((s32[32,64,128]{2,1,0:T(8,128)S(1)}, s32[32,64,128]{2,1,0:T(8,128)}, u32[]{:S(2)}) %copy-start.8) | copy-done | bytes 1048600
  4.3 0.4 shard_map.50
  4.7 0.0 copy-start.1
  4.7 2.2 %collective-permute-start = (f32[1088,128]{1,0:T(8,128)S(1)}, f32[1088,128]{1,0:T(8,128)S(1)}, u32[]{:S(2)}, u32[]{:S(2)}) collective-permute-start(f32[1088,128]{1,0:T(8,128)S(1)} %get-tuple-element.12), channel_id=1, source_target_pairs={{0,16},{16,32},{32,48},{48,64},{64,80},{80,96},{96,112},{112,128},... | collective-permute-start | bytes 1671176 | tf_op jit(solution)/shard_map/ppermute | solution.py:393
  6.9 3.7 %collective-permute-start.1 = (f32[1088,128]{1,0:T(8,128)S(1)}, f32[1088,128]{1,0:T(8,128)S(1)}, u32[]{:S(2)}, u32[]{:S(2)}) collective-permute-start(f32[1088,128]{1,0:T(8,128)S(1)} %get-tuple-element.13), channel_id=1, source_target_pairs={{0,240},{16,0},{32,16},{48,32},{64,48},{80,64},{96,80},{112,96},{1... | collective-permute-start | bytes 1671176 | tf_op jit(solution)/shard_map/ppermute | solution.py:393
  10.6 10.3 %collective-permute-done.before = f32[1088,128]{1,0:T(8,128)S(1)} collective-permute-done((f32[1088,128]{1,0:T(8,128)S(1)}, f32[1088,128]{1,0:T(8,128)S(1)}, u32[]{:S(2)}, u32[]{:S(2)}) %collective-permute-start) | collective-permute-done | bytes 557088 | tf_op jit(solution)/shard_map/ppermute | solution.py:393
  20.9 0.0 collective-permute-done.1.after
  20.9 0.1 shard_map.51
  21.0 4.7 %collective-permute-start.2 = (f32[840,128]{1,0:T(8,128)S(1)}, f32[840,128]{1,0:T(8,128)S(1)}, u32[]{:S(2)}, u32[]{:S(2)}) collective-permute-start(f32[840,128]{1,0:T(8,128)S(1)} %get-tuple-element.14), channel_id=1, source_target_pairs={{0,1},{1,2},{2,3},{3,4},{4,5},{5,6},{6,7},{7,8},{8,9},{9,10},{10,1... | collective-permute-start | bytes 1290248 | tf_op jit(solution)/shard_map/ppermute | solution.py:393
  25.7 5.1 %collective-permute-done.2.below = f32[840,128]{1,0:T(8,128)S(1)} collective-permute-done((f32[840,128]{1,0:T(8,128)S(1)}, f32[840,128]{1,0:T(8,128)S(1)}, u32[]{:S(2)}, u32[]{:S(2)}) %collective-permute-start.2) | collective-permute-done | bytes 430112 | tf_op jit(solution)/shard_map/ppermute | solution.py:393
  30.8 2.8 %collective-permute-done.3.above = f32[840,128]{1,0:T(8,128)S(1)} collective-permute-done((f32[840,128]{1,0:T(8,128)S(1)}, f32[840,128]{1,0:T(8,128)S(1)}, u32[]{:S(2)}, u32[]{:S(2)}) %collective-permute-start.3) | collective-permute-done | bytes 430112 | tf_op jit(solution)/shard_map/ppermute | solution.py:393
  33.6 8.8 %shard_map.52 = (f32[48,96,128]{2,1,0:T(8,128)S(1)}, f32[42,96,128]{2,1,0:T(8,128)S(1)}, f32[32,64,128]{2,1,0:T(8,128)}, f32[256,128]{1,0:T(8,128)}) custom-call(f32[32,64,128]{2,1,0:T(8,128)S(1)} %copy-done.1, f32[32,64,128]{2,1,0:T(8,128)S(1)} %get-tuple-element.11.source, f32[1088,128]{1,0:T(8,128)S(1)} %collective-permute-done.before, ...), custom_call_target="tpu_custom_call" | custom-call | tf_op jit(solution)/shard_map/pallas_call | solution.py:377
  42.4 1.3 %copy-done.2 = f32[42,96,128]{2,1,0:T(8,128)} copy-done((f32[42,96,128]{2,1,0:T(8,128)}, f32[42,96,128]{2,1,0:T(8,128)S(1)}, u32[]{:S(2)}) %copy-start.2) | copy-done | bytes 2064408
  43.7 13.3 %all-to-all-start = ((f32[256,1,128]{2,1,0:T(1,128)}), f32[256,1,128]{2,1,0:T(1,128)S(1)}, u32[]{:S(2)}, u32[]{:S(2)}) async-start(f32[256,1,128]{2,1,0:T(1,128)} %bitcast.1), calls=%async_computation | async-start | bytes 262144 | tf_op jit(solution)/shard_map/all_to_all | solution.py:413
  57.1 1.6 %copy-done.3 = f32[42,96,128]{2,1,0:T(8,128)S(1)} copy-done((f32[42,96,128]{2,1,0:T(8,128)S(1)}, f32[42,96,128]{2,1,0:T(8,128)}, u32[]{:S(2)}) %copy-start.3) | copy-done | bytes 2064408
  58.6 12.9 %shard_map.53.rate = f32[42,96,128]{2,1,0:T(8,128)S(1)} custom-call(f32[48,96,128]{2,1,0:T(8,128)S(1)} %get-tuple-element.16.level, f32[42,96,128]{2,1,0:T(8,128)S(1)} %copy-done.3), custom_call_target="tpu_custom_call" | custom-call | tf_op jit(solution)/shard_map/pallas_call | solution.py:377
  71.5 1.3 %copy-done.5 = f32[42,96,128]{2,1,0:T(8,128)} copy-done((f32[42,96,128]{2,1,0:T(8,128)}, f32[42,96,128]{2,1,0:T(8,128)S(1)}, u32[]{:S(2)}) %copy-start.5) | copy-done | bytes 2064408
  72.8 0.0 all-to-all-done
  72.8 1.6 %copy-done.4 = f32[42,96,128]{2,1,0:T(8,128)S(1)} copy-done((f32[42,96,128]{2,1,0:T(8,128)S(1)}, f32[42,96,128]{2,1,0:T(8,128)}, u32[]{:S(2)}) %copy-start.4) | copy-done | bytes 2064408
  74.4 1.6 %copy-done.6 = f32[42,96,128]{2,1,0:T(8,128)S(1)} copy-done((f32[42,96,128]{2,1,0:T(8,128)S(1)}, f32[42,96,128]{2,1,0:T(8,128)}, u32[]{:S(2)}) %copy-start.6) | copy-done | bytes 2064408
  76.0 15.8 %shard_map.54 = f32[32,64,128]{2,1,0:T(8,128)} custom-call(f32[48,96,128]{2,1,0:T(8,128)S(1)} %get-tuple-element.16.level, f32[42,96,128]{2,1,0:T(8,128)S(1)} %copy-done.4, f32[42,96,128]{2,1,0:T(8,128)S(1)} %copy-done.6, f32[256,128]{1,0:T(8,128)S(1)} %bitcast.4), custom_call_target="tpu_custom_call" | custom-call | tf_op jit(solution)/shard_map/pallas_call | solution.py:377
  (9 shorter events, 0.0 us)
Async XLA Ops:
  0.6 1.2 %copy-start = (f32[32,64,128]{2,1,0:T(8,128)S(1)}, f32[32,64,128]{2,1,0:T(8,128)}, u32[]{:S(2)}) copy-start(f32[32,64,128]{2,1,0:T(8,128)} %level.5) | copy-start | bytes 3145732
  1.9 1.2 %copy-start.7 = (f32[32,64,128]{2,1,0:T(8,128)S(1)}, f32[32,64,128]{2,1,0:T(8,128)}, u32[]{:S(2)}) copy-start(f32[32,64,128]{2,1,0:T(8,128)} %stress.1) | copy-start | bytes 3145732
  3.1 1.2 %copy-start.8 = (s32[32,64,128]{2,1,0:T(8,128)S(1)}, s32[32,64,128]{2,1,0:T(8,128)}, u32[]{:S(2)}) copy-start(s32[32,64,128]{2,1,0:T(8,128)} %materials.1) | copy-start | bytes 3145732
  4.7 28.9 %copy-start.1 = (f32[32,64,128]{2,1,0:T(8,128)S(1)}, f32[32,64,128]{2,1,0:T(8,128)}, u32[]{:S(2)}) copy-start(f32[32,64,128]{2,1,0:T(8,128)} %level.5) | copy-start | bytes 3145732
  4.7 16.2 %collective-permute-start = (f32[1088,128]{1,0:T(8,128)S(1)}, f32[1088,128]{1,0:T(8,128)S(1)}, u32[]{:S(2)}, u32[]{:S(2)}) collective-permute-start(f32[1088,128]{1,0:T(8,128)S(1)} %get-tuple-element.12), channel_id=1, source_target_pairs={{0,16},{16,32},{32,48},{48,64},{64,80},{80,96},{96,112},{112,128},... | collective-permute-start | bytes 1671176 | tf_op jit(solution)/shard_map/ppermute | solution.py:393
  6.9 14.0 %collective-permute-start.1 = (f32[1088,128]{1,0:T(8,128)S(1)}, f32[1088,128]{1,0:T(8,128)S(1)}, u32[]{:S(2)}, u32[]{:S(2)}) collective-permute-start(f32[1088,128]{1,0:T(8,128)S(1)} %get-tuple-element.13), channel_id=1, source_target_pairs={{0,240},{16,0},{32,16},{48,32},{64,48},{80,64},{96,80},{112,96},{1... | collective-permute-start | bytes 1671176 | tf_op jit(solution)/shard_map/ppermute | solution.py:393
  21.0 9.8 %collective-permute-start.2 = (f32[840,128]{1,0:T(8,128)S(1)}, f32[840,128]{1,0:T(8,128)S(1)}, u32[]{:S(2)}, u32[]{:S(2)}) collective-permute-start(f32[840,128]{1,0:T(8,128)S(1)} %get-tuple-element.14), channel_id=1, source_target_pairs={{0,1},{1,2},{2,3},{3,4},{4,5},{5,6},{6,7},{7,8},{8,9},{9,10},{10,1... | collective-permute-start | bytes 1290248 | tf_op jit(solution)/shard_map/ppermute | solution.py:393
  25.7 7.9 %collective-permute-start.3 = (f32[840,128]{1,0:T(8,128)S(1)}, f32[840,128]{1,0:T(8,128)S(1)}, u32[]{:S(2)}, u32[]{:S(2)}) collective-permute-start(f32[840,128]{1,0:T(8,128)S(1)} %get-tuple-element.15), channel_id=1, source_target_pairs={{0,15},{1,0},{2,1},{3,2},{4,3},{5,4},{6,5},{7,6},{8,7},{9,8},{10,9... | collective-permute-start | bytes 1290248 | tf_op jit(solution)/shard_map/ppermute | solution.py:393
  42.4 1.3 %copy-start.2 = (f32[42,96,128]{2,1,0:T(8,128)}, f32[42,96,128]{2,1,0:T(8,128)S(1)}, u32[]{:S(2)}) copy-start(f32[42,96,128]{2,1,0:T(8,128)S(1)} %get-tuple-element.17.speed) | copy-start | bytes 6193156
  43.7 29.1 %all-to-all-start = ((f32[256,1,128]{2,1,0:T(1,128)}), f32[256,1,128]{2,1,0:T(1,128)S(1)}, u32[]{:S(2)}, u32[]{:S(2)}) async-start(f32[256,1,128]{2,1,0:T(1,128)} %bitcast.1), calls=%async_computation | async-start | bytes 262144 | tf_op jit(solution)/shard_map/all_to_all | solution.py:413
  57.0 1.6 %copy-start.3 = (f32[42,96,128]{2,1,0:T(8,128)S(1)}, f32[42,96,128]{2,1,0:T(8,128)}, u32[]{:S(2)}) copy-start(f32[42,96,128]{2,1,0:T(8,128)} %copy-done.2) | copy-start | bytes 6193156
  71.5 1.3 %copy-start.5 = (f32[42,96,128]{2,1,0:T(8,128)}, f32[42,96,128]{2,1,0:T(8,128)S(1)}, u32[]{:S(2)}) copy-start(f32[42,96,128]{2,1,0:T(8,128)S(1)} %shard_map.53.rate) | copy-start | bytes 6193156
  72.8 1.6 %copy-start.4 = (f32[42,96,128]{2,1,0:T(8,128)S(1)}, f32[42,96,128]{2,1,0:T(8,128)}, u32[]{:S(2)}) copy-start(f32[42,96,128]{2,1,0:T(8,128)} %copy-done.2) | copy-start | bytes 6193156
  74.4 1.6 %copy-start.6 = (f32[42,96,128]{2,1,0:T(8,128)S(1)}, f32[42,96,128]{2,1,0:T(8,128)}, u32[]{:S(2)}) copy-start(f32[42,96,128]{2,1,0:T(8,128)} %copy-done.5) | copy-start | bytes 6193156

commit v3 on v2

--- a/solution.py
+++ b/solution.py
@@ -193,98 +193,73 @@
     lax.fori_loop(0, planes, body, 0, unroll=2)
 
 
-def pack_x(level, stress, materials, source, low, high):
+def copies(pairs, sems):
+    started = [pltpu.make_async_copy(s, d, sems.at[k]) for k, (s, d) in enumerate(pairs)]
+    for copy in started:
+        copy.start()
+    return started
+
+
+def weigh(stress, materials):
+    weight = jnp.where(materials == 0, 1.0, jnp.where(materials == 1, 0.6, 0.0))
+    return weight.astype(jnp.float32) * stress
+
+
+def pack_source(source, before, after, low, high):
+    nx, ny, _ = source.shape
+    wide = nx + 2 * SRC
+    rest = wide * 8
+    planes = [before[k] for k in range(SRC)] + [source[k] for k in range(nx)]
+    planes = planes + [after[k] for k in range(SRC)]
+    for k, plane in enumerate(planes):
+        low[k * 8 : k * 8 + 8] = plane[0:8]
+        high[k * 8 : k * 8 + 8] = plane[ny - 8 : ny]
+        low[rest + k : rest + k + 1] = plane[8:9]
+        high[rest + k : rest + k + 1] = plane[ny - 9 : ny - 8]
+    tail = low.shape[0] - rest - wide
+    low[rest + wide :] = jnp.zeros((tail, 128), jnp.float32)
+    high[rest + wide :] = jnp.zeros((tail, 128), jnp.float32)
+
+
+def pack_level(level, before, after, order, low, high):
     nx, ny, _ = level.shape
-
-    def weigh(x, _):
-        label = materials[x]
-        weight = jnp.where(label == 0, 1.0, jnp.where(label == 1, 0.6, 0.0)).astype(jnp.float32)
-        source[x] = weight * stress[x]
-        return _
-
-    lax.fori_loop(0, nx, weigh, 0)
-    for k in range(SRC):
-        low[pl.ds(k * ny, ny), :] = source[k]
-        high[pl.ds(k * ny, ny), :] = source[nx - SRC + k]
-    for k in range(LEV):
-        low[pl.ds((SRC + k) * ny, ny), :] = level[k]
-        high[pl.ds((SRC + k) * ny, ny), :] = level[nx - LEV + k]
-
-
-def pack_y(level, source, before, after, low, high):
-    nx, ny, _ = level.shape
+    for k in range(nx + 2 * LEV):
+        ref, j = (level, k - LEV)
+        if k < LEV:
+            ref, j = (before, k)
+        elif k >= LEV + nx:
+            ref, j = (after, k - LEV - nx)
+        low[k] = ref[j, 0:8]
+        high[k] = ref[j, ny - 8 : ny]
+
+
+def velocity(
+    source, before, after, below_any, above_any, order, speed_hbm, own_speed, peaks,
+    src, one, two, speed, below, above, sems,
+):
+    nx, ny, _ = source.shape
     wide = nx + 2 * SRC
-    tall = nx + 2 * LEV
-    extra = tall * 8 + wide * 8
-
-    def put_level(k, piece_low, piece_high):
-        low[pl.ds(k * 8, 8), :] = piece_low
-        high[pl.ds(k * 8, 8), :] = piece_high
-
-    def put_source(k, piece_low, row_low, piece_high, row_high):
-        low[pl.ds((tall + k) * 8, 8), :] = piece_low
-        high[pl.ds((tall + k) * 8, 8), :] = piece_high
-        low[pl.ds(extra + k, 1), :] = row_low
-        high[pl.ds(extra + k, 1), :] = row_high
-
-    for k in range(nx):
-        put_level(LEV + k, level[k, 0:8], level[k, ny - 8 : ny])
-        put_source(
-            SRC + k,
-            source[k, 0:8],
-            source[k, 8:9],
-            source[k, ny - 8 : ny],
-            source[k, ny - 9 : ny - 8],
-        )
-    for ref, at in ((before, 0), (after, 1)):
-        for k in range(SRC):
-            b = k * ny
-            put_source(
-                k + at * (SRC + nx),
-                ref[b : b + 8],
-                ref[b + 8 : b + 9],
-                ref[b + ny - 8 : b + ny],
-                ref[b + ny - 9 : b + ny - 8],
-            )
-        for k in range(LEV):
-            b = (SRC + k) * ny
-            put_level(k + at * (LEV + nx), ref[b : b + 8], ref[b + ny - 8 : b + ny])
-    low[pl.ds(extra + wide, 8 - wide % 8), :] = jnp.zeros((8 - wide % 8, 128), jnp.float32)
-    high[pl.ds(extra + wide, 8 - wide % 8), :] = jnp.zeros((8 - wide % 8, 128), jnp.float32)
-
-
-def extend(level, source, before, after, below, above, level_out, source_out):
-    nx, ny, _ = level.shape
-    wide = nx + 2 * SRC
-    tall = nx + 2 * LEV
-    extra = tall * 8 + wide * 8
     top = OWN + ny
-    for k in range(nx):
-        level_out[LEV + k, OWN:top] = level[k]
-        source_out[SRC + k, OWN:top] = source[k]
-    for ref, at in ((before, 0), (after, 1)):
-        for k in range(SRC):
-            source_out[k + at * (SRC + nx), OWN:top] = ref[k * ny : (k + 1) * ny]
-        for k in range(LEV):
-            b = (SRC + k) * ny
-            level_out[k + at * (LEV + nx), OWN:top] = ref[b : b + ny]
-    for k in range(tall):
-        level_out[k, OWN - 8 : OWN] = below[k * 8 : k * 8 + 8]
-        level_out[k, top : top + 8] = above[k * 8 : k * 8 + 8]
+    rest = wide * 8
+    arrivals = copies(
+        [
+            (below_any, below),
+            (above_any, above),
+            (source, src.at[pl.ds(SRC, nx), pl.ds(OWN, ny)]),
+            (before, src.at[pl.ds(0, SRC), pl.ds(OWN, ny)]),
+            (after, src.at[pl.ds(SRC + nx, SRC), pl.ds(OWN, ny)]),
+        ],
+        sems,
+    )
+    for arrival in arrivals[:2]:
+        arrival.wait()
     for k in range(wide):
-        b = (tall + k) * 8
-        source_out[k, OWN - 8 : OWN] = below[b : b + 8]
-        source_out[k, top : top + 8] = above[b : b + 8]
-        source_out[k, OWN - 9 : OWN - 8] = below[extra + k : extra + k + 1]
-        source_out[k, top + 8 : top + 9] = above[extra + k : extra + k + 1]
-
-
-def velocity(
-    level, source, before, after, below, above, level_out, speed, own_speed, peaks, src, one, two
-):
-    extend(level, source, before, after, below, above, level_out, src)
-    nx, ny, _ = level.shape
-    wide = nx + 2 * SRC
+        src[k, OWN - 8 : OWN] = below[k * 8 : k * 8 + 8]
+        src[k, top : top + 8] = above[k * 8 : k * 8 + 8]
+        src[k, OWN - 9 : OWN - 8] = below[rest + k : rest + k + 1]
+        src[k, top + 8 : top + 9] = above[rest + k : rest + k + 1]
+    for arrival in arrivals[2:]:
+        arrival.wait()
     coefficients = velocity_polynomial()
     step = (ny + 2 * (SRC - 1)) // 8
     start = OWN - (SRC - 1)
@@ -315,6 +290,8 @@
     sweep(one, two, 0, 2, wide - 2, None, coefficients[2])
     sweep(two, one, 0, 3, wide - 3, None, coefficients[1])
     sweep(one, speed, SRC - SPD, 4, wide - 4, None, coefficients[0])
+    out = pltpu.make_async_copy(speed, speed_hbm, sems.at[0])
+    out.start()
 
     def largest(x, carry):
         mine = speed[SPD + x, OWN : OWN + ny]
@@ -323,21 +300,35 @@
 
     top = lax.fori_loop(0, nx, largest, jnp.zeros((ny, 128), jnp.float32))
     peaks[...] = jnp.broadcast_to(jnp.max(top), peaks.shape)
-
-
-def first_stage(level, speed, rate, acc):
-    planes = rate.shape[0]
-    step = 10
-    start = OWN - SPD
-
-    def emit(x, t, value):
-        rate[x, pl.ds(start + t, 8, stride=step), :] = value
-
-    weno_rates(level, LEV - SPD, speed, 0, acc, planes, start, step, emit)
-
-
-def second_stage(level, speed, rate, peaks, new_level, stage, advected, swept, acc):
+    out.wait()
+
+
+def evolve(
+    own_level, before, after, below, above, speed_hbm, peaks, new_level,
+    level, speed, rate, stage, advected, swept, acc, sems,
+):
     nx, ny, _ = new_level.shape
+    tall = nx + 2 * LEV
+    rows = pl.ds(OWN, ny)
+    arrivals = copies(
+        [
+            (own_level, level.at[pl.ds(LEV, nx), rows]),
+            (before, level.at[pl.ds(0, LEV), rows]),
+            (after, level.at[pl.ds(LEV + nx, LEV), rows]),
+            (below, level.at[pl.ds(0, tall), pl.ds(OWN - 8, 8)]),
+            (above, level.at[pl.ds(0, tall), pl.ds(OWN + ny, 8)]),
+            (speed_hbm, speed),
+        ],
+        sems,
+    )
+    for arrival in arrivals:
+        arrival.wait()
+
+    def emit_rate(x, t, value):
+        rate[x, pl.ds(OWN - SPD + t, 8, stride=10), :] = value
+
+    weno_rates(level, LEV - SPD, speed, 0, acc, nx + 2 * SPD, OWN - SPD, 10, emit_rate)
+
     peak = jnp.max(peaks[...], axis=0, keepdims=True)
     time_step = courant / (peak + 1e-06)
     step_row = jnp.broadcast_to(time_step, (8, 128))
@@ -370,54 +361,94 @@
     reinit_sweep(swept, 1, advected, 2, nx, OWN, ny // 8, emit_two)
 
 
+BIG = 56
 VM = pl.BlockSpec(memory_space=pltpu.VMEM)
-
-
-def call(kernel, outs, scratch, args, megabytes=18):
+HBM = pl.BlockSpec(memory_space=pltpu.HBM)
+ANY = pl.BlockSpec(memory_space=pl.ANY)
+
+
+def call(kernel, outs, scratch, args, megabytes, copied=0):
+    ins = [a if isinstance(a, tuple) else (a, VM) for a in args]
+    outs = [o if isinstance(o[0], tuple) else (o, VM) for o in outs]
+    scratch = [s if isinstance(s[0], tuple) else (s, jnp.float32) for s in scratch]
+    scratch_shapes = [pltpu.VMEM(shape, dtype) for shape, dtype in scratch]
+    if copied:
+        scratch_shapes.append(pltpu.SemaphoreType.DMA((copied,)))
     return pl.pallas_call(
         kernel,
-        out_shape=[jax.ShapeDtypeStruct(s, jnp.float32) for s in outs],
-        in_specs=[VM] * len(args),
-        out_specs=[VM] * len(outs),
-        scratch_shapes=[pltpu.VMEM(s, jnp.float32) for s in scratch],
+        out_shape=[jax.ShapeDtypeStruct(shape, jnp.float32) for shape, _ in outs],
+        in_specs=[place for _, place in ins],
+        out_specs=[place for _, place in outs],
+        scratch_shapes=scratch_shapes,
         compiler_params=pltpu.CompilerParams(vmem_limit_bytes=megabytes * 1024 * 1024),
-    )(*args)
+    )(*[array for array, _ in ins])
 
 
 def local(level_set, stress_jump, materials):
-    nx, ny, nz = level_set.shape
+    tile = level_set.shape
+    nx, ny, nz = tile
     wide, tall, mid = nx + 2 * SRC, nx + 2 * LEV, nx + 2 * SPD
     size_x, size_y = lax.axis_size("gx"), lax.axis_size("gy")
+    devices = size_x * size_y
 
     def shift(value, axis, size, by):
         return lax.ppermute(value, axis, [(i, (i + by) % size) for i in range(size)])
 
-    message = ((SRC + LEV) * ny, nz)
-    source, low, high = call(
-        pack_x, [(nx, ny, nz), message, message], [], (level_set, stress_jump, materials)
-    )
-    after = shift(low, "gx", size_x, -1)
-    before = shift(high, "gx", size_x, 1)
-    message = (tall * 8 + wide * 8 + (wide + 7) // 8 * 8, nz)
-    low, high = call(pack_y, [message, message], [], (level_set, source, before, after))
-    above = shift(low, "gy", size_y, -1)
-    below = shift(high, "gy", size_y, 1)
-    devices = size_x * size_y
-    level, speed, normal_speed, peaks = call(
+    low = weigh(stress_jump[:SRC], materials[:SRC])
+    high = weigh(stress_jump[nx - SRC :], materials[nx - SRC :])
+    source_after = shift(low, "gx", size_x, -1)
+    source_before = shift(high, "gx", size_x, 1)
+    source = weigh(stress_jump, materials)
+    level_low, level_high, _, _ = lax.optimization_barrier(
+        (level_set[:LEV], level_set[nx - LEV :], low, high)
+    )
+    level_after = shift(level_low, "gx", size_x, -1)
+    level_before = shift(level_high, "gx", size_x, 1)
+    message = rows_message = (wide * 8 + (wide + 7) // 8 * 8, nz)
+    low, high = call(
+        pack_source, [message, message], [], (source, source_before, source_after), 8
+    )
+    source_above = shift(low, "gy", size_y, -1)
+    source_below = shift(high, "gy", size_y, 1)
+    message = (tall, 8, nz)
+    low, high = call(
+        pack_level,
+        [message, message],
+        [],
+        (level_set, level_before, level_after, (low, ANY)),
+        8,
+    )
+    level_above = shift(low, "gy", size_y, -1)
+    level_below = shift(high, "gy", size_y, 1)
+    speed, normal_speed, peaks = call(
         velocity,
-        [(tall, ROWS, nz), (mid, ROWS, nz), (nx, ny, nz), (devices, nz)],
-        [(wide, ROWS, nz)] * 3,
-        (level_set, source, before, after, below, above),
-        megabytes=24,
-    )
+        [((mid, ROWS, nz), HBM), tile, (devices, nz)],
+        [(wide, ROWS, nz)] * 3 + [(mid, ROWS, nz), rows_message, rows_message],
+        [(a, ANY) for a in (source, source_before, source_after, source_below, source_above, low)],
+        BIG,
+        copied=5,
+    )
+    peaks, level_above, level_below = lax.optimization_barrier((peaks, level_above, level_below))
     peaks = lax.all_to_all(peaks.reshape(devices, 1, nz), ("gx", "gy"), 0, 0)
-    peaks = peaks.reshape(devices, nz)
-    (rate,) = call(first_stage, [(mid, ROWS, nz)], [(mid, 10, 8, nz)], (level, speed))
     (new_level,) = call(
-        second_stage,
-        [(nx, ny, nz)],
-        [(mid, ROWS, nz), (nx + 4, ROWS, nz), (nx + 2, ROWS, nz), (nx + 4, 9, 8, nz)],
-        (level, speed, rate, peaks),
+        evolve,
+        [tile],
+        [
+            (tall, ROWS, nz),
+            (mid, ROWS, nz),
+            (mid, ROWS, nz),
+            (mid, ROWS, nz),
+            (nx + 4, ROWS, nz),
+            (nx + 2, ROWS, nz),
+            (mid, 10, 8, nz),
+        ],
+        [
+            (a, ANY)
+            for a in (level_set, level_before, level_after, level_below, level_above, speed)
+        ]
+        + [peaks.reshape(devices, nz)],
+        BIG,
+        copied=6,
     )
     return (new_level, normal_speed)
 

time: 92.2 us -> 95.2 us (1.033)
  blocking collectives: 0 us -> 27.4 us
  waiting for transfers between devices: 18.2 us -> 0.7 us
  local copies, waits for them, and re-layouts: 11 us -> 1.4 us
  starting transfers between devices: 24 us -> 18.7 us
  Pallas kernels: 37.9 us -> 43.1 us
  other arithmetic: 0 us -> 2.93 us
    all_to_all x0 -> x1, blocking collectives: none -> 27.4 us  [local(): peaks = lax.all_to_all(peaks.reshape(devices, 1, nz), ('gx', 'gy'), 0, 0)]
    ppermute x4 -> x8, waiting for transfers between devices: 18.2 us -> 0.7 us  [shift(): lax.ppermute(value, axis, [(i, (i + by) % size) for i in range(size)])]
    all_to_all x1 -> x0, starting transfers between devices: 13.3 us -> none  [local(): peaks = lax.all_to_all(peaks.reshape(devices, 1, nz), ('gx', 'gy'), 0, 0)]
    unnamed x18 -> x24, local copies, waits for them, and re-layouts: 11 us -> 1.37 us
    ppermute x4 -> x8, starting transfers between devices: 10.7 us -> 18.7 us  [shift(): lax.ppermute(value, axis, [(i, (i + by) % size) for i in range(size)])]
    pallas_call x5 -> x4, Pallas kernels: 37.9 us -> 43.1 us  [call(): pl.pallas_call(kernel, out_shape=[jax.ShapeDtypeStruct(shape, jnp.float32...]
    mul x0 -> x2, other arithmetic: none -> 2.93 us  [weigh(): return weight.astype(jnp.float32) * stress]
  transfers between devices with their start and end apart: 5 -> 8, of which waited for: 3 -> 1; matrix products, arithmetic and copies ran while one was open for 0% -> 2% of each run, Pallas kernels for 14% -> 12%
where the time goes in v3:
time: 95.2 us; the launch traced here: 94.9 us
  Pallas kernels  43.1 us (45%)
  blocking collectives  27.4 us (29%)
  starting transfers between devices  18.7 us (20%)
  other arithmetic  2.93 us (3%)
  local copies, waits for them, and re-layouts  1.4 us (1%)
    pallas_call x4, Pallas kernels, call(): pl.pallas_call(kernel, out_shape=[jax.ShapeDtypeStruct(shape, jnp.float32...  43.1 us
    all_to_all x1, blocking collectives, local(): peaks = lax.all_to_all(peaks.reshape(devices, 1, nz), ('gx', 'gy'), 0, 0)  27.4 us
    ppermute x8, starting transfers between devices, shift(): lax.ppermute(value, axis, [(i, (i + by) % size) for i in range(size)])  18.7 us
    mul x2, other arithmetic, weigh(): return weight.astype(jnp.float32) * stress  2.93 us
  transfers between devices with their start and end apart: 8, of which 1 were waited for; matrix products, arithmetic and copies ran while one was open for 2% of the time, Pallas kernels for 12%

profile of v3, /device:TPU:1, one launch (start us, length us, event | category | flops | bytes accessed | tf_op | source)
XLA Modules:
  0.0 94.9 jit_solution(55654006280247237)
XLA Ops:
  0.6 0.0 copy-start.1
  0.7 1.5 %slice_multiply_fusion = (f32[9,64,128]{2,1,0:T(8,128)S(1)}, f32[9,64,128]{2,1,0:T(8,128)S(1)}) fusion(f32[32,64,128]{2,1,0:T(8,128)} %param.4, s32[32,64,128]{2,1,0:T(8,128)} %param.5), kind=kLoop, calls=%fused_computation.1 | loop fusion | flops 737280 | bytes 1769472 | tf_op jit(solution)/shard_map/mul | solution.py:205
  2.1 2.2 %collective-permute-start.2 = (f32[9,64,128]{2,1,0:T(8,128)S(1)}, f32[9,64,128]{2,1,0:T(8,128)S(1)}, u32[]{:S(2)}, u32[]{:S(2)}) collective-permute-start(f32[9,64,128]{2,1,0:T(8,128)S(1)} %get-tuple-element.26), channel_id=1, source_target_pairs={{0,16},{16,32},{32,48},{48,64},{64,80},{80,96},{96,112},{112,128},... | collective-permute-start | bytes 884744 | tf_op jit(solution)/shard_map/ppermute | solution.py:395
  4.3 3.7 %collective-permute-start.3 = (f32[9,64,128]{2,1,0:T(8,128)S(1)}, f32[9,64,128]{2,1,0:T(8,128)S(1)}, u32[]{:S(2)}, u32[]{:S(2)}) collective-permute-start(f32[9,64,128]{2,1,0:T(8,128)S(1)} %get-tuple-element.27), channel_id=1, source_target_pairs={{0,240},{16,0},{32,16},{48,32},{64,48},{80,64},{96,80},{112,96},{1... | collective-permute-start | bytes 884744 | tf_op jit(solution)/shard_map/ppermute | solution.py:395
  8.1 0.1 collective-permute-start
  8.2 4.8 %collective-permute-start.1 = (f32[8,64,128]{2,1,0:T(8,128)S(1)}, f32[8,64,128]{2,1,0:T(8,128)S(1)}, u32[]{:S(2)}, u32[]{:S(2)}) collective-permute-start(f32[8,64,128]{2,1,0:T(8,128)S(1)} %get-tuple-element.15), channel_id=1, source_target_pairs={{0,240},{16,0},{32,16},{48,32},{64,48},{80,64},{96,80},{112,96},{1... | collective-permute-start | bytes 786440 | tf_op jit(solution)/shard_map/ppermute | solution.py:395
  13.0 1.4 %select_multiply_fusion.source = f32[32,64,128]{2,1,0:T(8,128)S(1)} fusion(f32[32,64,128]{2,1,0:T(8,128)S(1)} %copy-done.7, s32[32,64,128]{2,1,0:T(8,128)} %param.5), kind=kLoop, calls=%fused_computation | loop fusion | flops 1310720 | bytes 3145728 | tf_op jit(solution)/shard_map/mul | solution.py:205
  14.4 0.0 copy-start
  14.5 0.0 collective-permute-done.3.after
  14.5 0.1 shard_map.50
  14.5 3.3 %collective-permute-start.5 = (f32[456,128]{1,0:T(8,128)S(1)}, f32[456,128]{1,0:T(8,128)S(1)}, u32[]{:S(2)}, u32[]{:S(2)}) collective-permute-start(f32[456,128]{1,0:T(8,128)S(1)} %get-tuple-element.17.order), channel_id=1, source_target_pairs={{0,15},{1,0},{2,1},{3,2},{4,3},{5,4},{6,5},{7,6},{8,7},{9,8},{10,9... | collective-permute-start | bytes 700424 | tf_op jit(solution)/shard_map/ppermute | solution.py:395
  17.9 0.7 collective-permute-start.4
  18.5 0.7 collective-permute-done.before
  19.3 2.3 %collective-permute-start.6 = (f32[48,8,128]{2,1,0:T(8,128)S(1)}, f32[48,8,128]{2,1,0:T(8,128)S(1)}, u32[]{:S(2)}, u32[]{:S(2)}) collective-permute-start(f32[48,8,128]{2,1,0:T(8,128)S(1)} %get-tuple-element.18.order), channel_id=1, source_target_pairs={{0,15},{1,0},{2,1},{3,2},{4,3},{5,4},{6,5},{7,6},{8,7},{9,8},{10,9... | collective-permute-start | bytes 589832 | tf_op jit(solution)/shard_map/ppermute | solution.py:395
  21.6 1.5 %collective-permute-start.7 = (f32[48,8,128]{2,1,0:T(8,128)S(1)}, f32[48,8,128]{2,1,0:T(8,128)S(1)}, u32[]{:S(2)}, u32[]{:S(2)}) collective-permute-start(f32[48,8,128]{2,1,0:T(8,128)S(1)} %get-tuple-element.20), channel_id=1, source_target_pairs={{0,1},{1,2},{2,3},{3,4},{4,5},{5,6},{6,7},{7,8},{8,9},{9,10},{10,1... | collective-permute-start | bytes 589832 | tf_op jit(solution)/shard_map/ppermute | solution.py:395
  23.2 0.0 collective-permute-done.5.above_any
  23.2 0.0 collective-permute-done.4.below_any
  23.2 0.6 copy-done.8
  23.9 0.7 copy-done.9
  24.5 11.1 %shard_map.52 = (f32[42,96,128]{2,1,0:T(8,128)}, f32[32,64,128]{2,1,0:T(8,128)}, f32[256,128]{1,0:T(8,128)}) custom-call(f32[32,64,128]{2,1,0:T(8,128)} %copy-done, f32[9,64,128]{2,1,0:T(8,128)} %copy-done.2, f32[9,64,128]{2,1,0:T(8,128)} %copy-done.3, f32[456,128]{1,0:T(8,128)} %copy-done.9, f32[456,128]{1,0:T(8,128)} %copy-done.8, f32[48,8,128]{2,1,0:T(8,128)} %copy-done.6), custom_call_target="tpu_custom_call" | custom-call | tf_op jit(solution)/shard_map/pallas_call | solution.py:377
  35.6 0.0 collective-permute-done.6.above
  35.7 0.0 collective-permute-done.7.below
  35.7 27.4 %all_to_all.5 = f32[256,1,128]{2,1,0:T(1,128)} all-to-all(f32[256,1,128]{2,1,0:T(1,128)} %bitcast.5), channel_id=1, replica_groups=mesh['gx'=16,'gy'=16] {'gx','gy'}, dimensions={0} | all-to-all | bytes 262144 | tf_op jit(solution)/shard_map/all_to_all | solution.py:432
  63.1 31.9 %shard_map.53 = f32[32,64,128]{2,1,0:T(8,128)} custom-call(f32[32,64,128]{2,1,0:T(8,128)} %own_level.1, f32[8,64,128]{2,1,0:T(8,128)} %copy-done.4, f32[8,64,128]{2,1,0:T(8,128)} %copy-done.5, f32[48,8,128]{2,1,0:T(8,128)} %copy-done.11, f32[48,8,128]{2,1,0:T(8,128)} %copy-done.10, f32[42,96,128]{2,1,0:T(8,128)} %get-tuple-element.23.speed_hbm, ...), custom_call_target="tpu_custom_call" | custom-call | tf_op jit(solution)/shard_map/pallas_call | solution.py:377
  (24 shorter events, 0.1 us)
Async XLA Ops:
  0.6 7.4 %copy-start.1 = (f32[32,64,128]{2,1,0:T(8,128)S(1)}, f32[32,64,128]{2,1,0:T(8,128)}, u32[]{:S(2)}) copy-start(f32[32,64,128]{2,1,0:T(8,128)} %own_level.1) | copy-start | bytes 3145732
  0.6 12.3 %copy-start.7 = (f32[32,64,128]{2,1,0:T(8,128)S(1)}, f32[32,64,128]{2,1,0:T(8,128)}, u32[]{:S(2)}) copy-start(f32[32,64,128]{2,1,0:T(8,128)} %param.4) | copy-start | bytes 3145732
  2.1 12.3 %collective-permute-start.2 = (f32[9,64,128]{2,1,0:T(8,128)S(1)}, f32[9,64,128]{2,1,0:T(8,128)S(1)}, u32[]{:S(2)}, u32[]{:S(2)}) collective-permute-start(f32[9,64,128]{2,1,0:T(8,128)S(1)} %get-tuple-element.26), channel_id=1, source_target_pairs={{0,16},{16,32},{32,48},{48,64},{64,80},{80,96},{96,112},{112,128},... | collective-permute-start | bytes 884744 | tf_op jit(solution)/shard_map/ppermute | solution.py:395
  4.3 10.1 %collective-permute-start.3 = (f32[9,64,128]{2,1,0:T(8,128)S(1)}, f32[9,64,128]{2,1,0:T(8,128)S(1)}, u32[]{:S(2)}, u32[]{:S(2)}) collective-permute-start(f32[9,64,128]{2,1,0:T(8,128)S(1)} %get-tuple-element.27), channel_id=1, source_target_pairs={{0,240},{16,0},{32,16},{48,32},{64,48},{80,64},{96,80},{112,96},{1... | collective-permute-start | bytes 884744 | tf_op jit(solution)/shard_map/ppermute | solution.py:395
  8.1 11.1 %collective-permute-start = (f32[8,64,128]{2,1,0:T(8,128)S(1)}, f32[8,64,128]{2,1,0:T(8,128)S(1)}, u32[]{:S(2)}, u32[]{:S(2)}) collective-permute-start(f32[8,64,128]{2,1,0:T(8,128)S(1)} %get-tuple-element.14), channel_id=1, source_target_pairs={{0,16},{16,32},{32,48},{48,64},{64,80},{80,96},{96,112},{112,128},... | collective-permute-start | bytes 786440 | tf_op jit(solution)/shard_map/ppermute | solution.py:395
  8.2 11.0 %collective-permute-start.1 = (f32[8,64,128]{2,1,0:T(8,128)S(1)}, f32[8,64,128]{2,1,0:T(8,128)S(1)}, u32[]{:S(2)}, u32[]{:S(2)}) collective-permute-start(f32[8,64,128]{2,1,0:T(8,128)S(1)} %get-tuple-element.15), channel_id=1, source_target_pairs={{0,240},{16,0},{32,16},{48,32},{64,48},{80,64},{96,80},{112,96},{1... | collective-permute-start | bytes 786440 | tf_op jit(solution)/shard_map/ppermute | solution.py:395
  14.4 8.8 %copy-start = (f32[32,64,128]{2,1,0:T(8,128)}, f32[32,64,128]{2,1,0:T(8,128)S(1)}, u32[]{:S(2)}) copy-start(f32[32,64,128]{2,1,0:T(8,128)S(1)} %select_multiply_fusion.source) | copy-start | bytes 3145732
  14.5 8.7 %copy-start.2 = (f32[9,64,128]{2,1,0:T(8,128)}, f32[9,64,128]{2,1,0:T(8,128)S(1)}, u32[]{:S(2)}) copy-start(f32[9,64,128]{2,1,0:T(8,128)S(1)} %collective-permute-done.2.before) | copy-start | bytes 884740
  14.5 8.7 %copy-start.3 = (f32[9,64,128]{2,1,0:T(8,128)}, f32[9,64,128]{2,1,0:T(8,128)S(1)}, u32[]{:S(2)}) copy-start(f32[9,64,128]{2,1,0:T(8,128)S(1)} %collective-permute-done.3.after) | copy-start | bytes 884740
  14.5 8.6 %collective-permute-start.5 = (f32[456,128]{1,0:T(8,128)S(1)}, f32[456,128]{1,0:T(8,128)S(1)}, u32[]{:S(2)}, u32[]{:S(2)}) collective-permute-start(f32[456,128]{1,0:T(8,128)S(1)} %get-tuple-element.17.order), channel_id=1, source_target_pairs={{0,15},{1,0},{2,1},{3,2},{4,3},{5,4},{6,5},{7,6},{8,7},{9,8},{10,9... | collective-permute-start | bytes 700424 | tf_op jit(solution)/shard_map/ppermute | solution.py:395
  17.9 5.3 %collective-permute-start.4 = (f32[456,128]{1,0:T(8,128)S(1)}, f32[456,128]{1,0:T(8,128)S(1)}, u32[]{:S(2)}, u32[]{:S(2)}) collective-permute-start(f32[456,128]{1,0:T(8,128)S(1)} %get-tuple-element.16), channel_id=1, source_target_pairs={{0,1},{1,2},{2,3},{3,4},{4,5},{5,6},{6,7},{7,8},{8,9},{9,10},{10,1... | collective-permute-start | bytes 700424 | tf_op jit(solution)/shard_map/ppermute | solution.py:395
  19.2 43.8 %copy-start.4 = (f32[8,64,128]{2,1,0:T(8,128)}, f32[8,64,128]{2,1,0:T(8,128)S(1)}, u32[]{:S(2)}) copy-start(f32[8,64,128]{2,1,0:T(8,128)S(1)} %collective-permute-done.before) | copy-start | bytes 786436
  19.2 43.8 %copy-start.5 = (f32[8,64,128]{2,1,0:T(8,128)}, f32[8,64,128]{2,1,0:T(8,128)S(1)}, u32[]{:S(2)}) copy-start(f32[8,64,128]{2,1,0:T(8,128)S(1)} %collective-permute-done.1.after) | copy-start | bytes 786436
  19.3 3.9 %copy-start.6 = (f32[48,8,128]{2,1,0:T(8,128)}, f32[48,8,128]{2,1,0:T(8,128)S(1)}, u32[]{:S(2)}) copy-start(f32[48,8,128]{2,1,0:T(8,128)S(1)} %get-tuple-element.18.order) | copy-start | bytes 589828
  19.3 16.4 %collective-permute-start.6 = (f32[48,8,128]{2,1,0:T(8,128)S(1)}, f32[48,8,128]{2,1,0:T(8,128)S(1)}, u32[]{:S(2)}, u32[]{:S(2)}) collective-permute-start(f32[48,8,128]{2,1,0:T(8,128)S(1)} %get-tuple-element.18.order), channel_id=1, source_target_pairs={{0,15},{1,0},{2,1},{3,2},{4,3},{5,4},{6,5},{7,6},{8,7},{9,8},{10,9... | collective-permute-start | bytes 589832 | tf_op jit(solution)/shard_map/ppermute | solution.py:395
  21.6 14.0 %collective-permute-start.7 = (f32[48,8,128]{2,1,0:T(8,128)S(1)}, f32[48,8,128]{2,1,0:T(8,128)S(1)}, u32[]{:S(2)}, u32[]{:S(2)}) collective-permute-start(f32[48,8,128]{2,1,0:T(8,128)S(1)} %get-tuple-element.20), channel_id=1, source_target_pairs={{0,1},{1,2},{2,3},{3,4},{4,5},{5,6},{6,7},{7,8},{8,9},{9,10},{10,1... | collective-permute-start | bytes 589832 | tf_op jit(solution)/shard_map/ppermute | solution.py:395
  23.2 0.7 copy-start.8
  23.9 0.7 copy-start.9
  35.6 27.4 %copy-start.10 = (f32[48,8,128]{2,1,0:T(8,128)}, f32[48,8,128]{2,1,0:T(8,128)S(1)}, u32[]{:S(2)}) copy-start(f32[48,8,128]{2,1,0:T(8,128)S(1)} %collective-permute-done.6.above) | copy-start | bytes 589828
  35.7 27.4 %copy-start.11 = (f32[48,8,128]{2,1,0:T(8,128)}, f32[48,8,128]{2,1,0:T(8,128)S(1)}, u32[]{:S(2)}) copy-start(f32[48,8,128]{2,1,0:T(8,128)S(1)} %collective-permute-done.7.below) | copy-start | bytes 589828

commit v4 on v3

--- a/solution.py
+++ b/solution.py
@@ -193,13 +193,6 @@
     lax.fori_loop(0, planes, body, 0, unroll=2)
 
 
-def copies(pairs, sems):
-    started = [pltpu.make_async_copy(s, d, sems.at[k]) for k, (s, d) in enumerate(pairs)]
-    for copy in started:
-        copy.start()
-    return started
-
-
 def weigh(stress, materials):
     weight = jnp.where(materials == 0, 1.0, jnp.where(materials == 1, 0.6, 0.0))
     return weight.astype(jnp.float32) * stress
@@ -234,32 +227,22 @@
 
 
 def velocity(
-    source, before, after, below_any, above_any, order, speed_hbm, own_speed, peaks,
-    src, one, two, speed, below, above, sems,
+    source, before, after, below, above, order, speed, own_speed, peaks, src, one, two
 ):
     nx, ny, _ = source.shape
     wide = nx + 2 * SRC
     top = OWN + ny
     rest = wide * 8
-    arrivals = copies(
-        [
-            (below_any, below),
-            (above_any, above),
-            (source, src.at[pl.ds(SRC, nx), pl.ds(OWN, ny)]),
-            (before, src.at[pl.ds(0, SRC), pl.ds(OWN, ny)]),
-            (after, src.at[pl.ds(SRC + nx, SRC), pl.ds(OWN, ny)]),
-        ],
-        sems,
-    )
-    for arrival in arrivals[:2]:
-        arrival.wait()
+    for k in range(nx):
+        src[SRC + k, OWN:top] = source[k]
+    for k in range(SRC):
+        src[k, OWN:top] = before[k]
+        src[SRC + nx + k, OWN:top] = after[k]
     for k in range(wide):
         src[k, OWN - 8 : OWN] = below[k * 8 : k * 8 + 8]
         src[k, top : top + 8] = above[k * 8 : k * 8 + 8]
         src[k, OWN - 9 : OWN - 8] = below[rest + k : rest + k + 1]
         src[k, top + 8 : top + 9] = above[rest + k : rest + k + 1]
-    for arrival in arrivals[2:]:
-        arrival.wait()
     coefficients = velocity_polynomial()
     step = (ny + 2 * (SRC - 1)) // 8
     start = OWN - (SRC - 1)
@@ -290,8 +273,6 @@
     sweep(one, two, 0, 2, wide - 2, None, coefficients[2])
     sweep(two, one, 0, 3, wide - 3, None, coefficients[1])
     sweep(one, speed, SRC - SPD, 4, wide - 4, None, coefficients[0])
-    out = pltpu.make_async_copy(speed, speed_hbm, sems.at[0])
-    out.start()
 
     def largest(x, carry):
         mine = speed[SPD + x, OWN : OWN + ny]
@@ -300,29 +281,23 @@
 
     top = lax.fori_loop(0, nx, largest, jnp.zeros((ny, 128), jnp.float32))
     peaks[...] = jnp.broadcast_to(jnp.max(top), peaks.shape)
-    out.wait()
 
 
 def evolve(
-    own_level, before, after, below, above, speed_hbm, peaks, new_level,
-    level, speed, rate, stage, advected, swept, acc, sems,
+    own_level, before, after, below, above, speed, peaks, new_level,
+    level, rate, stage, advected, swept, acc,
 ):
     nx, ny, _ = new_level.shape
     tall = nx + 2 * LEV
-    rows = pl.ds(OWN, ny)
-    arrivals = copies(
-        [
-            (own_level, level.at[pl.ds(LEV, nx), rows]),
-            (before, level.at[pl.ds(0, LEV), rows]),
-            (after, level.at[pl.ds(LEV + nx, LEV), rows]),
-            (below, level.at[pl.ds(0, tall), pl.ds(OWN - 8, 8)]),
-            (above, level.at[pl.ds(0, tall), pl.ds(OWN + ny, 8)]),
-            (speed_hbm, speed),
-        ],
-        sems,
-    )
-    for arrival in arrivals:
-        arrival.wait()
+    top = OWN + ny
+    for k in range(nx):
+        level[LEV + k, OWN:top] = own_level[k]
+    for k in range(LEV):
+        level[k, OWN:top] = before[k]
+        level[LEV + nx + k, OWN:top] = after[k]
+    for k in range(tall):
+        level[k, OWN - 8 : OWN] = below[k]
+        level[k, top : top + 8] = above[k]
 
     def emit_rate(x, t, value):
         rate[x, pl.ds(OWN - SPD + t, 8, stride=10), :] = value
@@ -361,25 +336,19 @@
     reinit_sweep(swept, 1, advected, 2, nx, OWN, ny // 8, emit_two)
 
 
-BIG = 56
+BIG = 32
 VM = pl.BlockSpec(memory_space=pltpu.VMEM)
-HBM = pl.BlockSpec(memory_space=pltpu.HBM)
 ANY = pl.BlockSpec(memory_space=pl.ANY)
 
 
-def call(kernel, outs, scratch, args, megabytes, copied=0):
+def call(kernel, outs, scratch, args, megabytes):
     ins = [a if isinstance(a, tuple) else (a, VM) for a in args]
-    outs = [o if isinstance(o[0], tuple) else (o, VM) for o in outs]
-    scratch = [s if isinstance(s[0], tuple) else (s, jnp.float32) for s in scratch]
-    scratch_shapes = [pltpu.VMEM(shape, dtype) for shape, dtype in scratch]
-    if copied:
-        scratch_shapes.append(pltpu.SemaphoreType.DMA((copied,)))
     return pl.pallas_call(
         kernel,
-        out_shape=[jax.ShapeDtypeStruct(shape, jnp.float32) for shape, _ in outs],
+        out_shape=[jax.ShapeDtypeStruct(shape, jnp.float32) for shape in outs],
         in_specs=[place for _, place in ins],
-        out_specs=[place for _, place in outs],
-        scratch_shapes=scratch_shapes,
+        out_specs=[VM] * len(outs),
+        scratch_shapes=[pltpu.VMEM(shape, jnp.float32) for shape in scratch],
         compiler_params=pltpu.CompilerParams(vmem_limit_bytes=megabytes * 1024 * 1024),
     )(*[array for array, _ in ins])
 
@@ -404,7 +373,7 @@
     )
     level_after = shift(level_low, "gx", size_x, -1)
     level_before = shift(level_high, "gx", size_x, 1)
-    message = rows_message = (wide * 8 + (wide + 7) // 8 * 8, nz)
+    message = (wide * 8 + (wide + 7) // 8 * 8, nz)
     low, high = call(
         pack_source, [message, message], [], (source, source_before, source_after), 8
     )
@@ -422,11 +391,10 @@
     level_below = shift(high, "gy", size_y, 1)
     speed, normal_speed, peaks = call(
         velocity,
-        [((mid, ROWS, nz), HBM), tile, (devices, nz)],
-        [(wide, ROWS, nz)] * 3 + [(mid, ROWS, nz), rows_message, rows_message],
-        [(a, ANY) for a in (source, source_before, source_after, source_below, source_above, low)],
+        [(mid, ROWS, nz), tile, (devices, nz)],
+        [(wide, ROWS, nz)] * 3,
+        (source, source_before, source_after, source_below, source_above, (low, ANY)),
         BIG,
-        copied=5,
     )
     peaks, level_above, level_below = lax.optimization_barrier((peaks, level_above, level_below))
     peaks = lax.all_to_all(peaks.reshape(devices, 1, nz), ("gx", "gy"), 0, 0)
@@ -437,18 +405,20 @@
             (tall, ROWS, nz),
             (mid, ROWS, nz),
             (mid, ROWS, nz),
-            (mid, ROWS, nz),
             (nx + 4, ROWS, nz),
             (nx + 2, ROWS, nz),
             (mid, 10, 8, nz),
         ],
-        [
-            (a, ANY)
-            for a in (level_set, level_before, level_after, level_below, level_above, speed)
-        ]
-        + [peaks.reshape(devices, nz)],
+        (
+            level_set,
+            level_before,
+            level_after,
+            level_below,
+            level_above,
+            speed,
+            peaks.reshape(devices, nz),
+        ),
         BIG,
-        copied=6,
     )
     return (new_level, normal_speed)
 

time: 95.2 us -> 87.9 us (0.923)
  Pallas kernels: 43.1 us -> 37.5 us
  local copies, waits for them, and re-layouts: 1.4 us -> 0.04 us
    pallas_call x4, Pallas kernels: 43.1 us -> 37.5 us  [call(): pl.pallas_call(kernel, out_shape=[jax.ShapeDtypeStruct(shape, jnp.float32...]
    unnamed x24 -> x4, local copies, waits for them, and re-layouts: 1.37 us -> 0.01 us
  transfers between devices with their start and end apart: 8 -> 8, of which waited for: 1 -> 1; matrix products, arithmetic and copies ran while one was open for 2% -> 2% of each run, Pallas kernels for 12% -> 10%
where the time goes in v4:
time: 87.9 us; the launch traced here: 87.8 us
  Pallas kernels  37.5 us (43%)
  blocking collectives  27.2 us (31%)
  starting transfers between devices  18.7 us (21%)
  other arithmetic  2.95 us (3%)
    pallas_call x4, Pallas kernels, call(): pl.pallas_call(kernel, out_shape=[jax.ShapeDtypeStruct(shape, jnp.float32...  37.5 us
    all_to_all x1, blocking collectives, local(): peaks = lax.all_to_all(peaks.reshape(devices, 1, nz), ('gx', 'gy'), 0, 0)  27.2 us
    ppermute x8, starting transfers between devices, shift(): lax.ppermute(value, axis, [(i, (i + by) % size) for i in range(size)])  18.7 us
    mul x2, other arithmetic, weigh(): return weight.astype(jnp.float32) * stress  2.95 us
  transfers between devices with their start and end apart: 8, of which 1 were waited for; matrix products, arithmetic and copies ran while one was open for 2% of the time, Pallas kernels for 10%

profile of v4, /device:TPU:1, one launch (start us, length us, event | category | flops | bytes accessed | tf_op | source)
XLA Modules:
  0.0 87.8 jit_solution(6684859840836965721)
XLA Ops:
  0.6 0.0 copy-start
  0.6 0.0 copy-start.1
  0.6 1.5 %slice_multiply_fusion = (f32[9,64,128]{2,1,0:T(8,128)S(1)}, f32[9,64,128]{2,1,0:T(8,128)S(1)}) fusion(f32[32,64,128]{2,1,0:T(8,128)} %param.4, s32[32,64,128]{2,1,0:T(8,128)} %param.5), kind=kLoop, calls=%fused_computation.1 | loop fusion | flops 737280 | bytes 1769472 | tf_op jit(solution)/shard_map/mul | solution.py:198
  2.2 2.2 %collective-permute-start.2 = (f32[9,64,128]{2,1,0:T(8,128)S(1)}, f32[9,64,128]{2,1,0:T(8,128)S(1)}, u32[]{:S(2)}, u32[]{:S(2)}) collective-permute-start(f32[9,64,128]{2,1,0:T(8,128)S(1)} %get-tuple-element.26), channel_id=1, source_target_pairs={{0,16},{16,32},{32,48},{48,64},{64,80},{80,96},{96,112},{112,128},... | collective-permute-start | bytes 884744 | tf_op jit(solution)/shard_map/ppermute | solution.py:364
  4.4 3.7 %collective-permute-start.3 = (f32[9,64,128]{2,1,0:T(8,128)S(1)}, f32[9,64,128]{2,1,0:T(8,128)S(1)}, u32[]{:S(2)}, u32[]{:S(2)}) collective-permute-start(f32[9,64,128]{2,1,0:T(8,128)S(1)} %get-tuple-element.27), channel_id=1, source_target_pairs={{0,240},{16,0},{32,16},{48,32},{64,48},{80,64},{96,80},{112,96},{1... | collective-permute-start | bytes 884744 | tf_op jit(solution)/shard_map/ppermute | solution.py:364
  8.1 0.1 collective-permute-start
  8.2 4.8 %collective-permute-start.1 = (f32[8,64,128]{2,1,0:T(8,128)S(1)}, f32[8,64,128]{2,1,0:T(8,128)S(1)}, u32[]{:S(2)}, u32[]{:S(2)}) collective-permute-start(f32[8,64,128]{2,1,0:T(8,128)S(1)} %get-tuple-element.15), channel_id=1, source_target_pairs={{0,240},{16,0},{32,16},{48,32},{64,48},{80,64},{96,80},{112,96},{1... | collective-permute-start | bytes 786440 | tf_op jit(solution)/shard_map/ppermute | solution.py:364
  13.0 1.4 %select_multiply_fusion.source = f32[32,64,128]{2,1,0:T(8,128)S(1)} fusion(f32[32,64,128]{2,1,0:T(8,128)S(1)} %copy-done.1, s32[32,64,128]{2,1,0:T(8,128)} %param.5), kind=kLoop, calls=%fused_computation | loop fusion | flops 1310720 | bytes 3145728 | tf_op jit(solution)/shard_map/mul | solution.py:198
  14.4 0.0 collective-permute-done.2.before
  14.5 0.0 collective-permute-done.3.after
  14.5 0.1 shard_map.50
  14.5 3.3 %collective-permute-start.5 = (f32[456,128]{1,0:T(8,128)S(1)}, f32[456,128]{1,0:T(8,128)S(1)}, u32[]{:S(2)}, u32[]{:S(2)}) collective-permute-start(f32[456,128]{1,0:T(8,128)S(1)} %get-tuple-element.17.order), channel_id=1, source_target_pairs={{0,15},{1,0},{2,1},{3,2},{4,3},{5,4},{6,5},{7,6},{8,7},{9,8},{10,9... | collective-permute-start | bytes 700424 | tf_op jit(solution)/shard_map/ppermute | solution.py:364
  17.8 0.7 collective-permute-start.4
  18.6 0.7 collective-permute-done.before
  19.2 0.0 collective-permute-done.1.after
  19.3 2.3 %collective-permute-start.6 = (f32[48,8,128]{2,1,0:T(8,128)S(1)}, f32[48,8,128]{2,1,0:T(8,128)S(1)}, u32[]{:S(2)}, u32[]{:S(2)}) collective-permute-start(f32[48,8,128]{2,1,0:T(8,128)S(1)} %get-tuple-element.18.order), channel_id=1, source_target_pairs={{0,15},{1,0},{2,1},{3,2},{4,3},{5,4},{6,5},{7,6},{8,7},{9,8},{10,9... | collective-permute-start | bytes 589832 | tf_op jit(solution)/shard_map/ppermute | solution.py:364
  21.6 1.5 %collective-permute-start.7 = (f32[48,8,128]{2,1,0:T(8,128)S(1)}, f32[48,8,128]{2,1,0:T(8,128)S(1)}, u32[]{:S(2)}, u32[]{:S(2)}) collective-permute-start(f32[48,8,128]{2,1,0:T(8,128)S(1)} %get-tuple-element.20), channel_id=1, source_target_pairs={{0,1},{1,2},{2,3},{3,4},{4,5},{5,6},{6,7},{7,8},{8,9},{9,10},{10,1... | collective-permute-start | bytes 589832 | tf_op jit(solution)/shard_map/ppermute | solution.py:364
  23.2 0.0 collective-permute-done.5.above
  23.2 0.0 collective-permute-done.4.below
  23.2 8.6 %shard_map.52 = (f32[42,96,128]{2,1,0:T(8,128)S(1)}, f32[32,64,128]{2,1,0:T(8,128)}, f32[256,128]{1,0:T(8,128)S(1)}) custom-call(f32[32,64,128]{2,1,0:T(8,128)S(1)} %select_multiply_fusion.source, f32[9,64,128]{2,1,0:T(8,128)S(1)} %collective-permute-done.2.before, f32[9,64,128]{2,1,0:T(8,128)S(1)} %collective-permute-done.3.after, ...), custom_call_target="tpu_custom_call" | custom-call | tf_op jit(solution)/shard_map/pallas_call | solution.py:346
  31.7 0.0 collective-permute-done.6.above
  31.8 0.0 collective-permute-done.7.below
  31.8 27.2 %all_to_all.5 = f32[256,1,128]{2,1,0:T(1,128)S(1)} all-to-all(f32[256,1,128]{2,1,0:T(1,128)S(1)} %bitcast.5), channel_id=1, replica_groups=mesh['gx'=16,'gy'=16] {'gx','gy'}, dimensions={0} | all-to-all | bytes 262144 | tf_op jit(solution)/shard_map/all_to_all | solution.py:400
  58.9 28.9 %shard_map.53 = f32[32,64,128]{2,1,0:T(8,128)} custom-call(f32[32,64,128]{2,1,0:T(8,128)S(1)} %copy-done, f32[8,64,128]{2,1,0:T(8,128)S(1)} %collective-permute-done.before, f32[8,64,128]{2,1,0:T(8,128)S(1)} %collective-permute-done.1.after, f32[48,8,128]{2,1,0:T(8,128)S(1)} %collective-permute-done.7.below, f32[48,8,128]{2,1,0:T(8,128)S(1)} %collective-permute-done.6.above, ...), custom_call_target="tpu_custom_call" | custom-call | tf_op jit(solution)/shard_map/pallas_call | solution.py:346
  (4 shorter events, 0.1 us)
Async XLA Ops:
  0.6 7.5 %copy-start = (f32[32,64,128]{2,1,0:T(8,128)S(1)}, f32[32,64,128]{2,1,0:T(8,128)}, u32[]{:S(2)}) copy-start(f32[32,64,128]{2,1,0:T(8,128)} %own_level.1) | copy-start | bytes 3145732
  0.6 12.4 %copy-start.1 = (f32[32,64,128]{2,1,0:T(8,128)S(1)}, f32[32,64,128]{2,1,0:T(8,128)}, u32[]{:S(2)}) copy-start(f32[32,64,128]{2,1,0:T(8,128)} %param.4) | copy-start | bytes 3145732
  2.2 12.3 %collective-permute-start.2 = (f32[9,64,128]{2,1,0:T(8,128)S(1)}, f32[9,64,128]{2,1,0:T(8,128)S(1)}, u32[]{:S(2)}, u32[]{:S(2)}) collective-permute-start(f32[9,64,128]{2,1,0:T(8,128)S(1)} %get-tuple-element.26), channel_id=1, source_target_pairs={{0,16},{16,32},{32,48},{48,64},{64,80},{80,96},{96,112},{112,128},... | collective-permute-start | bytes 884744 | tf_op jit(solution)/shard_map/ppermute | solution.py:364
  4.4 10.1 %collective-permute-start.3 = (f32[9,64,128]{2,1,0:T(8,128)S(1)}, f32[9,64,128]{2,1,0:T(8,128)S(1)}, u32[]{:S(2)}, u32[]{:S(2)}) collective-permute-start(f32[9,64,128]{2,1,0:T(8,128)S(1)} %get-tuple-element.27), channel_id=1, source_target_pairs={{0,240},{16,0},{32,16},{48,32},{64,48},{80,64},{96,80},{112,96},{1... | collective-permute-start | bytes 884744 | tf_op jit(solution)/shard_map/ppermute | solution.py:364
  8.1 11.1 %collective-permute-start = (f32[8,64,128]{2,1,0:T(8,128)S(1)}, f32[8,64,128]{2,1,0:T(8,128)S(1)}, u32[]{:S(2)}, u32[]{:S(2)}) collective-permute-start(f32[8,64,128]{2,1,0:T(8,128)S(1)} %get-tuple-element.14), channel_id=1, source_target_pairs={{0,16},{16,32},{32,48},{48,64},{64,80},{80,96},{96,112},{112,128},... | collective-permute-start | bytes 786440 | tf_op jit(solution)/shard_map/ppermute | solution.py:364
  8.2 11.0 %collective-permute-start.1 = (f32[8,64,128]{2,1,0:T(8,128)S(1)}, f32[8,64,128]{2,1,0:T(8,128)S(1)}, u32[]{:S(2)}, u32[]{:S(2)}) collective-permute-start(f32[8,64,128]{2,1,0:T(8,128)S(1)} %get-tuple-element.15), channel_id=1, source_target_pairs={{0,240},{16,0},{32,16},{48,32},{64,48},{80,64},{96,80},{112,96},{1... | collective-permute-start | bytes 786440 | tf_op jit(solution)/shard_map/ppermute | solution.py:364
  14.5 8.6 %collective-permute-start.5 = (f32[456,128]{1,0:T(8,128)S(1)}, f32[456,128]{1,0:T(8,128)S(1)}, u32[]{:S(2)}, u32[]{:S(2)}) collective-permute-start(f32[456,128]{1,0:T(8,128)S(1)} %get-tuple-element.17.order), channel_id=1, source_target_pairs={{0,15},{1,0},{2,1},{3,2},{4,3},{5,4},{6,5},{7,6},{8,7},{9,8},{10,9... | collective-permute-start | bytes 700424 | tf_op jit(solution)/shard_map/ppermute | solution.py:364
  17.8 5.3 %collective-permute-start.4 = (f32[456,128]{1,0:T(8,128)S(1)}, f32[456,128]{1,0:T(8,128)S(1)}, u32[]{:S(2)}, u32[]{:S(2)}) collective-permute-start(f32[456,128]{1,0:T(8,128)S(1)} %get-tuple-element.16), channel_id=1, source_target_pairs={{0,1},{1,2},{2,3},{3,4},{4,5},{5,6},{6,7},{7,8},{8,9},{9,10},{10,1... | collective-permute-start | bytes 700424 | tf_op jit(solution)/shard_map/ppermute | solution.py:364
  19.3 12.5 %collective-permute-start.6 = (f32[48,8,128]{2,1,0:T(8,128)S(1)}, f32[48,8,128]{2,1,0:T(8,128)S(1)}, u32[]{:S(2)}, u32[]{:S(2)}) collective-permute-start(f32[48,8,128]{2,1,0:T(8,128)S(1)} %get-tuple-element.18.order), channel_id=1, source_target_pairs={{0,15},{1,0},{2,1},{3,2},{4,3},{5,4},{6,5},{7,6},{8,7},{9,8},{10,9... | collective-permute-start | bytes 589832 | tf_op jit(solution)/shard_map/ppermute | solution.py:364
  21.6 10.1 %collective-permute-start.7 = (f32[48,8,128]{2,1,0:T(8,128)S(1)}, f32[48,8,128]{2,1,0:T(8,128)S(1)}, u32[]{:S(2)}, u32[]{:S(2)}) collective-permute-start(f32[48,8,128]{2,1,0:T(8,128)S(1)} %get-tuple-element.20), channel_id=1, source_target_pairs={{0,1},{1,2},{2,3},{3,4},{4,5},{5,6},{6,7},{7,8},{8,9},{9,10},{10,1... | collective-permute-start | bytes 589832 | tf_op jit(solution)/shard_map/ppermute | solution.py:364

commit v5 on v4

--- a/solution.py
+++ b/solution.py
@@ -4,7 +4,7 @@
 from jax import lax
 from jax.experimental import pallas as pl
 from jax.experimental.pallas import tpu as pltpu
-from jax.sharding import PartitionSpec as P
+from jax.sharding import Mesh, PartitionSpec as P
 
 SWEEPS = 4
 REINIT = 2
@@ -283,11 +283,12 @@
     peaks[...] = jnp.broadcast_to(jnp.max(top), peaks.shape)
 
 
-def evolve(
-    own_level, before, after, below, above, speed, peaks, new_level,
-    level, rate, stage, advected, swept, acc,
-):
-    nx, ny, _ = new_level.shape
+def gather_peaks(mine, other, peaks):
+    peaks[...] = jnp.broadcast_to(jnp.maximum(mine[0:1], other[0:1]), peaks.shape)
+
+
+def first_stage(own_level, before, after, below, above, speed, level, rate, acc):
+    nx, ny, _ = own_level.shape
     tall = nx + 2 * LEV
     top = OWN + ny
     for k in range(nx):
@@ -299,11 +300,14 @@
         level[k, OWN - 8 : OWN] = below[k]
         level[k, top : top + 8] = above[k]
 
-    def emit_rate(x, t, value):
+    def emit(x, t, value):
         rate[x, pl.ds(OWN - SPD + t, 8, stride=10), :] = value
 
-    weno_rates(level, LEV - SPD, speed, 0, acc, nx + 2 * SPD, OWN - SPD, 10, emit_rate)
-
+    weno_rates(level, LEV - SPD, speed, 0, acc, nx + 2 * SPD, OWN - SPD, 10, emit)
+
+
+def second_stage(level, speed, rate, peaks, new_level, stage, advected, swept, acc):
+    nx, ny, _ = new_level.shape
     peak = jnp.max(peaks[...], axis=0, keepdims=True)
     time_step = courant / (peak + 1e-06)
     step_row = jnp.broadcast_to(time_step, (8, 128))
@@ -357,7 +361,7 @@
     tile = level_set.shape
     nx, ny, nz = tile
     wide, tall, mid = nx + 2 * SRC, nx + 2 * LEV, nx + 2 * SPD
-    size_x, size_y = lax.axis_size("gx"), lax.axis_size("gy")
+    size_x, size_y = lax.axis_size("gx"), 2 * lax.axis_size("gz")
     devices = size_x * size_y
 
     def shift(value, axis, size, by):
@@ -377,8 +381,8 @@
     low, high = call(
         pack_source, [message, message], [], (source, source_before, source_after), 8
     )
-    source_above = shift(low, "gy", size_y, -1)
-    source_below = shift(high, "gy", size_y, 1)
+    source_above = shift(low, ("gz", "core"), size_y, -1)
+    source_below = shift(high, ("gz", "core"), size_y, 1)
     message = (tall, 8, nz)
     low, high = call(
         pack_level,
@@ -387,43 +391,41 @@
         (level_set, level_before, level_after, (low, ANY)),
         8,
     )
-    level_above = shift(low, "gy", size_y, -1)
-    level_below = shift(high, "gy", size_y, 1)
-    speed, normal_speed, peaks = call(
+    level_above = shift(low, ("gz", "core"), size_y, -1)
+    level_below = shift(high, ("gz", "core"), size_y, 1)
+    speed, normal_speed, peak = call(
         velocity,
-        [(mid, ROWS, nz), tile, (devices, nz)],
+        [(mid, ROWS, nz), tile, (8, nz)],
         [(wide, ROWS, nz)] * 3,
         (source, source_before, source_after, source_below, source_above, (low, ANY)),
         BIG,
     )
-    peaks, level_above, level_below = lax.optimization_barrier((peaks, level_above, level_below))
-    peaks = lax.all_to_all(peaks.reshape(devices, 1, nz), ("gx", "gy"), 0, 0)
+    peak, level_above, level_below = lax.optimization_barrier((peak, level_above, level_below))
+    other = lax.ppermute(peak, "core", [(0, 1), (1, 0)])
+    chips = devices // 2
+    (peaks,) = call(gather_peaks, [(chips, nz)], [], (peak, other), 4)
+    peaks = lax.all_to_all(peaks.reshape(chips, 1, nz), ("gx", "gz"), 0, 0)
+    level, rate = call(
+        first_stage,
+        [(tall, ROWS, nz), (mid, ROWS, nz)],
+        [(mid, 10, 8, nz)],
+        (level_set, level_before, level_after, level_below, level_above, speed),
+        BIG,
+    )
     (new_level,) = call(
-        evolve,
+        second_stage,
         [tile],
-        [
-            (tall, ROWS, nz),
-            (mid, ROWS, nz),
-            (mid, ROWS, nz),
-            (nx + 4, ROWS, nz),
-            (nx + 2, ROWS, nz),
-            (mid, 10, 8, nz),
-        ],
-        (
-            level_set,
-            level_before,
-            level_after,
-            level_below,
-            level_above,
-            speed,
-            peaks.reshape(devices, nz),
-        ),
+        [(mid, ROWS, nz), (nx + 4, ROWS, nz), (nx + 2, ROWS, nz), (nx + 4, 9, 8, nz)],
+        (level, speed, rate, peaks.reshape(chips, nz)),
         BIG,
     )
     return (new_level, normal_speed)
 
 
 def solution(mesh):
-    in_specs = (P("gx", "gy", None), P("gx", "gy", None), P("gx", "gy", None))
-    out_specs = (P("gx", "gy", None), P("gx", "gy", None))
-    return jax.shard_map(local, mesh=mesh, in_specs=in_specs, out_specs=out_specs, check_vma=False)
+    size_x, size_y = mesh.devices.shape
+    chips = Mesh(mesh.devices.reshape(size_x, size_y // 2, 2), ("gx", "gz", "core"))
+    spec = P("gx", ("gz", "core"), None)
+    return jax.shard_map(
+        local, mesh=chips, in_specs=(spec,) * 3, out_specs=(spec,) * 2, check_vma=False
+    )

time: 87.9 us -> 89 us (1.013)
  blocking collectives: 27.2 us -> 0 us
  starting transfers between devices: 18.7 us -> 34.1 us
  local copies, waits for them, and re-layouts: 0.04 us -> 10.2 us
  waiting for transfers between devices: 0.7 us -> 2.54 us
    all_to_all x1 -> x0, blocking collectives: 27.2 us -> none  [local(): peaks = lax.all_to_all(peaks.reshape(devices, 1, nz), ('gx', 'gy'), 0, 0)]
    all_to_all x0 -> x1, starting transfers between devices: none -> 13.3 us  [local(): peaks = lax.all_to_all(peaks.reshape(chips, 1, nz), ('gx', 'gz'), 0, 0)]
    unnamed x4 -> x24, local copies, waits for them, and re-layouts: 0.01 us -> 10.2 us
    ppermute x0 -> x1, starting transfers between devices: none -> 2.11 us  [local(): other = lax.ppermute(peak, 'core', [(0, 1), (1, 0)])]
    ppermute x8, waiting for transfers between devices: 0.7 us -> 1.71 us  [shift(): lax.ppermute(value, axis, [(i, (i + by) % size) for i in range(size)])]
    pallas_call x4 -> x6, Pallas kernels: 37.5 us -> 38.1 us  [call(): pl.pallas_call(kernel, out_shape=[jax.ShapeDtypeStruct(shape, jnp.float32...]
  transfers between devices with their start and end apart: 8 -> 10, of which waited for: 1 -> 3; matrix products, arithmetic and copies ran while one was open for 2% -> 2% of each run, Pallas kernels for 10% -> 24%
where the time goes in v5:
time: 89 us; the launch traced here: 88.7 us
  Pallas kernels  38.1 us (43%)
  starting transfers between devices  34.1 us (38%)
  local copies, waits for them, and re-layouts  10.2 us (11%)
  other arithmetic  2.95 us (3%)
  waiting for transfers between devices  2.54 us (3%)
    pallas_call x6, Pallas kernels, call(): pl.pallas_call(kernel, out_shape=[jax.ShapeDtypeStruct(shape, jnp.float32...  38.1 us
    ppermute x8, starting transfers between devices, shift(): lax.ppermute(value, axis, [(i, (i + by) % size) for i in range(size)])  18.7 us
    all_to_all x1, starting transfers between devices, local(): peaks = lax.all_to_all(peaks.reshape(chips, 1, nz), ('gx', 'gz'), 0, 0)  13.3 us
    unnamed x24, local copies, waits for them, and re-layouts  10.2 us
    mul x2, other arithmetic, weigh(): return weight.astype(jnp.float32) * stress  2.95 us
    ppermute x1, starting transfers between devices, local(): other = lax.ppermute(peak, 'core', [(0, 1), (1, 0)])  2.11 us
  transfers between devices with their start and end apart: 10, of which 3 were waited for; matrix products, arithmetic and copies ran while one was open for 2% of the time, Pallas kernels for 24%

profile of v5, /device:TPU:1, one launch (start us, length us, event | category | flops | bytes accessed | tf_op | source)
XLA Modules:
  0.0 88.7 jit_solution(6398606768727944578)
XLA Ops:
  0.6 1.5 %slice_multiply_fusion = (f32[9,64,128]{2,1,0:T(8,128)S(1)}, f32[9,64,128]{2,1,0:T(8,128)S(1)}) fusion(f32[32,64,128]{2,1,0:T(8,128)} %param.4, s32[32,64,128]{2,1,0:T(8,128)} %param.5), kind=kLoop, calls=%fused_computation.1 | loop fusion | flops 737280 | bytes 1769472 | tf_op jit(solution)/shard_map/mul | solution.py:198
  2.2 2.2 %collective-permute-start.2 = (f32[9,64,128]{2,1,0:T(8,128)S(1)}, f32[9,64,128]{2,1,0:T(8,128)S(1)}, u32[]{:S(2)}, u32[]{:S(2)}) collective-permute-start(f32[9,64,128]{2,1,0:T(8,128)S(1)} %get-tuple-element.30), channel_id=1, source_target_pairs={{0,16},{16,32},{32,48},{48,64},{64,80},{80,96},{96,112},{112,128},... | collective-permute-start | bytes 884744 | tf_op jit(solution)/shard_map/ppermute | solution.py:368
  4.4 3.7 %collective-permute-start.3 = (f32[9,64,128]{2,1,0:T(8,128)S(1)}, f32[9,64,128]{2,1,0:T(8,128)S(1)}, u32[]{:S(2)}, u32[]{:S(2)}) collective-permute-start(f32[9,64,128]{2,1,0:T(8,128)S(1)} %get-tuple-element.31), channel_id=1, source_target_pairs={{0,240},{16,0},{32,16},{48,32},{64,48},{80,64},{96,80},{112,96},{1... | collective-permute-start | bytes 884744 | tf_op jit(solution)/shard_map/ppermute | solution.py:368
  8.2 4.8 %collective-permute-start.1 = (f32[8,64,128]{2,1,0:T(8,128)S(1)}, f32[8,64,128]{2,1,0:T(8,128)S(1)}, u32[]{:S(2)}, u32[]{:S(2)}) collective-permute-start(f32[8,64,128]{2,1,0:T(8,128)S(1)} %get-tuple-element.17), channel_id=1, source_target_pairs={{0,240},{16,0},{32,16},{48,32},{64,48},{80,64},{96,80},{112,96},{1... | collective-permute-start | bytes 786440 | tf_op jit(solution)/shard_map/ppermute | solution.py:368
  13.0 1.4 %select_multiply_fusion.source = f32[32,64,128]{2,1,0:T(8,128)S(1)} fusion(f32[32,64,128]{2,1,0:T(8,128)S(1)} %copy-done.11, s32[32,64,128]{2,1,0:T(8,128)} %param.5), kind=kLoop, calls=%fused_computation | loop fusion | flops 1310720 | bytes 3145728 | tf_op jit(solution)/shard_map/mul | solution.py:198
  14.5 4.0 %collective-permute-start.4 = (f32[456,128]{1,0:T(8,128)S(1)}, f32[456,128]{1,0:T(8,128)S(1)}, u32[]{:S(2)}, u32[]{:S(2)}) collective-permute-start(f32[456,128]{1,0:T(8,128)S(1)} %get-tuple-element.18), channel_id=1, source_target_pairs={{0,1},{1,2},{2,3},{3,4},{4,5},{5,6},{6,7},{7,8},{8,9},{9,10},{10,1... | collective-permute-start | bytes 700424 | tf_op jit(solution)/shard_map/ppermute | solution.py:368
  18.5 0.7 collective-permute-done.before
  19.3 3.9 %collective-permute-start.7 = (f32[48,8,128]{2,1,0:T(8,128)S(1)}, f32[48,8,128]{2,1,0:T(8,128)S(1)}, u32[]{:S(2)}, u32[]{:S(2)}) collective-permute-start(f32[48,8,128]{2,1,0:T(8,128)S(1)} %get-tuple-element.22), channel_id=1, source_target_pairs={{0,1},{1,2},{2,3},{3,4},{4,5},{5,6},{6,7},{7,8},{8,9},{9,10},{10,1... | collective-permute-start | bytes 589832 | tf_op jit(solution)/shard_map/ppermute | solution.py:368
  23.2 1.0 %collective-permute-done.5.above = f32[456,128]{1,0:T(8,128)S(1)} collective-permute-done((f32[456,128]{1,0:T(8,128)S(1)}, f32[456,128]{1,0:T(8,128)S(1)}, u32[]{:S(2)}, u32[]{:S(2)}) %collective-permute-start.5) | collective-permute-done | bytes 233504 | tf_op jit(solution)/shard_map/ppermute | solution.py:368
  24.1 8.6 %shard_map.52 = (f32[42,96,128]{2,1,0:T(8,128)S(1)}, f32[32,64,128]{2,1,0:T(8,128)}, f32[8,128]{1,0:T(8,128)S(1)}) custom-call(f32[32,64,128]{2,1,0:T(8,128)S(1)} %select_multiply_fusion.source, f32[9,64,128]{2,1,0:T(8,128)S(1)} %collective-permute-done.2.before, f32[9,64,128]{2,1,0:T(8,128)S(1)} %collective-permute-done.3.after, ...), custom_call_target="tpu_custom_call" | custom-call | tf_op jit(solution)/shard_map/pallas_call | solution.py:350
  32.7 0.7 copy-done.7
  33.4 0.7 copy-done.9
  34.1 2.1 %collective-permute-start.8 = (f32[8,128]{1,0:T(8,128)S(1)}, f32[8,128]{1,0:T(8,128)S(1)}, u32[]{:S(2)}, u32[]{:S(2)}) collective-permute-start(f32[8,128]{1,0:T(8,128)S(1)} %get-tuple-element.28.mine), channel_id=1, source_target_pairs={{0,1},{1,0},{2,3},{3,2},{4,5},{5,4},{6,7},{7,6},{8,9},{9,8},{10,11... | collective-permute-start | bytes 12296 | tf_op jit(solution)/shard_map/ppermute | solution.py:404
  36.2 0.8 collective-permute-done.8.other
  37.7 13.3 %all-to-all-start = ((f32[128,1,128]{2,1,0:T(1,128)}), f32[128,1,128]{2,1,0:T(1,128)S(1)}, u32[]{:S(2)}, u32[]{:S(2)}) async-start(f32[128,1,128]{2,1,0:T(1,128)} %bitcast.1), calls=%async_computation | async-start | bytes 131072 | tf_op jit(solution)/shard_map/all_to_all | solution.py:407
  51.0 0.9 %copy-done.6 = f32[8,64,128]{2,1,0:T(8,128)S(1)} copy-done((f32[8,64,128]{2,1,0:T(8,128)S(1)}, f32[8,64,128]{2,1,0:T(8,128)}, u32[]{:S(2)}) %copy-start.6) | copy-done | bytes 262168
  52.0 0.9 %copy-done.8 = f32[48,8,128]{2,1,0:T(8,128)S(1)} copy-done((f32[48,8,128]{2,1,0:T(8,128)S(1)}, f32[48,8,128]{2,1,0:T(8,128)}, u32[]{:S(2)}) %copy-start.8) | copy-done | bytes 196632
  52.9 0.9 %copy-done.10 = f32[48,8,128]{2,1,0:T(8,128)S(1)} copy-done((f32[48,8,128]{2,1,0:T(8,128)S(1)}, f32[48,8,128]{2,1,0:T(8,128)}, u32[]{:S(2)}) %copy-start.10) | copy-done | bytes 196632
  53.8 13.0 %shard_map.53 = (f32[48,96,128]{2,1,0:T(8,128)S(1)}, f32[42,96,128]{2,1,0:T(8,128)S(1)}) custom-call(f32[32,64,128]{2,1,0:T(8,128)S(1)} %copy-done, f32[8,64,128]{2,1,0:T(8,128)S(1)} %collective-permute-done.before, f32[8,64,128]{2,1,0:T(8,128)S(1)} %copy-done.6, f32[48,8,128]{2,1,0:T(8,128)S(1)} %copy-done.8, f32[48,8,128]{2,1,0:T(8,128)S(1)} %copy-done.10, ...), custom_call_target="tpu_custom_call" | custom-call | tf_op jit(solution)/shard_map/pallas_call | solution.py:350
  66.8 1.4 %copy-done.1 = f32[48,96,128]{2,1,0:T(8,128)} copy-done((f32[48,96,128]{2,1,0:T(8,128)}, f32[48,96,128]{2,1,0:T(8,128)S(1)}, u32[]{:S(2)}) %copy-start.1) | copy-done | bytes 2359320
  68.3 1.3 %copy-done.3 = f32[42,96,128]{2,1,0:T(8,128)} copy-done((f32[42,96,128]{2,1,0:T(8,128)}, f32[42,96,128]{2,1,0:T(8,128)S(1)}, u32[]{:S(2)}) %copy-start.3) | copy-done | bytes 2064408
  69.6 1.7 %copy-done.2 = f32[48,96,128]{2,1,0:T(8,128)S(1)} copy-done((f32[48,96,128]{2,1,0:T(8,128)S(1)}, f32[48,96,128]{2,1,0:T(8,128)}, u32[]{:S(2)}) %copy-start.2) | copy-done | bytes 2359320
  71.3 1.6 %copy-done.4 = f32[42,96,128]{2,1,0:T(8,128)S(1)} copy-done((f32[42,96,128]{2,1,0:T(8,128)S(1)}, f32[42,96,128]{2,1,0:T(8,128)}, u32[]{:S(2)}) %copy-start.4) | copy-done | bytes 2064408
  72.8 15.8 %shard_map.55 = f32[32,64,128]{2,1,0:T(8,128)} custom-call(f32[48,96,128]{2,1,0:T(8,128)S(1)} %copy-done.2, f32[42,96,128]{2,1,0:T(8,128)S(1)} %get-tuple-element.25.speed, f32[42,96,128]{2,1,0:T(8,128)S(1)} %copy-done.4, f32[128,128]{1,0:T(8,128)S(1)} %bitcast.4), custom_call_target="tpu_custom_call" | custom-call | tf_op jit(solution)/shard_map/pallas_call | solution.py:350
  (29 shorter events, 0.9 us)
Async XLA Ops:
  0.6 7.5 %copy-start = (f32[32,64,128]{2,1,0:T(8,128)S(1)}, f32[32,64,128]{2,1,0:T(8,128)}, u32[]{:S(2)}) copy-start(f32[32,64,128]{2,1,0:T(8,128)} %own_level.1) | copy-start | bytes 3145732
  0.6 12.4 %copy-start.11 = (f32[32,64,128]{2,1,0:T(8,128)S(1)}, f32[32,64,128]{2,1,0:T(8,128)}, u32[]{:S(2)}) copy-start(f32[32,64,128]{2,1,0:T(8,128)} %param.4) | copy-start | bytes 3145732
  2.2 12.3 %collective-permute-start.2 = (f32[9,64,128]{2,1,0:T(8,128)S(1)}, f32[9,64,128]{2,1,0:T(8,128)S(1)}, u32[]{:S(2)}, u32[]{:S(2)}) collective-permute-start(f32[9,64,128]{2,1,0:T(8,128)S(1)} %get-tuple-element.30), channel_id=1, source_target_pairs={{0,16},{16,32},{32,48},{48,64},{64,80},{80,96},{96,112},{112,128},... | collective-permute-start | bytes 884744 | tf_op jit(solution)/shard_map/ppermute | solution.py:368
  4.4 10.1 %collective-permute-start.3 = (f32[9,64,128]{2,1,0:T(8,128)S(1)}, f32[9,64,128]{2,1,0:T(8,128)S(1)}, u32[]{:S(2)}, u32[]{:S(2)}) collective-permute-start(f32[9,64,128]{2,1,0:T(8,128)S(1)} %get-tuple-element.31), channel_id=1, source_target_pairs={{0,240},{16,0},{32,16},{48,32},{64,48},{80,64},{96,80},{112,96},{1... | collective-permute-start | bytes 884744 | tf_op jit(solution)/shard_map/ppermute | solution.py:368
  8.1 11.1 %collective-permute-start = (f32[8,64,128]{2,1,0:T(8,128)S(1)}, f32[8,64,128]{2,1,0:T(8,128)S(1)}, u32[]{:S(2)}, u32[]{:S(2)}) collective-permute-start(f32[8,64,128]{2,1,0:T(8,128)S(1)} %get-tuple-element.16), channel_id=1, source_target_pairs={{0,16},{16,32},{32,48},{48,64},{64,80},{80,96},{96,112},{112,128},... | collective-permute-start | bytes 786440 | tf_op jit(solution)/shard_map/ppermute | solution.py:368
  8.2 11.0 %collective-permute-start.1 = (f32[8,64,128]{2,1,0:T(8,128)S(1)}, f32[8,64,128]{2,1,0:T(8,128)S(1)}, u32[]{:S(2)}, u32[]{:S(2)}) collective-permute-start(f32[8,64,128]{2,1,0:T(8,128)S(1)} %get-tuple-element.17), channel_id=1, source_target_pairs={{0,240},{16,0},{32,16},{48,32},{64,48},{80,64},{96,80},{112,96},{1... | collective-permute-start | bytes 786440 | tf_op jit(solution)/shard_map/ppermute | solution.py:368
  14.5 8.6 %collective-permute-start.4 = (f32[456,128]{1,0:T(8,128)S(1)}, f32[456,128]{1,0:T(8,128)S(1)}, u32[]{:S(2)}, u32[]{:S(2)}) collective-permute-start(f32[456,128]{1,0:T(8,128)S(1)} %get-tuple-element.18), channel_id=1, source_target_pairs={{0,1},{1,2},{2,3},{3,4},{4,5},{5,6},{6,7},{7,8},{8,9},{9,10},{10,1... | collective-permute-start | bytes 700424 | tf_op jit(solution)/shard_map/ppermute | solution.py:368
  18.5 5.6 %collective-permute-start.5 = (f32[456,128]{1,0:T(8,128)S(1)}, f32[456,128]{1,0:T(8,128)S(1)}, u32[]{:S(2)}, u32[]{:S(2)}) collective-permute-start(f32[456,128]{1,0:T(8,128)S(1)} %get-tuple-element.19.order), channel_id=1, source_target_pairs={{0,15},{1,0},{2,1},{3,2},{4,3},{5,4},{6,5},{7,6},{8,7},{9,8},{10,9... | collective-permute-start | bytes 700424 | tf_op jit(solution)/shard_map/ppermute | solution.py:368
  19.2 18.4 %copy-start.5 = (f32[8,64,128]{2,1,0:T(8,128)}, f32[8,64,128]{2,1,0:T(8,128)S(1)}, u32[]{:S(2)}) copy-start(f32[8,64,128]{2,1,0:T(8,128)S(1)} %collective-permute-done.1.after) | copy-start | bytes 786436
  19.3 13.4 %collective-permute-start.7 = (f32[48,8,128]{2,1,0:T(8,128)S(1)}, f32[48,8,128]{2,1,0:T(8,128)S(1)}, u32[]{:S(2)}, u32[]{:S(2)}) collective-permute-start(f32[48,8,128]{2,1,0:T(8,128)S(1)} %get-tuple-element.22), channel_id=1, source_target_pairs={{0,1},{1,2},{2,3},{3,4},{4,5},{5,6},{6,7},{7,8},{8,9},{9,10},{10,1... | collective-permute-start | bytes 589832 | tf_op jit(solution)/shard_map/ppermute | solution.py:368
  23.1 10.3 %collective-permute-start.6 = (f32[48,8,128]{2,1,0:T(8,128)S(1)}, f32[48,8,128]{2,1,0:T(8,128)S(1)}, u32[]{:S(2)}, u32[]{:S(2)}) collective-permute-start(f32[48,8,128]{2,1,0:T(8,128)S(1)} %get-tuple-element.20.order), channel_id=1, source_target_pairs={{0,15},{1,0},{2,1},{3,2},{4,3},{5,4},{6,5},{7,6},{8,7},{9,8},{10,9... | collective-permute-start | bytes 589832 | tf_op jit(solution)/shard_map/ppermute | solution.py:368
  32.7 0.7 copy-start.7
  33.4 0.7 copy-start.9
  34.1 2.9 %collective-permute-start.8 = (f32[8,128]{1,0:T(8,128)S(1)}, f32[8,128]{1,0:T(8,128)S(1)}, u32[]{:S(2)}, u32[]{:S(2)}) collective-permute-start(f32[8,128]{1,0:T(8,128)S(1)} %get-tuple-element.28.mine), channel_id=1, source_target_pairs={{0,1},{1,0},{2,3},{3,2},{4,5},{5,4},{6,7},{7,6},{8,9},{9,8},{10,11... | collective-permute-start | bytes 12296 | tf_op jit(solution)/shard_map/ppermute | solution.py:404
  37.7 31.9 %all-to-all-start = ((f32[128,1,128]{2,1,0:T(1,128)}), f32[128,1,128]{2,1,0:T(1,128)S(1)}, u32[]{:S(2)}, u32[]{:S(2)}) async-start(f32[128,1,128]{2,1,0:T(1,128)} %bitcast.1), calls=%async_computation | async-start | bytes 131072 | tf_op jit(solution)/shard_map/all_to_all | solution.py:407
  51.0 1.0 %copy-start.6 = (f32[8,64,128]{2,1,0:T(8,128)S(1)}, f32[8,64,128]{2,1,0:T(8,128)}, u32[]{:S(2)}) copy-start(f32[8,64,128]{2,1,0:T(8,128)} %copy-done.5) | copy-start | bytes 786436
  51.9 0.9 %copy-start.8 = (f32[48,8,128]{2,1,0:T(8,128)S(1)}, f32[48,8,128]{2,1,0:T(8,128)}, u32[]{:S(2)}) copy-start(f32[48,8,128]{2,1,0:T(8,128)} %copy-done.7) | copy-start | bytes 589828
  52.9 0.9 %copy-start.10 = (f32[48,8,128]{2,1,0:T(8,128)S(1)}, f32[48,8,128]{2,1,0:T(8,128)}, u32[]{:S(2)}) copy-start(f32[48,8,128]{2,1,0:T(8,128)} %copy-done.9) | copy-start | bytes 589828
  66.8 1.4 %copy-start.1 = (f32[48,96,128]{2,1,0:T(8,128)}, f32[48,96,128]{2,1,0:T(8,128)S(1)}, u32[]{:S(2)}) copy-start(f32[48,96,128]{2,1,0:T(8,128)S(1)} %get-tuple-element.26.level) | copy-start | bytes 7077892
  68.3 1.3 %copy-start.3 = (f32[42,96,128]{2,1,0:T(8,128)}, f32[42,96,128]{2,1,0:T(8,128)S(1)}, u32[]{:S(2)}) copy-start(f32[42,96,128]{2,1,0:T(8,128)S(1)} %get-tuple-element.27.rate) | copy-start | bytes 6193156
  69.6 1.7 %copy-start.2 = (f32[48,96,128]{2,1,0:T(8,128)S(1)}, f32[48,96,128]{2,1,0:T(8,128)}, u32[]{:S(2)}) copy-start(f32[48,96,128]{2,1,0:T(8,128)} %copy-done.1) | copy-start | bytes 7077892
  71.3 1.6 %copy-start.4 = (f32[42,96,128]{2,1,0:T(8,128)S(1)}, f32[42,96,128]{2,1,0:T(8,128)}, u32[]{:S(2)}) copy-start(f32[42,96,128]{2,1,0:T(8,128)} %copy-done.3) | copy-start | bytes 6193156

commit v6 on v4

--- a/solution.py
+++ b/solution.py
@@ -112,8 +112,22 @@
 
 
 def weno_lanes(f):
-    shifted = {k: along_lanes(f, k) if k else f for k in range(-3, 4)}
-    ((_, left, right),) = weno_line(lambda j: shifted[j], 1)
+    cells = {k: along_lanes(f, k) if k else f for k in range(-3, 3)}
+    first = {k: cells[k + 1] - cells[k] for k in range(-3, 2)}
+    second = {k: first[k] - first[k - 1] for k in range(-2, 2)}
+    third = {k: second[k + 1] - second[k] for k in range(-2, 1)}
+
+    def terms(k):
+        return smooth_terms(
+            second[k], second[k + 1], third[k], 1.5 * second[k], 1.5 * second[k + 1]
+        )
+
+    ratio_left, ratio_right = side_ratios(
+        terms(-2)[0], terms(-1)[1], terms(0)[2], third[0] - third[-1], third[-1] - third[-2]
+    )
+    wide = 6.0 * (first[0] + first[-1])
+    left = (wide - (third[-1] + third[-1])) - ratio_left
+    right = ((third[0] + third[0]) - wide) - along_lanes(ratio_right, 1)
     return left, right
 
 
@@ -160,7 +174,7 @@
             emit(x, t, velocity * (root(total) * (-1.0 / 12.0)))
         return _
 
-    lax.fori_loop(0, planes, along_yz, 0, unroll=2)
+    lax.fori_loop(0, planes, along_yz, 0, unroll=3)
 
 
 def reinit_sweep(field, fx, origin, ox, planes, start, step, emit):
@@ -190,7 +204,7 @@
             emit(x, t, centre - pseudo_step * sign_field * (root(total) - 1.0))
         return _
 
-    lax.fori_loop(0, planes, body, 0, unroll=2)
+    lax.fori_loop(0, planes, body, 0, unroll=4)
 
 
 def weigh(stress, materials):
@@ -267,7 +281,7 @@
                 new[x - shift, pl.ds(start + t, 8, stride=step), :] = beside + constant * own
             return _
 
-        lax.fori_loop(lo, hi, body, 0, unroll=4)
+        lax.fori_loop(lo, hi, body, 0, unroll=11)
 
     sweep(src, one, 0, 1, wide - 1, coefficients[4], coefficients[3])
     sweep(one, two, 0, 2, wide - 2, None, coefficients[2])

time: 87.9 us -> 83.6 us (0.951)
  Pallas kernels: 37.5 us -> 33.1 us
    pallas_call x4, Pallas kernels: 37.5 us -> 33.1 us  [call(): pl.pallas_call(kernel, out_shape=[jax.ShapeDtypeStruct(shape, jnp.float32...]
  transfers between devices with their start and end apart: 8 -> 8, of which waited for: 1 -> 1; matrix products, arithmetic and copies ran while one was open for 2% -> 2% of each run, Pallas kernels for 10% -> 9%
where the time goes in v6:
time: 83.6 us; the launch traced here: 83.4 us
  Pallas kernels  33.1 us (40%)
  blocking collectives  27.2 us (33%)
  starting transfers between devices  18.7 us (22%)
  other arithmetic  2.95 us (4%)
    pallas_call x4, Pallas kernels, call(): pl.pallas_call(kernel, out_shape=[jax.ShapeDtypeStruct(shape, jnp.float32...  33.1 us
    all_to_all x1, blocking collectives, local(): peaks = lax.all_to_all(peaks.reshape(devices, 1, nz), ('gx', 'gy'), 0, 0)  27.2 us
    ppermute x8, starting transfers between devices, shift(): lax.ppermute(value, axis, [(i, (i + by) % size) for i in range(size)])  18.7 us
    mul x2, other arithmetic, weigh(): return weight.astype(jnp.float32) * stress  2.95 us
  transfers between devices with their start and end apart: 8, of which 1 were waited for; matrix products, arithmetic and copies ran while one was open for 2% of the time, Pallas kernels for 9%

profile of v6, /device:TPU:1, one launch (start us, length us, event | category | flops | bytes accessed | tf_op | source)
XLA Modules:
  0.0 83.4 jit_solution(8647343936959965524)
XLA Ops:
  0.6 0.0 copy-start
  0.6 0.0 copy-start.1
  0.6 1.5 %slice_multiply_fusion = (f32[9,64,128]{2,1,0:T(8,128)S(1)}, f32[9,64,128]{2,1,0:T(8,128)S(1)}) fusion(f32[32,64,128]{2,1,0:T(8,128)} %param.4, s32[32,64,128]{2,1,0:T(8,128)} %param.5), kind=kLoop, calls=%fused_computation.1 | loop fusion | flops 737280 | bytes 1769472 | tf_op jit(solution)/shard_map/mul | solution.py:212
  2.2 2.2 %collective-permute-start.2 = (f32[9,64,128]{2,1,0:T(8,128)S(1)}, f32[9,64,128]{2,1,0:T(8,128)S(1)}, u32[]{:S(2)}, u32[]{:S(2)}) collective-permute-start(f32[9,64,128]{2,1,0:T(8,128)S(1)} %get-tuple-element.26), channel_id=1, source_target_pairs={{0,16},{16,32},{32,48},{48,64},{64,80},{80,96},{96,112},{112,128},... | collective-permute-start | bytes 884744 | tf_op jit(solution)/shard_map/ppermute | solution.py:378
  4.4 3.7 %collective-permute-start.3 = (f32[9,64,128]{2,1,0:T(8,128)S(1)}, f32[9,64,128]{2,1,0:T(8,128)S(1)}, u32[]{:S(2)}, u32[]{:S(2)}) collective-permute-start(f32[9,64,128]{2,1,0:T(8,128)S(1)} %get-tuple-element.27), channel_id=1, source_target_pairs={{0,240},{16,0},{32,16},{48,32},{64,48},{80,64},{96,80},{112,96},{1... | collective-permute-start | bytes 884744 | tf_op jit(solution)/shard_map/ppermute | solution.py:378
  8.1 0.1 collective-permute-start
  8.2 4.8 %collective-permute-start.1 = (f32[8,64,128]{2,1,0:T(8,128)S(1)}, f32[8,64,128]{2,1,0:T(8,128)S(1)}, u32[]{:S(2)}, u32[]{:S(2)}) collective-permute-start(f32[8,64,128]{2,1,0:T(8,128)S(1)} %get-tuple-element.15), channel_id=1, source_target_pairs={{0,240},{16,0},{32,16},{48,32},{64,48},{80,64},{96,80},{112,96},{1... | collective-permute-start | bytes 786440 | tf_op jit(solution)/shard_map/ppermute | solution.py:378
  13.0 1.4 %select_multiply_fusion.source = f32[32,64,128]{2,1,0:T(8,128)S(1)} fusion(f32[32,64,128]{2,1,0:T(8,128)S(1)} %copy-done.1, s32[32,64,128]{2,1,0:T(8,128)} %param.5), kind=kLoop, calls=%fused_computation | loop fusion | flops 1310720 | bytes 3145728 | tf_op jit(solution)/shard_map/mul | solution.py:212
  14.4 0.0 collective-permute-done.2.before
  14.5 0.0 collective-permute-done.3.after
  14.5 0.1 shard_map.50
  14.5 3.3 %collective-permute-start.5 = (f32[456,128]{1,0:T(8,128)S(1)}, f32[456,128]{1,0:T(8,128)S(1)}, u32[]{:S(2)}, u32[]{:S(2)}) collective-permute-start(f32[456,128]{1,0:T(8,128)S(1)} %get-tuple-element.17.order), channel_id=1, source_target_pairs={{0,15},{1,0},{2,1},{3,2},{4,3},{5,4},{6,5},{7,6},{8,7},{9,8},{10,9... | collective-permute-start | bytes 700424 | tf_op jit(solution)/shard_map/ppermute | solution.py:378
  17.8 0.7 collective-permute-start.4
  18.6 0.7 collective-permute-done.before
  19.2 0.0 collective-permute-done.1.after
  19.3 2.3 %collective-permute-start.6 = (f32[48,8,128]{2,1,0:T(8,128)S(1)}, f32[48,8,128]{2,1,0:T(8,128)S(1)}, u32[]{:S(2)}, u32[]{:S(2)}) collective-permute-start(f32[48,8,128]{2,1,0:T(8,128)S(1)} %get-tuple-element.18.order), channel_id=1, source_target_pairs={{0,15},{1,0},{2,1},{3,2},{4,3},{5,4},{6,5},{7,6},{8,7},{9,8},{10,9... | collective-permute-start | bytes 589832 | tf_op jit(solution)/shard_map/ppermute | solution.py:378
  21.6 1.5 %collective-permute-start.7 = (f32[48,8,128]{2,1,0:T(8,128)S(1)}, f32[48,8,128]{2,1,0:T(8,128)S(1)}, u32[]{:S(2)}, u32[]{:S(2)}) collective-permute-start(f32[48,8,128]{2,1,0:T(8,128)S(1)} %get-tuple-element.20), channel_id=1, source_target_pairs={{0,1},{1,2},{2,3},{3,4},{4,5},{5,6},{6,7},{7,8},{8,9},{9,10},{10,1... | collective-permute-start | bytes 589832 | tf_op jit(solution)/shard_map/ppermute | solution.py:378
  23.2 0.0 collective-permute-done.5.above
  23.2 0.0 collective-permute-done.4.below
  23.2 7.3 %shard_map.52 = (f32[42,96,128]{2,1,0:T(8,128)S(1)}, f32[32,64,128]{2,1,0:T(8,128)}, f32[256,128]{1,0:T(8,128)S(1)}) custom-call(f32[32,64,128]{2,1,0:T(8,128)S(1)} %select_multiply_fusion.source, f32[9,64,128]{2,1,0:T(8,128)S(1)} %collective-permute-done.2.before, f32[9,64,128]{2,1,0:T(8,128)S(1)} %collective-permute-done.3.after, ...), custom_call_target="tpu_custom_call" | custom-call | tf_op jit(solution)/shard_map/pallas_call | solution.py:360
  30.5 0.0 collective-permute-done.6.above
  30.5 0.0 collective-permute-done.7.below
  30.5 27.2 %all_to_all.5 = f32[256,1,128]{2,1,0:T(1,128)S(1)} all-to-all(f32[256,1,128]{2,1,0:T(1,128)S(1)} %bitcast.5), channel_id=1, replica_groups=mesh['gx'=16,'gy'=16] {'gx','gy'}, dimensions={0} | all-to-all | bytes 262144 | tf_op jit(solution)/shard_map/all_to_all | solution.py:414
  57.7 25.7 %shard_map.53 = f32[32,64,128]{2,1,0:T(8,128)} custom-call(f32[32,64,128]{2,1,0:T(8,128)S(1)} %copy-done, f32[8,64,128]{2,1,0:T(8,128)S(1)} %collective-permute-done.before, f32[8,64,128]{2,1,0:T(8,128)S(1)} %collective-permute-done.1.after, f32[48,8,128]{2,1,0:T(8,128)S(1)} %collective-permute-done.7.below, f32[48,8,128]{2,1,0:T(8,128)S(1)} %collective-permute-done.6.above, ...), custom_call_target="tpu_custom_call" | custom-call | tf_op jit(solution)/shard_map/pallas_call | solution.py:360
  (4 shorter events, 0.1 us)
Async XLA Ops:
  0.6 7.5 %copy-start = (f32[32,64,128]{2,1,0:T(8,128)S(1)}, f32[32,64,128]{2,1,0:T(8,128)}, u32[]{:S(2)}) copy-start(f32[32,64,128]{2,1,0:T(8,128)} %own_level.1) | copy-start | bytes 3145732
  0.6 12.4 %copy-start.1 = (f32[32,64,128]{2,1,0:T(8,128)S(1)}, f32[32,64,128]{2,1,0:T(8,128)}, u32[]{:S(2)}) copy-start(f32[32,64,128]{2,1,0:T(8,128)} %param.4) | copy-start | bytes 3145732
  2.2 12.3 %collective-permute-start.2 = (f32[9,64,128]{2,1,0:T(8,128)S(1)}, f32[9,64,128]{2,1,0:T(8,128)S(1)}, u32[]{:S(2)}, u32[]{:S(2)}) collective-permute-start(f32[9,64,128]{2,1,0:T(8,128)S(1)} %get-tuple-element.26), channel_id=1, source_target_pairs={{0,16},{16,32},{32,48},{48,64},{64,80},{80,96},{96,112},{112,128},... | collective-permute-start | bytes 884744 | tf_op jit(solution)/shard_map/ppermute | solution.py:378
  4.4 10.1 %collective-permute-start.3 = (f32[9,64,128]{2,1,0:T(8,128)S(1)}, f32[9,64,128]{2,1,0:T(8,128)S(1)}, u32[]{:S(2)}, u32[]{:S(2)}) collective-permute-start(f32[9,64,128]{2,1,0:T(8,128)S(1)} %get-tuple-element.27), channel_id=1, source_target_pairs={{0,240},{16,0},{32,16},{48,32},{64,48},{80,64},{96,80},{112,96},{1... | collective-permute-start | bytes 884744 | tf_op jit(solution)/shard_map/ppermute | solution.py:378
  8.1 11.1 %collective-permute-start = (f32[8,64,128]{2,1,0:T(8,128)S(1)}, f32[8,64,128]{2,1,0:T(8,128)S(1)}, u32[]{:S(2)}, u32[]{:S(2)}) collective-permute-start(f32[8,64,128]{2,1,0:T(8,128)S(1)} %get-tuple-element.14), channel_id=1, source_target_pairs={{0,16},{16,32},{32,48},{48,64},{64,80},{80,96},{96,112},{112,128},... | collective-permute-start | bytes 786440 | tf_op jit(solution)/shard_map/ppermute | solution.py:378
  8.2 11.0 %collective-permute-start.1 = (f32[8,64,128]{2,1,0:T(8,128)S(1)}, f32[8,64,128]{2,1,0:T(8,128)S(1)}, u32[]{:S(2)}, u32[]{:S(2)}) collective-permute-start(f32[8,64,128]{2,1,0:T(8,128)S(1)} %get-tuple-element.15), channel_id=1, source_target_pairs={{0,240},{16,0},{32,16},{48,32},{64,48},{80,64},{96,80},{112,96},{1... | collective-permute-start | bytes 786440 | tf_op jit(solution)/shard_map/ppermute | solution.py:378
  14.5 8.6 %collective-permute-start.5 = (f32[456,128]{1,0:T(8,128)S(1)}, f32[456,128]{1,0:T(8,128)S(1)}, u32[]{:S(2)}, u32[]{:S(2)}) collective-permute-start(f32[456,128]{1,0:T(8,128)S(1)} %get-tuple-element.17.order), channel_id=1, source_target_pairs={{0,15},{1,0},{2,1},{3,2},{4,3},{5,4},{6,5},{7,6},{8,7},{9,8},{10,9... | collective-permute-start | bytes 700424 | tf_op jit(solution)/shard_map/ppermute | solution.py:378
  17.8 5.3 %collective-permute-start.4 = (f32[456,128]{1,0:T(8,128)S(1)}, f32[456,128]{1,0:T(8,128)S(1)}, u32[]{:S(2)}, u32[]{:S(2)}) collective-permute-start(f32[456,128]{1,0:T(8,128)S(1)} %get-tuple-element.16), channel_id=1, source_target_pairs={{0,1},{1,2},{2,3},{3,4},{4,5},{5,6},{6,7},{7,8},{8,9},{9,10},{10,1... | collective-permute-start | bytes 700424 | tf_op jit(solution)/shard_map/ppermute | solution.py:378
  19.3 11.2 %collective-permute-start.6 = (f32[48,8,128]{2,1,0:T(8,128)S(1)}, f32[48,8,128]{2,1,0:T(8,128)S(1)}, u32[]{:S(2)}, u32[]{:S(2)}) collective-permute-start(f32[48,8,128]{2,1,0:T(8,128)S(1)} %get-tuple-element.18.order), channel_id=1, source_target_pairs={{0,15},{1,0},{2,1},{3,2},{4,3},{5,4},{6,5},{7,6},{8,7},{9,8},{10,9... | collective-permute-start | bytes 589832 | tf_op jit(solution)/shard_map/ppermute | solution.py:378
  21.6 8.9 %collective-permute-start.7 = (f32[48,8,128]{2,1,0:T(8,128)S(1)}, f32[48,8,128]{2,1,0:T(8,128)S(1)}, u32[]{:S(2)}, u32[]{:S(2)}) collective-permute-start(f32[48,8,128]{2,1,0:T(8,128)S(1)} %get-tuple-element.20), channel_id=1, source_target_pairs={{0,1},{1,2},{2,3},{3,4},{4,5},{5,6},{6,7},{7,8},{8,9},{9,10},{10,1... | collective-permute-start | bytes 589832 | tf_op jit(solution)/shard_map/ppermute | solution.py:378

commit v7 on v6

--- a/solution.py
+++ b/solution.py
@@ -143,7 +143,7 @@
     return ref[x, pl.ds(start, 8, stride=step), :]
 
 
-def weno_rates(field, fx, speed, sx, acc, planes, start, step, emit):
+def weno_rates(field, fx, speed, sx, acc, planes, start, step, emit, lanes=None):
     def along_x(t, _):
         row = start + t
 
@@ -169,8 +169,11 @@
             velocity = strided(speed, sx + x, start + t, step)
             sign = sign_of(velocity)
             total = acc[x, t] + upwind_square(left, right, sign)
-            left, right = weno_lanes(f(t))
-            total = total + upwind_square(left, right, sign)
+            if lanes is None:
+                left, right = weno_lanes(f(t))
+                total = total + upwind_square(left, right, sign)
+            else:
+                total = total + strided(lanes, x, start + t, step)
             emit(x, t, velocity * (root(total) * (-1.0 / 12.0)))
         return _
 
@@ -238,6 +241,48 @@
             ref, j = (after, k - LEV - nx)
         low[k] = ref[j, 0:8]
         high[k] = ref[j, ny - 8 : ny]
+
+
+def own_lanes(level, low, high, upper, lower):
+    nx, ny, _ = level.shape
+
+    def body(x, _):
+        for t in range(0, ny, 8):
+            left, right = weno_lanes(level[x, t : t + 8])
+            upper[x, t : t + 8] = jnp.square(jnp.maximum(jnp.maximum(left, right), 0.0))
+            lower[x, t : t + 8] = jnp.square(jnp.minimum(jnp.minimum(left, right), 0.0))
+        return _
+
+    lax.fori_loop(0, nx, body, 0, unroll=2)
+
+
+def other_lanes(level, speed, upper, lower, lanes):
+    nx, ny, _ = upper.shape
+    top = OWN + ny
+
+    def outside(x, row):
+        left, right = weno_lanes(level[x + LEV - SPD, row : row + 8])
+        lanes[x, row : row + 8] = upwind_square(left, right, sign_of(speed[x, row : row + 8]))
+
+    def rows(x, _):
+        outside(x, OWN - 8)
+        outside(x, top)
+        return _
+
+    def ends(x, _):
+        for row in range(OWN, top, 8):
+            outside(x, row)
+            outside(x + SPD + nx, row)
+        return _
+
+    def own(x, _):
+        positive = speed[SPD + x, OWN:top] > 0
+        lanes[SPD + x, OWN:top] = jnp.where(positive, upper[x], lower[x])
+        return _
+
+    lax.fori_loop(0, nx + 2 * SPD, rows, 0, unroll=14)
+    lax.fori_loop(0, SPD, ends, 0)
+    lax.fori_loop(0, nx, own, 0, unroll=2)
 
 
 def velocity(
@@ -298,8 +343,8 @@
 
 
 def evolve(
-    own_level, before, after, below, above, speed, peaks, new_level,
-    level, rate, stage, advected, swept, acc,
+    own_level, before, after, below, above, speed, upper, lower, peaks, new_level,
+    level, rate, lanes, stage, advected, swept, acc,
 ):
     nx, ny, _ = new_level.shape
     tall = nx + 2 * LEV
@@ -316,7 +361,8 @@
     def emit_rate(x, t, value):
         rate[x, pl.ds(OWN - SPD + t, 8, stride=10), :] = value
 
-    weno_rates(level, LEV - SPD, speed, 0, acc, nx + 2 * SPD, OWN - SPD, 10, emit_rate)
+    other_lanes(level, speed, upper, lower, lanes)
+    weno_rates(level, LEV - SPD, speed, 0, acc, nx + 2 * SPD, OWN - SPD, 10, emit_rate, lanes)
 
     peak = jnp.max(peaks[...], axis=0, keepdims=True)
     time_step = courant / (peak + 1e-06)
@@ -382,8 +428,9 @@
     source_after = shift(low, "gx", size_x, -1)
     source_before = shift(high, "gx", size_x, 1)
     source = weigh(stress_jump, materials)
-    level_low, level_high, _, _ = lax.optimization_barrier(
-        (level_set[:LEV], level_set[nx - LEV :], low, high)
+    upper, lower = call(own_lanes, [tile, tile], [], (level_set, (low, ANY), (high, ANY)), 8)
+    level_low, level_high, upper, lower, source = lax.optimization_barrier(
+        (level_set[:LEV], level_set[nx - LEV :], upper, lower, source)
     )
     level_after = shift(level_low, "gx", size_x, -1)
     level_before = shift(level_high, "gx", size_x, 1)
@@ -417,6 +464,7 @@
         [tile],
         [
             (tall, ROWS, nz),
+            (mid, ROWS, nz),
             (mid, ROWS, nz),
             (mid, ROWS, nz),
             (nx + 4, ROWS, nz),
@@ -430,6 +478,8 @@
             level_below,
             level_above,
             speed,
+            upper,
+            lower,
             peaks.reshape(devices, nz),
         ),
         BIG,

time: 83.6 us -> 84.4 us (level)
  Pallas kernels: 33.1 us -> 35.5 us
  blocking collectives: 27.2 us -> 25.5 us
    pallas_call x4 -> x5, Pallas kernels: 33.1 us -> 35.5 us  [call(): pl.pallas_call(kernel, out_shape=[jax.ShapeDtypeStruct(shape, jnp.float32...]
    all_to_all x1, blocking collectives: 27.2 us -> 25.5 us  [local(): peaks = lax.all_to_all(peaks.reshape(devices, 1, nz), ('gx', 'gy'), 0, 0)]
  transfers between devices with their start and end apart: 8 -> 8, of which waited for: 1 -> 1; matrix products, arithmetic and copies ran while one was open for 2% -> 2% of each run, Pallas kernels for 9% -> 14%
where the time goes in v7:
time: 84.4 us; the launch traced here: 84.2 us
  Pallas kernels  35.5 us (42%)
  blocking collectives  25.5 us (30%)
  starting transfers between devices  19.2 us (23%)
  other arithmetic  2.93 us (3%)
    pallas_call x5, Pallas kernels, call(): pl.pallas_call(kernel, out_shape=[jax.ShapeDtypeStruct(shape, jnp.float32...  35.5 us
    all_to_all x1, blocking collectives, local(): peaks = lax.all_to_all(peaks.reshape(devices, 1, nz), ('gx', 'gy'), 0, 0)  25.5 us
    ppermute x8, starting transfers between devices, shift(): lax.ppermute(value, axis, [(i, (i + by) % size) for i in range(size)])  19.2 us
    mul x2, other arithmetic, weigh(): return weight.astype(jnp.float32) * stress  2.93 us
  transfers between devices with their start and end apart: 8, of which 1 were waited for; matrix products, arithmetic and copies ran while one was open for 2% of the time, Pallas kernels for 14%

profile of v7, /device:TPU:1, one launch (start us, length us, event | category | flops | bytes accessed | tf_op | source)
XLA Modules:
  0.0 84.2 jit_solution(15558786103443497999)
XLA Ops:
  0.6 1.5 %slice_multiply_fusion = (f32[9,64,128]{2,1,0:T(8,128)S(1)}, f32[9,64,128]{2,1,0:T(8,128)S(1)}) fusion(f32[32,64,128]{2,1,0:T(8,128)} %param.4, s32[32,64,128]{2,1,0:T(8,128)} %param.5), kind=kLoop, calls=%fused_computation.1 | loop fusion | flops 737280 | bytes 1769472 | tf_op jit(solution)/shard_map/mul | solution.py:215
  2.1 2.2 %collective-permute-start.2 = (f32[9,64,128]{2,1,0:T(8,128)S(1)}, f32[9,64,128]{2,1,0:T(8,128)S(1)}, u32[]{:S(2)}, u32[]{:S(2)}) collective-permute-start(f32[9,64,128]{2,1,0:T(8,128)S(1)} %get-tuple-element.36.high), channel_id=1, source_target_pairs={{0,16},{16,32},{32,48},{48,64},{64,80},{80,96},{96,112},{112,128},... | collective-permute-start | bytes 884744 | tf_op jit(solution)/shard_map/ppermute | solution.py:424
  4.3 3.7 %collective-permute-start.3 = (f32[9,64,128]{2,1,0:T(8,128)S(1)}, f32[9,64,128]{2,1,0:T(8,128)S(1)}, u32[]{:S(2)}, u32[]{:S(2)}) collective-permute-start(f32[9,64,128]{2,1,0:T(8,128)S(1)} %get-tuple-element.37.low), channel_id=1, source_target_pairs={{0,240},{16,0},{32,16},{48,32},{64,48},{80,64},{96,80},{112,96},{1... | collective-permute-start | bytes 884744 | tf_op jit(solution)/shard_map/ppermute | solution.py:424
  8.1 1.4 %select_multiply_fusion.source = f32[32,64,128]{2,1,0:T(8,128)S(1)} fusion(f32[32,64,128]{2,1,0:T(8,128)S(1)} %copy-done.1, s32[32,64,128]{2,1,0:T(8,128)} %param.5), kind=kLoop, calls=%fused_computation | loop fusion | flops 1310720 | bytes 3145728 | tf_op jit(solution)/shard_map/mul | solution.py:215
  9.5 0.0 copy-done
  9.6 4.4 %shard_map.50 = (f32[32,64,128]{2,1,0:T(8,128)S(1)}, f32[32,64,128]{2,1,0:T(8,128)S(1)}) custom-call(f32[32,64,128]{2,1,0:T(8,128)S(1)} %copy-done, f32[9,64,128]{2,1,0:T(8,128)S(1)} %get-tuple-element.37.low, f32[9,64,128]{2,1,0:T(8,128)S(1)} %get-tuple-element.36.high), custom_call_target="tpu_custom_call" | custom-call | tf_op jit(solution)/shard_map/pallas_call | solution.py:406
  14.0 0.1 collective-permute-start
  14.1 4.8 %collective-permute-start.1 = (f32[8,64,128]{2,1,0:T(8,128)S(1)}, f32[8,64,128]{2,1,0:T(8,128)S(1)}, u32[]{:S(2)}, u32[]{:S(2)}) collective-permute-start(f32[8,64,128]{2,1,0:T(8,128)S(1)} %get-tuple-element.22), channel_id=1, source_target_pairs={{0,240},{16,0},{32,16},{48,32},{64,48},{80,64},{96,80},{112,96},{1... | collective-permute-start | bytes 786440 | tf_op jit(solution)/shard_map/ppermute | solution.py:424
  18.8 0.0 collective-permute-done.2.before
  18.8 0.0 collective-permute-done.3.after
  18.8 0.1 shard_map.51
  18.9 3.3 %collective-permute-start.5 = (f32[456,128]{1,0:T(8,128)S(1)}, f32[456,128]{1,0:T(8,128)S(1)}, u32[]{:S(2)}, u32[]{:S(2)}) collective-permute-start(f32[456,128]{1,0:T(8,128)S(1)} %get-tuple-element.25.order), channel_id=1, source_target_pairs={{0,15},{1,0},{2,1},{3,2},{4,3},{5,4},{6,5},{7,6},{8,7},{9,8},{10,9... | collective-permute-start | bytes 700424 | tf_op jit(solution)/shard_map/ppermute | solution.py:424
  22.2 0.0 collective-permute-start.4
  22.2 0.4 collective-permute-done.before
  22.6 0.0 collective-permute-done.1.after
  22.6 3.9 %collective-permute-start.6 = (f32[48,8,128]{2,1,0:T(8,128)S(1)}, f32[48,8,128]{2,1,0:T(8,128)S(1)}, u32[]{:S(2)}, u32[]{:S(2)}) collective-permute-start(f32[48,8,128]{2,1,0:T(8,128)S(1)} %get-tuple-element.26.order), channel_id=1, source_target_pairs={{0,15},{1,0},{2,1},{3,2},{4,3},{5,4},{6,5},{7,6},{8,7},{9,8},{10,9... | collective-permute-start | bytes 589832 | tf_op jit(solution)/shard_map/ppermute | solution.py:424
  26.5 1.2 %collective-permute-start.7 = (f32[48,8,128]{2,1,0:T(8,128)S(1)}, f32[48,8,128]{2,1,0:T(8,128)S(1)}, u32[]{:S(2)}, u32[]{:S(2)}) collective-permute-start(f32[48,8,128]{2,1,0:T(8,128)S(1)} %get-tuple-element.28), channel_id=1, source_target_pairs={{0,1},{1,2},{2,3},{3,4},{4,5},{5,6},{6,7},{7,8},{8,9},{9,10},{10,1... | collective-permute-start | bytes 589832 | tf_op jit(solution)/shard_map/ppermute | solution.py:424
  27.7 0.0 collective-permute-done.5.above
  27.7 0.0 collective-permute-done.4.below
  27.7 7.3 %shard_map.53 = (f32[42,96,128]{2,1,0:T(8,128)S(1)}, f32[32,64,128]{2,1,0:T(8,128)}, f32[256,128]{1,0:T(8,128)S(1)}) custom-call(f32[32,64,128]{2,1,0:T(8,128)S(1)} %select_multiply_fusion.source, f32[9,64,128]{2,1,0:T(8,128)S(1)} %collective-permute-done.2.before, f32[9,64,128]{2,1,0:T(8,128)S(1)} %collective-permute-done.3.after, ...), custom_call_target="tpu_custom_call" | custom-call | tf_op jit(solution)/shard_map/pallas_call | solution.py:406
  35.0 0.0 collective-permute-done.6.above
  35.0 0.0 collective-permute-done.7.below
  35.0 25.5 %all_to_all.5 = f32[256,1,128]{2,1,0:T(1,128)S(1)} all-to-all(f32[256,1,128]{2,1,0:T(1,128)S(1)} %bitcast.5), channel_id=1, replica_groups=mesh['gx'=16,'gy'=16] {'gx','gy'}, dimensions={0} | all-to-all | bytes 262144 | tf_op jit(solution)/shard_map/all_to_all | solution.py:461
  60.5 23.7 %shard_map.54 = f32[32,64,128]{2,1,0:T(8,128)} custom-call(f32[32,64,128]{2,1,0:T(8,128)S(1)} %copy-done, f32[8,64,128]{2,1,0:T(8,128)S(1)} %collective-permute-done.before, f32[8,64,128]{2,1,0:T(8,128)S(1)} %collective-permute-done.1.after, f32[48,8,128]{2,1,0:T(8,128)S(1)} %collective-permute-done.7.below, f32[48,8,128]{2,1,0:T(8,128)S(1)} %collective-permute-done.6.above, ...), custom_call_target="tpu_custom_call" | custom-call | tf_op jit(solution)/shard_map/pallas_call | solution.py:406
  (5 shorter events, 0.1 us)
Async XLA Ops:
  0.6 7.4 %copy-start.1 = (f32[32,64,128]{2,1,0:T(8,128)S(1)}, f32[32,64,128]{2,1,0:T(8,128)}, u32[]{:S(2)}) copy-start(f32[32,64,128]{2,1,0:T(8,128)} %param.4) | copy-start | bytes 3145732
  0.6 8.9 %copy-start = (f32[32,64,128]{2,1,0:T(8,128)S(1)}, f32[32,64,128]{2,1,0:T(8,128)}, u32[]{:S(2)}) copy-start(f32[32,64,128]{2,1,0:T(8,128)} %own_level.1) | copy-start | bytes 3145732
  2.1 16.7 %collective-permute-start.2 = (f32[9,64,128]{2,1,0:T(8,128)S(1)}, f32[9,64,128]{2,1,0:T(8,128)S(1)}, u32[]{:S(2)}, u32[]{:S(2)}) collective-permute-start(f32[9,64,128]{2,1,0:T(8,128)S(1)} %get-tuple-element.36.high), channel_id=1, source_target_pairs={{0,16},{16,32},{32,48},{48,64},{64,80},{80,96},{96,112},{112,128},... | collective-permute-start | bytes 884744 | tf_op jit(solution)/shard_map/ppermute | solution.py:424
  4.3 14.5 %collective-permute-start.3 = (f32[9,64,128]{2,1,0:T(8,128)S(1)}, f32[9,64,128]{2,1,0:T(8,128)S(1)}, u32[]{:S(2)}, u32[]{:S(2)}) collective-permute-start(f32[9,64,128]{2,1,0:T(8,128)S(1)} %get-tuple-element.37.low), channel_id=1, source_target_pairs={{0,240},{16,0},{32,16},{48,32},{64,48},{80,64},{96,80},{112,96},{1... | collective-permute-start | bytes 884744 | tf_op jit(solution)/shard_map/ppermute | solution.py:424
  14.0 8.6 %collective-permute-start = (f32[8,64,128]{2,1,0:T(8,128)S(1)}, f32[8,64,128]{2,1,0:T(8,128)S(1)}, u32[]{:S(2)}, u32[]{:S(2)}) collective-permute-start(f32[8,64,128]{2,1,0:T(8,128)S(1)} %get-tuple-element.21), channel_id=1, source_target_pairs={{0,16},{16,32},{32,48},{48,64},{64,80},{80,96},{96,112},{112,128},... | collective-permute-start | bytes 786440 | tf_op jit(solution)/shard_map/ppermute | solution.py:424
  14.1 8.5 %collective-permute-start.1 = (f32[8,64,128]{2,1,0:T(8,128)S(1)}, f32[8,64,128]{2,1,0:T(8,128)S(1)}, u32[]{:S(2)}, u32[]{:S(2)}) collective-permute-start(f32[8,64,128]{2,1,0:T(8,128)S(1)} %get-tuple-element.22), channel_id=1, source_target_pairs={{0,240},{16,0},{32,16},{48,32},{64,48},{80,64},{96,80},{112,96},{1... | collective-permute-start | bytes 786440 | tf_op jit(solution)/shard_map/ppermute | solution.py:424
  18.9 8.8 %collective-permute-start.5 = (f32[456,128]{1,0:T(8,128)S(1)}, f32[456,128]{1,0:T(8,128)S(1)}, u32[]{:S(2)}, u32[]{:S(2)}) collective-permute-start(f32[456,128]{1,0:T(8,128)S(1)} %get-tuple-element.25.order), channel_id=1, source_target_pairs={{0,15},{1,0},{2,1},{3,2},{4,3},{5,4},{6,5},{7,6},{8,7},{9,8},{10,9... | collective-permute-start | bytes 700424 | tf_op jit(solution)/shard_map/ppermute | solution.py:424
  22.2 5.5 %collective-permute-start.4 = (f32[456,128]{1,0:T(8,128)S(1)}, f32[456,128]{1,0:T(8,128)S(1)}, u32[]{:S(2)}, u32[]{:S(2)}) collective-permute-start(f32[456,128]{1,0:T(8,128)S(1)} %get-tuple-element.24), channel_id=1, source_target_pairs={{0,1},{1,2},{2,3},{3,4},{4,5},{5,6},{6,7},{7,8},{8,9},{9,10},{10,1... | collective-permute-start | bytes 700424 | tf_op jit(solution)/shard_map/ppermute | solution.py:424
  22.6 12.4 %collective-permute-start.6 = (f32[48,8,128]{2,1,0:T(8,128)S(1)}, f32[48,8,128]{2,1,0:T(8,128)S(1)}, u32[]{:S(2)}, u32[]{:S(2)}) collective-permute-start(f32[48,8,128]{2,1,0:T(8,128)S(1)} %get-tuple-element.26.order), channel_id=1, source_target_pairs={{0,15},{1,0},{2,1},{3,2},{4,3},{5,4},{6,5},{7,6},{8,7},{9,8},{10,9... | collective-permute-start | bytes 589832 | tf_op jit(solution)/shard_map/ppermute | solution.py:424
  26.5 8.5 %collective-permute-start.7 = (f32[48,8,128]{2,1,0:T(8,128)S(1)}, f32[48,8,128]{2,1,0:T(8,128)S(1)}, u32[]{:S(2)}, u32[]{:S(2)}) collective-permute-start(f32[48,8,128]{2,1,0:T(8,128)S(1)} %get-tuple-element.28), channel_id=1, source_target_pairs={{0,1},{1,2},{2,3},{3,4},{4,5},{5,6},{6,7},{7,8},{8,9},{9,10},{10,1... | collective-permute-start | bytes 589832 | tf_op jit(solution)/shard_map/ppermute | solution.py:424

commit v8 on v7

--- a/solution.py
+++ b/solution.py
@@ -215,7 +215,7 @@
     return weight.astype(jnp.float32) * stress
 
 
-def pack_source(source, before, after, low, high):
+def pack_source(source, before, after, order, low, high):
     nx, ny, _ = source.shape
     wide = nx + 2 * SRC
     rest = wide * 8
@@ -231,16 +231,13 @@
     high[rest + wide :] = jnp.zeros((tail, 128), jnp.float32)
 
 
-def pack_level(level, before, after, order, low, high):
+def pack_level(level, below, above, order, low, high):
     nx, ny, _ = level.shape
-    for k in range(nx + 2 * LEV):
-        ref, j = (level, k - LEV)
-        if k < LEV:
-            ref, j = (before, k)
-        elif k >= LEV + nx:
-            ref, j = (after, k - LEV - nx)
-        low[k] = ref[j, 0:8]
-        high[k] = ref[j, ny - 8 : ny]
+    for k in range(LEV):
+        for ref, j in ((low, k), (high, nx - LEV + k)):
+            ref[k, 0:8] = below[j]
+            ref[k, 8 : 8 + ny] = level[j]
+            ref[k, 8 + ny : 16 + ny] = above[j]
 
 
 def own_lanes(level, low, high, upper, lower):
@@ -347,16 +344,14 @@
     level, rate, lanes, stage, advected, swept, acc,
 ):
     nx, ny, _ = new_level.shape
-    tall = nx + 2 * LEV
     top = OWN + ny
     for k in range(nx):
         level[LEV + k, OWN:top] = own_level[k]
+        level[LEV + k, OWN - 8 : OWN] = below[k]
+        level[LEV + k, top : top + 8] = above[k]
     for k in range(LEV):
-        level[k, OWN:top] = before[k]
-        level[LEV + nx + k, OWN:top] = after[k]
-    for k in range(tall):
-        level[k, OWN - 8 : OWN] = below[k]
-        level[k, top : top + 8] = above[k]
+        level[k, OWN - 8 : top + 8] = before[k]
+        level[LEV + nx + k, OWN - 8 : top + 8] = after[k]
 
     def emit_rate(x, t, value):
         rate[x, pl.ds(OWN - SPD + t, 8, stride=10), :] = value
@@ -401,7 +396,7 @@
 ANY = pl.BlockSpec(memory_space=pl.ANY)
 
 
-def call(kernel, outs, scratch, args, megabytes):
+def call(kernel, outs, scratch, args, megabytes, weight=None):
     ins = [a if isinstance(a, tuple) else (a, VM) for a in args]
     return pl.pallas_call(
         kernel,
@@ -409,6 +404,8 @@
         in_specs=[place for _, place in ins],
         out_specs=[VM] * len(outs),
         scratch_shapes=[pltpu.VMEM(shape, jnp.float32) for shape in scratch],
+        cost_estimate=weight
+        and pl.CostEstimate(flops=0, bytes_accessed=weight, transcendentals=0),
         compiler_params=pltpu.CompilerParams(vmem_limit_bytes=megabytes * 1024 * 1024),
     )(*[array for array, _ in ins])
 
@@ -428,36 +425,43 @@
     source_after = shift(low, "gx", size_x, -1)
     source_before = shift(high, "gx", size_x, 1)
     source = weigh(stress_jump, materials)
-    upper, lower = call(own_lanes, [tile, tile], [], (level_set, (low, ANY), (high, ANY)), 8)
-    level_low, level_high, upper, lower, source = lax.optimization_barrier(
-        (level_set[:LEV], level_set[nx - LEV :], upper, lower, source)
-    )
-    level_after = shift(level_low, "gx", size_x, -1)
-    level_before = shift(level_high, "gx", size_x, 1)
+    level_low, level_high, _, _ = lax.optimization_barrier(
+        (level_set[:, :8], level_set[:, ny - 8 :], low, high)
+    )
+    level_above = shift(level_low, "gy", size_y, -1)
+    level_below = shift(level_high, "gy", size_y, 1)
+    upper, lower = call(
+        own_lanes, [tile, tile], [], (level_set, (level_low, ANY), (level_high, ANY)), 8
+    )
     message = (wide * 8 + (wide + 7) // 8 * 8, nz)
     low, high = call(
-        pack_source, [message, message], [], (source, source_before, source_after), 8
+        pack_source,
+        [message, message],
+        [],
+        (source, source_before, source_after, (upper, ANY)),
+        8,
     )
     source_above = shift(low, "gy", size_y, -1)
     source_below = shift(high, "gy", size_y, 1)
-    message = (tall, 8, nz)
+    message = (LEV, ny + 16, nz)
     low, high = call(
         pack_level,
         [message, message],
         [],
-        (level_set, level_before, level_after, (low, ANY)),
+        (level_set, level_below, level_above, (low, ANY)),
         8,
     )
-    level_above = shift(low, "gy", size_y, -1)
-    level_below = shift(high, "gy", size_y, 1)
+    level_after = shift(low, "gx", size_x, -1)
+    level_before = shift(high, "gx", size_x, 1)
     speed, normal_speed, peaks = call(
         velocity,
         [(mid, ROWS, nz), tile, (devices, nz)],
         [(wide, ROWS, nz)] * 3,
         (source, source_before, source_after, source_below, source_above, (low, ANY)),
         BIG,
-    )
-    peaks, level_above, level_below = lax.optimization_barrier((peaks, level_above, level_below))
+        weight=60_000_000,
+    )
+    peaks, level_before, level_after = lax.optimization_barrier((peaks, level_before, level_after))
     peaks = lax.all_to_all(peaks.reshape(devices, 1, nz), ("gx", "gy"), 0, 0)
     (new_level,) = call(
         evolve,

time: 84.4 us -> 85.8 us (1.017)
  starting transfers between devices: 19.2 us -> 14.9 us
  waiting for transfers between devices: 0.4 us -> 3.8 us
  blocking collectives: 25.5 us -> 28 us
  other arithmetic: 2.93 us -> 1.71 us
  local copies, waits for them, and re-layouts: 0.04 us -> 1 us
    ppermute x8, starting transfers between devices: 19.2 us -> 14.9 us  [shift(): lax.ppermute(value, axis, [(i, (i + by) % size) for i in range(size)])]
    ppermute x8, waiting for transfers between devices: 0.4 us -> 3.8 us  [shift(): lax.ppermute(value, axis, [(i, (i + by) % size) for i in range(size)])]
    all_to_all x1, blocking collectives: 25.5 us -> 28 us  [local(): peaks = lax.all_to_all(peaks.reshape(devices, 1, nz), ('gx', 'gy'), 0, 0)]
    mul x2, other arithmetic: 2.93 us -> 1.71 us  [weigh(): return weight.astype(jnp.float32) * stress]
    slice x1, local copies, waits for them, and re-layouts: 0.04 us -> 0.99 us  [local(): level_set[:, ny - 8:]]
  transfers between devices with their start and end apart: 8 -> 8, of which waited for: 1 -> 1; matrix products, arithmetic and copies ran while one was open for 2% -> 1% of each run, Pallas kernels for 14% -> 14%
where the time goes in v8:
time: 85.8 us; the launch traced here: 85.6 us
  Pallas kernels  35.5 us (41%)
  blocking collectives  28 us (33%)
  starting transfers between devices  14.9 us (17%)
  waiting for transfers between devices  3.8 us (4%)
  other arithmetic  1.71 us (2%)
  local copies, waits for them, and re-layouts  1 us (1%)
    pallas_call x5, Pallas kernels, call(): pl.pallas_call(kernel, out_shape=[jax.ShapeDtypeStruct(shape, jnp.float32...  35.5 us
    all_to_all x1, blocking collectives, local(): peaks = lax.all_to_all(peaks.reshape(devices, 1, nz), ('gx', 'gy'), 0, 0)  28 us
    ppermute x8, starting transfers between devices, shift(): lax.ppermute(value, axis, [(i, (i + by) % size) for i in range(size)])  14.9 us
    ppermute x8, waiting for transfers between devices, shift(): lax.ppermute(value, axis, [(i, (i + by) % size) for i in range(size)])  3.8 us
  transfers between devices with their start and end apart: 8, of which 1 were waited for; matrix products, arithmetic and copies ran while one was open for 1% of the time, Pallas kernels for 14%

profile of v8, /device:TPU:1, one launch (start us, length us, event | category | flops | bytes accessed | tf_op | source)
XLA Modules:
  0.0 85.6 jit_solution(6998951190490913147)
XLA Ops:
  0.6 1.5 %slice_multiply_fusion = (f32[9,64,128]{2,1,0:T(8,128)S(1)}, f32[9,64,128]{2,1,0:T(8,128)S(1)}) fusion(f32[32,64,128]{2,1,0:T(8,128)} %param.4, s32[32,64,128]{2,1,0:T(8,128)} %param.5), kind=kLoop, calls=%fused_computation.1 | loop fusion | flops 737280 | bytes 1769472 | tf_op jit(solution)/shard_map/mul | solution.py:215
  2.1 0.0 copy-start
  2.2 2.2 %collective-permute-start = (f32[9,64,128]{2,1,0:T(8,128)S(1)}, f32[9,64,128]{2,1,0:T(8,128)S(1)}, u32[]{:S(2)}, u32[]{:S(2)}) collective-permute-start(f32[9,64,128]{2,1,0:T(8,128)S(1)} %get-tuple-element.31), channel_id=1, source_target_pairs={{0,16},{16,32},{32,48},{48,64},{64,80},{80,96},{96,112},{112,128},... | collective-permute-start | bytes 884744 | tf_op jit(solution)/shard_map/ppermute | solution.py:421
  4.4 3.7 %collective-permute-start.1 = (f32[9,64,128]{2,1,0:T(8,128)S(1)}, f32[9,64,128]{2,1,0:T(8,128)S(1)}, u32[]{:S(2)}, u32[]{:S(2)}) collective-permute-start(f32[9,64,128]{2,1,0:T(8,128)S(1)} %get-tuple-element.30), channel_id=1, source_target_pairs={{0,240},{16,0},{32,16},{48,32},{64,48},{80,64},{96,80},{112,96},{1... | collective-permute-start | bytes 884744 | tf_op jit(solution)/shard_map/ppermute | solution.py:421
  8.1 1.0 %fusion = (f32[32,8,128]{2,1,0:T(8,128)S(1)}, f32[32,8,128]{2,1,0:T(8,128)S(1)}) fusion(f32[32,64,128]{2,1,0:T(8,128)} %own_level.1), kind=kLoop, calls=%fused_computation.3 | loop fusion | bytes 524288 | tf_op jit(solution)/shard_map/slice | solution.py:429
  9.1 2.5 %collective-permute-start.4 = (f32[32,8,128]{2,1,0:T(8,128)S(1)}, f32[32,8,128]{2,1,0:T(8,128)S(1)}, u32[]{:S(2)}, u32[]{:S(2)}) collective-permute-start(f32[32,8,128]{2,1,0:T(8,128)S(1)} %get-tuple-element.17.high), channel_id=1, source_target_pairs={{0,1},{1,2},{2,3},{3,4},{4,5},{5,6},{6,7},{7,8},{8,9},{9,10},{10,1... | collective-permute-start | bytes 393224 | tf_op jit(solution)/shard_map/ppermute | solution.py:421
  11.6 0.2 collective-permute-start.5
  11.9 0.2 select_multiply_fusion.source
  12.1 4.4 %shard_map.50 = (f32[32,64,128]{2,1,0:T(8,128)S(1)}, f32[32,64,128]{2,1,0:T(8,128)S(1)}) custom-call(f32[32,64,128]{2,1,0:T(8,128)S(1)} %copy-done, f32[32,8,128]{2,1,0:T(8,128)S(1)} %get-tuple-element.16.low, f32[32,8,128]{2,1,0:T(8,128)S(1)} %get-tuple-element.17.high), custom_call_target="tpu_custom_call" | custom-call | tf_op jit(solution)/shard_map/pallas_call | solution.py:401
  16.5 0.0 collective-permute-done.before
  16.5 0.0 collective-permute-done.1.after
  16.5 0.1 shard_map.51
  16.6 0.0 collective-permute-done.4.below
  16.6 0.0 collective-permute-done.5.above
  16.6 1.5 %collective-permute-start.7 = (f32[8,80,128]{2,1,0:T(8,128)S(1)}, f32[8,80,128]{2,1,0:T(8,128)S(1)}, u32[]{:S(2)}, u32[]{:S(2)}) collective-permute-start(f32[8,80,128]{2,1,0:T(8,128)S(1)} %get-tuple-element.21.order), channel_id=1, source_target_pairs={{0,240},{16,0},{32,16},{48,32},{64,48},{80,64},{96,80},{112,96},{1... | collective-permute-start | bytes 983048 | tf_op jit(solution)/shard_map/ppermute | solution.py:421
  18.1 0.1 collective-permute-start.6
  18.2 3.8 %collective-permute-start.3 = (f32[456,128]{1,0:T(8,128)S(1)}, f32[456,128]{1,0:T(8,128)S(1)}, u32[]{:S(2)}, u32[]{:S(2)}) collective-permute-start(f32[456,128]{1,0:T(8,128)S(1)} %get-tuple-element.20.order), channel_id=1, source_target_pairs={{0,15},{1,0},{2,1},{3,2},{4,3},{5,4},{6,5},{7,6},{8,7},{9,8},{10,9... | collective-permute-start | bytes 700424 | tf_op jit(solution)/shard_map/ppermute | solution.py:421
  22.0 0.9 %collective-permute-start.2 = (f32[456,128]{1,0:T(8,128)S(1)}, f32[456,128]{1,0:T(8,128)S(1)}, u32[]{:S(2)}, u32[]{:S(2)}) collective-permute-start(f32[456,128]{1,0:T(8,128)S(1)} %get-tuple-element.19), channel_id=1, source_target_pairs={{0,1},{1,2},{2,3},{3,4},{4,5},{5,6},{6,7},{7,8},{8,9},{9,10},{10,1... | collective-permute-start | bytes 700424 | tf_op jit(solution)/shard_map/ppermute | solution.py:421
  22.8 3.8 %collective-permute-done.3.above = f32[456,128]{1,0:T(8,128)S(1)} collective-permute-done((f32[456,128]{1,0:T(8,128)S(1)}, f32[456,128]{1,0:T(8,128)S(1)}, u32[]{:S(2)}, u32[]{:S(2)}) %collective-permute-start.3) | collective-permute-done | bytes 233504 | tf_op jit(solution)/shard_map/ppermute | solution.py:421
  26.6 0.0 collective-permute-done.2.below
  26.6 7.3 %shard_map.53 = (f32[42,96,128]{2,1,0:T(8,128)S(1)}, f32[32,64,128]{2,1,0:T(8,128)}, f32[256,128]{1,0:T(8,128)S(1)}) custom-call(f32[32,64,128]{2,1,0:T(8,128)S(1)} %select_multiply_fusion.source, f32[9,64,128]{2,1,0:T(8,128)S(1)} %collective-permute-done.before, f32[9,64,128]{2,1,0:T(8,128)S(1)} %collective-permute-done.1.after, ...), custom_call_target="tpu_custom_call" | custom-call | bytes 60000000 | tf_op jit(solution)/shard_map/pallas_call | solution.py:401
  34.0 0.0 collective-permute-done.6.before
  34.0 28.0 %all_to_all.5 = f32[256,1,128]{2,1,0:T(1,128)S(1)} all-to-all(f32[256,1,128]{2,1,0:T(1,128)S(1)} %bitcast.5), channel_id=1, replica_groups=mesh['gx'=16,'gy'=16] {'gx','gy'}, dimensions={0} | all-to-all | bytes 262144 | tf_op jit(solution)/shard_map/all_to_all | solution.py:465
  61.9 23.7 %shard_map.54 = f32[32,64,128]{2,1,0:T(8,128)} custom-call(f32[32,64,128]{2,1,0:T(8,128)S(1)} %copy-done, f32[8,80,128]{2,1,0:T(8,128)S(1)} %collective-permute-done.6.before, f32[8,80,128]{2,1,0:T(8,128)S(1)} %collective-permute-done.7.after, f32[32,8,128]{2,1,0:T(8,128)S(1)} %collective-permute-done.4.below, ...), custom_call_target="tpu_custom_call" | custom-call | tf_op jit(solution)/shard_map/pallas_call | solution.py:401
  (7 shorter events, 0.1 us)
Async XLA Ops:
  0.6 11.2 %copy-start.1 = (f32[32,64,128]{2,1,0:T(8,128)S(1)}, f32[32,64,128]{2,1,0:T(8,128)}, u32[]{:S(2)}) copy-start(f32[32,64,128]{2,1,0:T(8,128)} %param.4) | copy-start | bytes 3145732
  0.6 11.2 %copy-start.2 = (s32[32,64,128]{2,1,0:T(8,128)S(1)}, s32[32,64,128]{2,1,0:T(8,128)}, u32[]{:S(2)}) copy-start(s32[32,64,128]{2,1,0:T(8,128)} %param.5) | copy-start | bytes 3145732
  2.1 9.9 %copy-start = (f32[32,64,128]{2,1,0:T(8,128)S(1)}, f32[32,64,128]{2,1,0:T(8,128)}, u32[]{:S(2)}) copy-start(f32[32,64,128]{2,1,0:T(8,128)} %own_level.1) | copy-start | bytes 3145732
  2.2 14.3 %collective-permute-start = (f32[9,64,128]{2,1,0:T(8,128)S(1)}, f32[9,64,128]{2,1,0:T(8,128)S(1)}, u32[]{:S(2)}, u32[]{:S(2)}) collective-permute-start(f32[9,64,128]{2,1,0:T(8,128)S(1)} %get-tuple-element.31), channel_id=1, source_target_pairs={{0,16},{16,32},{32,48},{48,64},{64,80},{80,96},{96,112},{112,128},... | collective-permute-start | bytes 884744 | tf_op jit(solution)/shard_map/ppermute | solution.py:421
  4.4 12.1 %collective-permute-start.1 = (f32[9,64,128]{2,1,0:T(8,128)S(1)}, f32[9,64,128]{2,1,0:T(8,128)S(1)}, u32[]{:S(2)}, u32[]{:S(2)}) collective-permute-start(f32[9,64,128]{2,1,0:T(8,128)S(1)} %get-tuple-element.30), channel_id=1, source_target_pairs={{0,240},{16,0},{32,16},{48,32},{64,48},{80,64},{96,80},{112,96},{1... | collective-permute-start | bytes 884744 | tf_op jit(solution)/shard_map/ppermute | solution.py:421
  9.1 7.5 %collective-permute-start.4 = (f32[32,8,128]{2,1,0:T(8,128)S(1)}, f32[32,8,128]{2,1,0:T(8,128)S(1)}, u32[]{:S(2)}, u32[]{:S(2)}) collective-permute-start(f32[32,8,128]{2,1,0:T(8,128)S(1)} %get-tuple-element.17.high), channel_id=1, source_target_pairs={{0,1},{1,2},{2,3},{3,4},{4,5},{5,6},{6,7},{7,8},{8,9},{9,10},{10,1... | collective-permute-start | bytes 393224 | tf_op jit(solution)/shard_map/ppermute | solution.py:421
  11.6 5.0 %collective-permute-start.5 = (f32[32,8,128]{2,1,0:T(8,128)S(1)}, f32[32,8,128]{2,1,0:T(8,128)S(1)}, u32[]{:S(2)}, u32[]{:S(2)}) collective-permute-start(f32[32,8,128]{2,1,0:T(8,128)S(1)} %get-tuple-element.16.low), channel_id=1, source_target_pairs={{0,15},{1,0},{2,1},{3,2},{4,3},{5,4},{6,5},{7,6},{8,7},{9,8},{10,9... | collective-permute-start | bytes 393224 | tf_op jit(solution)/shard_map/ppermute | solution.py:421
  16.6 17.3 %collective-permute-start.7 = (f32[8,80,128]{2,1,0:T(8,128)S(1)}, f32[8,80,128]{2,1,0:T(8,128)S(1)}, u32[]{:S(2)}, u32[]{:S(2)}) collective-permute-start(f32[8,80,128]{2,1,0:T(8,128)S(1)} %get-tuple-element.21.order), channel_id=1, source_target_pairs={{0,240},{16,0},{32,16},{48,32},{64,48},{80,64},{96,80},{112,96},{1... | collective-permute-start | bytes 983048 | tf_op jit(solution)/shard_map/ppermute | solution.py:421
  18.1 15.9 %collective-permute-start.6 = (f32[8,80,128]{2,1,0:T(8,128)S(1)}, f32[8,80,128]{2,1,0:T(8,128)S(1)}, u32[]{:S(2)}, u32[]{:S(2)}) collective-permute-start(f32[8,80,128]{2,1,0:T(8,128)S(1)} %get-tuple-element.23), channel_id=1, source_target_pairs={{0,16},{16,32},{32,48},{48,64},{64,80},{80,96},{96,112},{112,128},... | collective-permute-start | bytes 983048 | tf_op jit(solution)/shard_map/ppermute | solution.py:421
  18.2 8.4 %collective-permute-start.3 = (f32[456,128]{1,0:T(8,128)S(1)}, f32[456,128]{1,0:T(8,128)S(1)}, u32[]{:S(2)}, u32[]{:S(2)}) collective-permute-start(f32[456,128]{1,0:T(8,128)S(1)} %get-tuple-element.20.order), channel_id=1, source_target_pairs={{0,15},{1,0},{2,1},{3,2},{4,3},{5,4},{6,5},{7,6},{8,7},{9,8},{10,9... | collective-permute-start | bytes 700424 | tf_op jit(solution)/shard_map/ppermute | solution.py:421
  22.0 4.7 %collective-permute-start.2 = (f32[456,128]{1,0:T(8,128)S(1)}, f32[456,128]{1,0:T(8,128)S(1)}, u32[]{:S(2)}, u32[]{:S(2)}) collective-permute-start(f32[456,128]{1,0:T(8,128)S(1)} %get-tuple-element.19), channel_id=1, source_target_pairs={{0,1},{1,2},{2,3},{3,4},{4,5},{5,6},{6,7},{7,8},{8,9},{9,10},{10,1... | collective-permute-start | bytes 700424 | tf_op jit(solution)/shard_map/ppermute | solution.py:421

commit v9 on v7

--- a/solution.py
+++ b/solution.py
@@ -215,7 +215,7 @@
     return weight.astype(jnp.float32) * stress
 
 
-def pack_source(source, before, after, low, high):
+def pack_source(source, before, after, order, low, high):
     nx, ny, _ = source.shape
     wide = nx + 2 * SRC
     rest = wide * 8
@@ -428,15 +428,17 @@
     source_after = shift(low, "gx", size_x, -1)
     source_before = shift(high, "gx", size_x, 1)
     source = weigh(stress_jump, materials)
-    upper, lower = call(own_lanes, [tile, tile], [], (level_set, (low, ANY), (high, ANY)), 8)
-    level_low, level_high, upper, lower, source = lax.optimization_barrier(
-        (level_set[:LEV], level_set[nx - LEV :], upper, lower, source)
+    level_low, level_high, _, _ = lax.optimization_barrier(
+        (level_set[:LEV], level_set[nx - LEV :], low, high)
     )
     level_after = shift(level_low, "gx", size_x, -1)
     level_before = shift(level_high, "gx", size_x, 1)
+    upper, lower = call(
+        own_lanes, [tile, tile], [], (level_set, (level_low, ANY), (level_high, ANY)), 8
+    )
     message = (wide * 8 + (wide + 7) // 8 * 8, nz)
     low, high = call(
-        pack_source, [message, message], [], (source, source_before, source_after), 8
+        pack_source, [message, message], [], (source, source_before, source_after, (upper, ANY)), 8
     )
     source_above = shift(low, "gy", size_y, -1)
     source_below = shift(high, "gy", size_y, 1)

time: 84.4 us -> 81.5 us (0.966)
  starting transfers between devices: 19.2 us -> 16.8 us
  other arithmetic: 2.93 us -> 1.73 us
    ppermute x8, starting transfers between devices: 19.2 us -> 16.8 us  [shift(): lax.ppermute(value, axis, [(i, (i + by) % size) for i in range(size)])]
    mul x2, other arithmetic: 2.93 us -> 1.73 us  [weigh(): return weight.astype(jnp.float32) * stress]
  transfers between devices with their start and end apart: 8 -> 8, of which waited for: 1 -> 2; matrix products, arithmetic and copies ran while one was open for 2% -> 0% of each run, Pallas kernels for 14% -> 14%
where the time goes in v9:
time: 81.5 us; the launch traced here: 81.4 us
  Pallas kernels  35.5 us (44%)
  blocking collectives  25.7 us (32%)
  starting transfers between devices  16.8 us (21%)
  other arithmetic  1.73 us (2%)
  waiting for transfers between devices  0.94 us (1%)
    pallas_call x5, Pallas kernels, call(): pl.pallas_call(kernel, out_shape=[jax.ShapeDtypeStruct(shape, jnp.float32...  35.5 us
    all_to_all x1, blocking collectives, local(): peaks = lax.all_to_all(peaks.reshape(devices, 1, nz), ('gx', 'gy'), 0, 0)  25.7 us
    ppermute x8, starting transfers between devices, shift(): lax.ppermute(value, axis, [(i, (i + by) % size) for i in range(size)])  16.8 us
    mul x2, other arithmetic, weigh(): return weight.astype(jnp.float32) * stress  1.73 us
  transfers between devices with their start and end apart: 8, of which 2 were waited for; matrix products, arithmetic and copies ran while one was open for 0% of the time, Pallas kernels for 14%

profile of v9, /device:TPU:1, one launch (start us, length us, event | category | flops | bytes accessed | tf_op | source)
XLA Modules:
  0.0 81.4 jit_solution(16427267025659966299)
XLA Ops:
  0.7 1.5 %slice_multiply_fusion = (f32[9,64,128]{2,1,0:T(8,128)S(1)}, f32[9,64,128]{2,1,0:T(8,128)S(1)}) fusion(f32[32,64,128]{2,1,0:T(8,128)} %param.4, s32[32,64,128]{2,1,0:T(8,128)} %param.5), kind=kLoop, calls=%fused_computation.1 | loop fusion | flops 737280 | bytes 1769472 | tf_op jit(solution)/shard_map/mul | solution.py:215
  2.2 2.2 %collective-permute-start.2 = (f32[9,64,128]{2,1,0:T(8,128)S(1)}, f32[9,64,128]{2,1,0:T(8,128)S(1)}, u32[]{:S(2)}, u32[]{:S(2)}) collective-permute-start(f32[9,64,128]{2,1,0:T(8,128)S(1)} %get-tuple-element.30), channel_id=1, source_target_pairs={{0,16},{16,32},{32,48},{48,64},{64,80},{80,96},{96,112},{112,128},... | collective-permute-start | bytes 884744 | tf_op jit(solution)/shard_map/ppermute | solution.py:424
  4.4 3.7 %collective-permute-start.3 = (f32[9,64,128]{2,1,0:T(8,128)S(1)}, f32[9,64,128]{2,1,0:T(8,128)S(1)}, u32[]{:S(2)}, u32[]{:S(2)}) collective-permute-start(f32[9,64,128]{2,1,0:T(8,128)S(1)} %get-tuple-element.31), channel_id=1, source_target_pairs={{0,240},{16,0},{32,16},{48,32},{64,48},{80,64},{96,80},{112,96},{1... | collective-permute-start | bytes 884744 | tf_op jit(solution)/shard_map/ppermute | solution.py:424
  8.1 0.0 copy-done
  8.1 0.1 collective-permute-start
  8.2 4.8 %collective-permute-start.1 = (f32[8,64,128]{2,1,0:T(8,128)S(1)}, f32[8,64,128]{2,1,0:T(8,128)S(1)}, u32[]{:S(2)}, u32[]{:S(2)}) collective-permute-start(f32[8,64,128]{2,1,0:T(8,128)S(1)} %get-tuple-element.17.low), channel_id=1, source_target_pairs={{0,240},{16,0},{32,16},{48,32},{64,48},{80,64},{96,80},{112,96},{1... | collective-permute-start | bytes 786440 | tf_op jit(solution)/shard_map/ppermute | solution.py:424
  13.0 4.4 %shard_map.50 = (f32[32,64,128]{2,1,0:T(8,128)S(1)}, f32[32,64,128]{2,1,0:T(8,128)S(1)}) custom-call(f32[32,64,128]{2,1,0:T(8,128)S(1)} %copy-done, f32[8,64,128]{2,1,0:T(8,128)S(1)} %get-tuple-element.17.low, f32[8,64,128]{2,1,0:T(8,128)S(1)} %get-tuple-element.16.high), custom_call_target="tpu_custom_call" | custom-call | tf_op jit(solution)/shard_map/pallas_call | solution.py:406
  17.4 0.2 select_multiply_fusion.source
  17.6 0.0 collective-permute-done.2.before
  17.7 0.0 collective-permute-done.3.after
  17.7 0.1 shard_map.51
  17.7 3.3 %collective-permute-start.5 = (f32[456,128]{1,0:T(8,128)S(1)}, f32[456,128]{1,0:T(8,128)S(1)}, u32[]{:S(2)}, u32[]{:S(2)}) collective-permute-start(f32[456,128]{1,0:T(8,128)S(1)} %get-tuple-element.20.order), channel_id=1, source_target_pairs={{0,15},{1,0},{2,1},{3,2},{4,3},{5,4},{6,5},{7,6},{8,7},{9,8},{10,9... | collective-permute-start | bytes 700424 | tf_op jit(solution)/shard_map/ppermute | solution.py:424
  21.0 0.0 collective-permute-start.4
  21.0 0.0 collective-permute-done.before
  21.0 0.0 collective-permute-done.1.after
  21.1 2.7 %collective-permute-start.6 = (f32[48,8,128]{2,1,0:T(8,128)S(1)}, f32[48,8,128]{2,1,0:T(8,128)S(1)}, u32[]{:S(2)}, u32[]{:S(2)}) collective-permute-start(f32[48,8,128]{2,1,0:T(8,128)S(1)} %get-tuple-element.21.order), channel_id=1, source_target_pairs={{0,15},{1,0},{2,1},{3,2},{4,3},{5,4},{6,5},{7,6},{8,7},{9,8},{10,9... | collective-permute-start | bytes 589832 | tf_op jit(solution)/shard_map/ppermute | solution.py:424
  23.8 0.0 collective-permute-start.7
  23.8 0.8 collective-permute-done.5.above
  24.6 0.1 collective-permute-done.4.below
  24.7 7.3 %shard_map.53 = (f32[42,96,128]{2,1,0:T(8,128)S(1)}, f32[32,64,128]{2,1,0:T(8,128)}, f32[256,128]{1,0:T(8,128)S(1)}) custom-call(f32[32,64,128]{2,1,0:T(8,128)S(1)} %select_multiply_fusion.source, f32[9,64,128]{2,1,0:T(8,128)S(1)} %collective-permute-done.2.before, f32[9,64,128]{2,1,0:T(8,128)S(1)} %collective-permute-done.3.after, ...), custom_call_target="tpu_custom_call" | custom-call | tf_op jit(solution)/shard_map/pallas_call | solution.py:406
  32.0 0.0 collective-permute-done.6.above
  32.0 0.0 collective-permute-done.7.below
  32.0 25.7 %all_to_all.5 = f32[256,1,128]{2,1,0:T(1,128)S(1)} all-to-all(f32[256,1,128]{2,1,0:T(1,128)S(1)} %bitcast.5), channel_id=1, replica_groups=mesh['gx'=16,'gy'=16] {'gx','gy'}, dimensions={0} | all-to-all | bytes 262144 | tf_op jit(solution)/shard_map/all_to_all | solution.py:463
  57.7 23.7 %shard_map.54 = f32[32,64,128]{2,1,0:T(8,128)} custom-call(f32[32,64,128]{2,1,0:T(8,128)S(1)} %copy-done, f32[8,64,128]{2,1,0:T(8,128)S(1)} %collective-permute-done.before, f32[8,64,128]{2,1,0:T(8,128)S(1)} %collective-permute-done.1.after, f32[48,8,128]{2,1,0:T(8,128)S(1)} %collective-permute-done.7.below, f32[48,8,128]{2,1,0:T(8,128)S(1)} %collective-permute-done.6.above, ...), custom_call_target="tpu_custom_call" | custom-call | tf_op jit(solution)/shard_map/pallas_call | solution.py:406
  (7 shorter events, 0.1 us)
Async XLA Ops:
  0.6 7.5 %copy-start = (f32[32,64,128]{2,1,0:T(8,128)S(1)}, f32[32,64,128]{2,1,0:T(8,128)}, u32[]{:S(2)}) copy-start(f32[32,64,128]{2,1,0:T(8,128)} %own_level.1) | copy-start | bytes 3145732
  0.6 16.7 %copy-start.1 = (f32[32,64,128]{2,1,0:T(8,128)S(1)}, f32[32,64,128]{2,1,0:T(8,128)}, u32[]{:S(2)}) copy-start(f32[32,64,128]{2,1,0:T(8,128)} %param.4) | copy-start | bytes 3145732
  0.6 16.7 %copy-start.2 = (s32[32,64,128]{2,1,0:T(8,128)S(1)}, s32[32,64,128]{2,1,0:T(8,128)}, u32[]{:S(2)}) copy-start(s32[32,64,128]{2,1,0:T(8,128)} %param.5) | copy-start | bytes 3145732
  2.2 15.5 %collective-permute-start.2 = (f32[9,64,128]{2,1,0:T(8,128)S(1)}, f32[9,64,128]{2,1,0:T(8,128)S(1)}, u32[]{:S(2)}, u32[]{:S(2)}) collective-permute-start(f32[9,64,128]{2,1,0:T(8,128)S(1)} %get-tuple-element.30), channel_id=1, source_target_pairs={{0,16},{16,32},{32,48},{48,64},{64,80},{80,96},{96,112},{112,128},... | collective-permute-start | bytes 884744 | tf_op jit(solution)/shard_map/ppermute | solution.py:424
  4.4 13.3 %collective-permute-start.3 = (f32[9,64,128]{2,1,0:T(8,128)S(1)}, f32[9,64,128]{2,1,0:T(8,128)S(1)}, u32[]{:S(2)}, u32[]{:S(2)}) collective-permute-start(f32[9,64,128]{2,1,0:T(8,128)S(1)} %get-tuple-element.31), channel_id=1, source_target_pairs={{0,240},{16,0},{32,16},{48,32},{64,48},{80,64},{96,80},{112,96},{1... | collective-permute-start | bytes 884744 | tf_op jit(solution)/shard_map/ppermute | solution.py:424
  8.1 12.9 %collective-permute-start = (f32[8,64,128]{2,1,0:T(8,128)S(1)}, f32[8,64,128]{2,1,0:T(8,128)S(1)}, u32[]{:S(2)}, u32[]{:S(2)}) collective-permute-start(f32[8,64,128]{2,1,0:T(8,128)S(1)} %get-tuple-element.16.high), channel_id=1, source_target_pairs={{0,16},{16,32},{32,48},{48,64},{64,80},{80,96},{96,112},{112,128},... | collective-permute-start | bytes 786440 | tf_op jit(solution)/shard_map/ppermute | solution.py:424
  8.2 12.8 %collective-permute-start.1 = (f32[8,64,128]{2,1,0:T(8,128)S(1)}, f32[8,64,128]{2,1,0:T(8,128)S(1)}, u32[]{:S(2)}, u32[]{:S(2)}) collective-permute-start(f32[8,64,128]{2,1,0:T(8,128)S(1)} %get-tuple-element.17.low), channel_id=1, source_target_pairs={{0,240},{16,0},{32,16},{48,32},{64,48},{80,64},{96,80},{112,96},{1... | collective-permute-start | bytes 786440 | tf_op jit(solution)/shard_map/ppermute | solution.py:424
  17.7 6.8 %collective-permute-start.5 = (f32[456,128]{1,0:T(8,128)S(1)}, f32[456,128]{1,0:T(8,128)S(1)}, u32[]{:S(2)}, u32[]{:S(2)}) collective-permute-start(f32[456,128]{1,0:T(8,128)S(1)} %get-tuple-element.20.order), channel_id=1, source_target_pairs={{0,15},{1,0},{2,1},{3,2},{4,3},{5,4},{6,5},{7,6},{8,7},{9,8},{10,9... | collective-permute-start | bytes 700424 | tf_op jit(solution)/shard_map/ppermute | solution.py:424
  21.0 3.7 %collective-permute-start.4 = (f32[456,128]{1,0:T(8,128)S(1)}, f32[456,128]{1,0:T(8,128)S(1)}, u32[]{:S(2)}, u32[]{:S(2)}) collective-permute-start(f32[456,128]{1,0:T(8,128)S(1)} %get-tuple-element.19), channel_id=1, source_target_pairs={{0,1},{1,2},{2,3},{3,4},{4,5},{5,6},{6,7},{7,8},{8,9},{9,10},{10,1... | collective-permute-start | bytes 700424 | tf_op jit(solution)/shard_map/ppermute | solution.py:424
  21.1 10.9 %collective-permute-start.6 = (f32[48,8,128]{2,1,0:T(8,128)S(1)}, f32[48,8,128]{2,1,0:T(8,128)S(1)}, u32[]{:S(2)}, u32[]{:S(2)}) collective-permute-start(f32[48,8,128]{2,1,0:T(8,128)S(1)} %get-tuple-element.21.order), channel_id=1, source_target_pairs={{0,15},{1,0},{2,1},{3,2},{4,3},{5,4},{6,5},{7,6},{8,7},{9,8},{10,9... | collective-permute-start | bytes 589832 | tf_op jit(solution)/shard_map/ppermute | solution.py:424
  23.8 8.3 %collective-permute-start.7 = (f32[48,8,128]{2,1,0:T(8,128)S(1)}, f32[48,8,128]{2,1,0:T(8,128)S(1)}, u32[]{:S(2)}, u32[]{:S(2)}) collective-permute-start(f32[48,8,128]{2,1,0:T(8,128)S(1)} %get-tuple-element.23), channel_id=1, source_target_pairs={{0,1},{1,2},{2,3},{3,4},{4,5},{5,6},{6,7},{7,8},{8,9},{9,10},{10,1... | collective-permute-start | bytes 589832 | tf_op jit(solution)/shard_map/ppermute | solution.py:424

commit v10 on v6

--- a/solution.py
+++ b/solution.py
@@ -21,6 +21,8 @@
 SRC = 9
 LEV = 8
 SPD = 5
+GROUP = 16
+ROW_GROUPS = 6
 
 
 def velocity_polynomial():
@@ -111,8 +113,32 @@
         yield i, left, right
 
 
-def weno_lanes(f):
-    cells = {k: along_lanes(f, k) if k else f for k in range(-3, 3)}
+SHIFTS = (-3, -2, -1, 1, 2)
+
+
+def piped(groups, tiles, load, compute, buffers):
+    def fill(buffer, g):
+        for j in range(tiles):
+            f = load(g, j)
+            for n, k in enumerate(SHIFTS):
+                buffer[n, j] = along_lanes(f, k)
+
+    fill(buffers[0], 0)
+
+    def body(p, _):
+        for parity in range(2):
+            g = 2 * p + parity
+            fill(buffers[1 - parity], jnp.minimum(g + 1, groups - 1))
+            for j in range(tiles):
+                cells = {k: buffers[parity][n, j] for n, k in enumerate(SHIFTS)}
+                cells[0] = load(g, j)
+                compute(g, j, cells)
+        return _
+
+    lax.fori_loop(0, groups // 2, body, 0)
+
+
+def weno_lanes(cells):
     first = {k: cells[k + 1] - cells[k] for k in range(-3, 2)}
     second = {k: first[k] - first[k - 1] for k in range(-2, 2)}
     third = {k: second[k + 1] - second[k] for k in range(-2, 1)}
@@ -143,7 +169,7 @@
     return ref[x, pl.ds(start, 8, stride=step), :]
 
 
-def weno_rates(field, fx, speed, sx, acc, planes, start, step, emit):
+def weno_rates(field, fx, speed, sx, acc, planes, start, step, emit, lanes=None, buffers=None):
     def along_x(t, _):
         row = start + t
 
@@ -157,7 +183,11 @@
 
     lax.fori_loop(0, step, along_x, 0)
 
-    def along_yz(x, _):
+    def finish(x, t, total):
+        velocity = strided(speed, sx + x, start + t, step)
+        emit(x, t, velocity * (root(total) * (-1.0 / 12.0)))
+
+    def along_y(x, _):
         lines = {}
 
         def f(j):
@@ -166,15 +196,46 @@
             return lines[j]
 
         for t, left, right in weno_line(f, step):
-            velocity = strided(speed, sx + x, start + t, step)
-            sign = sign_of(velocity)
+            sign = sign_of(strided(speed, sx + x, start + t, step))
             total = acc[x, t] + upwind_square(left, right, sign)
-            left, right = weno_lanes(f(t))
-            total = total + upwind_square(left, right, sign)
-            emit(x, t, velocity * (root(total) * (-1.0 / 12.0)))
-        return _
-
-    lax.fori_loop(0, planes, along_yz, 0, unroll=3)
+            if lanes is None:
+                acc[x, t] = total
+            else:
+                finish(x, t, total + strided(lanes, x, start + t, step))
+        return _
+
+    def along_yz(p, _):
+        for parity in range(2):
+            x = 2 * p + parity
+            after = jnp.minimum(x + 1, planes - 1)
+            for t in range(step):
+                g = strided(field, fx + after, start + t, step)
+                for n, k in enumerate(SHIFTS):
+                    buffers[1 - parity][n, t] = along_lanes(g, k)
+            lines = {}
+
+            def f(j):
+                if j not in lines:
+                    lines[j] = strided(field, fx + x, start + j, step)
+                return lines[j]
+
+            for t, left, right in weno_line(f, step):
+                sign = sign_of(strided(speed, sx + x, start + t, step))
+                total = acc[x, t] + upwind_square(left, right, sign)
+                cells = {k: buffers[parity][n, t] for n, k in enumerate(SHIFTS)}
+                cells[0] = f(t)
+                left, right = weno_lanes(cells)
+                finish(x, t, total + upwind_square(left, right, sign))
+        return _
+
+    if lanes is None:
+        for t in range(step):
+            g = strided(field, fx, start + t, step)
+            for n, k in enumerate(SHIFTS):
+                buffers[0][n, t] = along_lanes(g, k)
+        lax.fori_loop(0, planes // 2, along_yz, 0)
+    else:
+        lax.fori_loop(0, planes, along_y, 0, unroll=3)
 
 
 def reinit_sweep(field, fx, origin, ox, planes, start, step, emit):
@@ -212,7 +273,7 @@
     return weight.astype(jnp.float32) * stress
 
 
-def pack_source(source, before, after, low, high):
+def pack_source(source, before, after, order, low, high):
     nx, ny, _ = source.shape
     wide = nx + 2 * SRC
     rest = wide * 8
@@ -240,8 +301,55 @@
         high[k] = ref[j, ny - 8 : ny]
 
 
+def own_lanes(level, low, high, upper, lower, *buffers):
+    nx, ny, _ = level.shape
+    rows = ny // 8
+
+    def tile(g, j):
+        return g * (GROUP // rows) + j // rows, slice(j % rows * 8, j % rows * 8 + 8)
+
+    def compute(g, j, cells):
+        left, right = weno_lanes(cells)
+        upper[tile(g, j)] = jnp.square(jnp.maximum(jnp.maximum(left, right), 0.0))
+        lower[tile(g, j)] = jnp.square(jnp.minimum(jnp.minimum(left, right), 0.0))
+
+    piped(nx * rows // GROUP, GROUP, lambda g, j: level[tile(g, j)], compute, buffers)
+
+
+def other_lanes(level, speed, upper, lower, lanes, buffers):
+    nx, ny, _ = upper.shape
+    top = OWN + ny
+
+    def outside(groups, tiles, tile):
+        def load(g, j):
+            x, row = tile(g, j)
+            return level[x + LEV - SPD, row : row + 8]
+
+        def compute(g, j, cells):
+            x, row = tile(g, j)
+            left, right = weno_lanes(cells)
+            sign = sign_of(speed[x, row : row + 8])
+            lanes[x, row : row + 8] = upwind_square(left, right, sign)
+
+        piped(groups, tiles, load, compute, buffers)
+
+    planes = nx + 2 * SPD
+    outside(ROW_GROUPS, 2 * planes // ROW_GROUPS, lambda g, j: (g * (planes // ROW_GROUPS) + j // 2, (OWN - 8, top)[j % 2]))
+    rows = ny // 8
+    outside(
+        2 * SPD, rows, lambda g, j: (g + jnp.where(g < SPD, 0, nx), OWN + 8 * j)
+    )
+
+    def own(x, _):
+        positive = speed[SPD + x, OWN:top] > 0
+        lanes[SPD + x, OWN:top] = jnp.where(positive, upper[x], lower[x])
+        return _
+
+    lax.fori_loop(0, nx, own, 0, unroll=2)
+
+
 def velocity(
-    source, before, after, below, above, order, speed, own_speed, peaks, src, one, two
+    source, before, after, below, above, order, speed, own_speed, peaks, src, one, two, sem
 ):
     nx, ny, _ = source.shape
     wide = nx + 2 * SRC
@@ -288,21 +396,26 @@
     sweep(two, one, 0, 3, wide - 3, None, coefficients[1])
     sweep(one, speed, SRC - SPD, 4, wide - 4, None, coefficients[0])
 
+    leaving = pltpu.make_async_copy(
+        speed.at[pl.ds(SPD, nx), pl.ds(OWN, ny)], own_speed, sem.at[0]
+    )
+    leaving.start()
+
     def largest(x, carry):
-        mine = speed[SPD + x, OWN : OWN + ny]
-        own_speed[x] = mine
-        return jnp.maximum(carry, jnp.abs(mine))
+        return jnp.maximum(carry, jnp.abs(speed[SPD + x, OWN : OWN + ny]))
 
     top = lax.fori_loop(0, nx, largest, jnp.zeros((ny, 128), jnp.float32))
     peaks[...] = jnp.broadcast_to(jnp.max(top), peaks.shape)
+    leaving.wait()
 
 
 def evolve(
-    own_level, before, after, below, above, speed, peaks, new_level,
-    level, rate, stage, advected, swept, acc,
+    own_level, before, after, below, above, speed, upper, lower, peaks, new_level,
+    level, rate, lanes, stage, advected, swept, acc, even, odd, result, sems,
 ):
     nx, ny, _ = new_level.shape
     tall = nx + 2 * LEV
+    buffers = (even, odd)
     top = OWN + ny
     for k in range(nx):
         level[LEV + k, OWN:top] = own_level[k]
@@ -316,7 +429,8 @@
     def emit_rate(x, t, value):
         rate[x, pl.ds(OWN - SPD + t, 8, stride=10), :] = value
 
-    weno_rates(level, LEV - SPD, speed, 0, acc, nx + 2 * SPD, OWN - SPD, 10, emit_rate)
+    other_lanes(level, speed, upper, lower, lanes, buffers)
+    weno_rates(level, LEV - SPD, speed, 0, acc, nx + 2 * SPD, OWN - SPD, 10, emit_rate, lanes)
 
     peak = jnp.max(peaks[...], axis=0, keepdims=True)
     time_step = courant / (peak + 1e-06)
@@ -337,32 +451,49 @@
         before = strided(level, x + LEV - 2, row, step)
         advected[x, pl.ds(row, 8, stride=step), :] = 0.5 * before + 0.5 * after
 
-    weno_rates(stage, SPD - 2, speed, SPD - 2, acc, nx + 4, start, step, emit)
+    weno_rates(stage, SPD - 2, speed, SPD - 2, acc, nx + 4, start, step, emit, None, buffers)
 
     def emit_one(x, t, value):
         swept[x, pl.ds(OWN - 1 + t, 8, stride=9), :] = value
 
     reinit_sweep(advected, 1, advected, 1, nx + 2, OWN - 1, 9, emit_one)
 
-    def emit_two(x, t, value):
-        new_level[x, pl.ds(t, 8, stride=ny // 8), :] = value
-
-    reinit_sweep(swept, 1, advected, 2, nx, OWN, ny // 8, emit_two)
-
-
+    part = nx // PARTS
+    leaving = []
+    for n in range(PARTS):
+        first = n * part
+
+        def emit_two(x, t, value):
+            result[first + x, pl.ds(t, 8, stride=ny // 8), :] = value
+
+        reinit_sweep(swept, 1 + first, advected, 2 + first, part, OWN, ny // 8, emit_two)
+        planes = pl.ds(first, part)
+        leaving.append(
+            pltpu.make_async_copy(result.at[planes], new_level.at[planes], sems.at[n])
+        )
+        leaving[n].start()
+    for copy in leaving:
+        copy.wait()
+
+
+PARTS = 4
 BIG = 32
 VM = pl.BlockSpec(memory_space=pltpu.VMEM)
 ANY = pl.BlockSpec(memory_space=pl.ANY)
 
 
-def call(kernel, outs, scratch, args, megabytes):
+def call(kernel, outs, scratch, args, megabytes, copies=0):
     ins = [a if isinstance(a, tuple) else (a, VM) for a in args]
+    outs = [o if isinstance(o[0], tuple) else (o, VM) for o in outs]
+    scratch = [pltpu.VMEM(shape, jnp.float32) for shape in scratch]
+    if copies:
+        scratch.append(pltpu.SemaphoreType.DMA((copies,)))
     return pl.pallas_call(
         kernel,
-        out_shape=[jax.ShapeDtypeStruct(shape, jnp.float32) for shape in outs],
+        out_shape=[jax.ShapeDtypeStruct(shape, jnp.float32) for shape, _ in outs],
         in_specs=[place for _, place in ins],
-        out_specs=[VM] * len(outs),
-        scratch_shapes=[pltpu.VMEM(shape, jnp.float32) for shape in scratch],
+        out_specs=[place for _, place in outs],
+        scratch_shapes=scratch,
         compiler_params=pltpu.CompilerParams(vmem_limit_bytes=megabytes * 1024 * 1024),
     )(*[array for array, _ in ins])
 
@@ -387,9 +518,12 @@
     )
     level_after = shift(level_low, "gx", size_x, -1)
     level_before = shift(level_high, "gx", size_x, 1)
+    upper, lower = call(
+        own_lanes, [tile, tile], [(5, GROUP, 8, nz)] * 2, (level_set, (level_low, ANY), (level_high, ANY)), 8
+    )
     message = (wide * 8 + (wide + 7) // 8 * 8, nz)
     low, high = call(
-        pack_source, [message, message], [], (source, source_before, source_after), 8
+        pack_source, [message, message], [], (source, source_before, source_after, (upper, ANY)), 8
     )
     source_above = shift(low, "gy", size_y, -1)
     source_below = shift(high, "gy", size_y, 1)
@@ -405,24 +539,28 @@
     level_below = shift(high, "gy", size_y, 1)
     speed, normal_speed, peaks = call(
         velocity,
-        [(mid, ROWS, nz), tile, (devices, nz)],
+        [(mid, ROWS, nz), (tile, ANY), (devices, nz)],
         [(wide, ROWS, nz)] * 3,
         (source, source_before, source_after, source_below, source_above, (low, ANY)),
         BIG,
+        copies=1,
     )
     peaks, level_above, level_below = lax.optimization_barrier((peaks, level_above, level_below))
     peaks = lax.all_to_all(peaks.reshape(devices, 1, nz), ("gx", "gy"), 0, 0)
     (new_level,) = call(
         evolve,
-        [tile],
+        [(tile, ANY)],
         [
             (tall, ROWS, nz),
+            (mid, ROWS, nz),
             (mid, ROWS, nz),
             (mid, ROWS, nz),
             (nx + 4, ROWS, nz),
             (nx + 2, ROWS, nz),
             (mid, 10, 8, nz),
-        ],
+        ]
+        + [(5, GROUP, 8, nz)] * 2
+        + [tile],
         (
             level_set,
             level_before,
@@ -430,9 +568,12 @@
             level_below,
             level_above,
             speed,
+            upper,
+            lower,
             peaks.reshape(devices, nz),
         ),
         BIG,
+        copies=PARTS,
     )
     return (new_level, normal_speed)
 

time: 83.6 us -> 80.2 us (0.959)
  other arithmetic: 2.95 us -> 1.73 us
  starting transfers between devices: 18.7 us -> 17.5 us
    mul x2, other arithmetic: 2.95 us -> 1.73 us  [weigh(): return weight.astype(jnp.float32) * stress]
    ppermute x8, starting transfers between devices: 18.7 us -> 17.5 us  [shift(): lax.ppermute(value, axis, [(i, (i + by) % size) for i in range(size)])]
    pallas_call x4 -> x5, Pallas kernels: 33.1 us -> 32.8 us  [call(): pl.pallas_call(kernel, out_shape=[jax.ShapeDtypeStruct(shape, jnp.float32...]
  transfers between devices with their start and end apart: 8 -> 8, of which waited for: 1 -> 2; matrix products, arithmetic and copies ran while one was open for 2% -> 0% of each run, Pallas kernels for 9% -> 13%
where the time goes in v10:
time: 80.2 us; the launch traced here: 80.1 us
  Pallas kernels  32.8 us (41%)
  blocking collectives  27 us (34%)
  starting transfers between devices  17.5 us (22%)
  other arithmetic  1.73 us (2%)
    pallas_call x5, Pallas kernels, call(): pl.pallas_call(kernel, out_shape=[jax.ShapeDtypeStruct(shape, jnp.float32...  32.8 us
    all_to_all x1, blocking collectives, local(): peaks = lax.all_to_all(peaks.reshape(devices, 1, nz), ('gx', 'gy'), 0, 0)  27 us
    ppermute x8, starting transfers between devices, shift(): lax.ppermute(value, axis, [(i, (i + by) % size) for i in range(size)])  17.5 us
    mul x2, other arithmetic, weigh(): return weight.astype(jnp.float32) * stress  1.73 us
  transfers between devices with their start and end apart: 8, of which 2 were waited for; matrix products, arithmetic and copies ran while one was open for 0% of the time, Pallas kernels for 13%

profile of v10, /device:TPU:1, one launch (start us, length us, event | category | flops | bytes accessed | tf_op | source)
XLA Modules:
  0.0 80.1 jit_solution(9508782276072750846)
XLA Ops:
  0.6 0.0 copy-start
  0.7 1.5 %slice_multiply_fusion = (f32[9,64,128]{2,1,0:T(8,128)S(1)}, f32[9,64,128]{2,1,0:T(8,128)S(1)}) fusion(f32[32,64,128]{2,1,0:T(8,128)} %param.4, s32[32,64,128]{2,1,0:T(8,128)} %param.5), kind=kLoop, calls=%fused_computation.1 | loop fusion | flops 737280 | bytes 1769472 | tf_op jit(solution)/shard_map/mul | solution.py:273
  2.2 2.2 %collective-permute-start.2 = (f32[9,64,128]{2,1,0:T(8,128)S(1)}, f32[9,64,128]{2,1,0:T(8,128)S(1)}, u32[]{:S(2)}, u32[]{:S(2)}) collective-permute-start(f32[9,64,128]{2,1,0:T(8,128)S(1)} %get-tuple-element.30), channel_id=1, source_target_pairs={{0,16},{16,32},{32,48},{48,64},{64,80},{80,96},{96,112},{112,128},... | collective-permute-start | bytes 884744 | tf_op jit(solution)/shard_map/ppermute | solution.py:509
  4.4 3.7 %collective-permute-start.3 = (f32[9,64,128]{2,1,0:T(8,128)S(1)}, f32[9,64,128]{2,1,0:T(8,128)S(1)}, u32[]{:S(2)}, u32[]{:S(2)}) collective-permute-start(f32[9,64,128]{2,1,0:T(8,128)S(1)} %get-tuple-element.31), channel_id=1, source_target_pairs={{0,240},{16,0},{32,16},{48,32},{64,48},{80,64},{96,80},{112,96},{1... | collective-permute-start | bytes 884744 | tf_op jit(solution)/shard_map/ppermute | solution.py:509
  8.1 0.1 collective-permute-start
  8.2 4.8 %collective-permute-start.1 = (f32[8,64,128]{2,1,0:T(8,128)S(1)}, f32[8,64,128]{2,1,0:T(8,128)S(1)}, u32[]{:S(2)}, u32[]{:S(2)}) collective-permute-start(f32[8,64,128]{2,1,0:T(8,128)S(1)} %get-tuple-element.17.low), channel_id=1, source_target_pairs={{0,240},{16,0},{32,16},{48,32},{64,48},{80,64},{96,80},{112,96},{1... | collective-permute-start | bytes 786440 | tf_op jit(solution)/shard_map/ppermute | solution.py:509
  13.0 3.1 %shard_map.50 = (f32[32,64,128]{2,1,0:T(8,128)S(1)}, f32[32,64,128]{2,1,0:T(8,128)S(1)}) custom-call(f32[32,64,128]{2,1,0:T(8,128)S(1)} %copy-done, f32[8,64,128]{2,1,0:T(8,128)S(1)} %get-tuple-element.17.low, f32[8,64,128]{2,1,0:T(8,128)S(1)} %get-tuple-element.16.high), custom_call_target="tpu_custom_call" | custom-call | tf_op jit(solution)/shard_map/pallas_call | solution.py:491
  16.1 0.2 select_multiply_fusion.source
  16.4 0.0 collective-permute-done.2.before
  16.4 0.0 collective-permute-done.3.after
  16.4 0.1 shard_map.51
  16.4 3.3 %collective-permute-start.5 = (f32[456,128]{1,0:T(8,128)S(1)}, f32[456,128]{1,0:T(8,128)S(1)}, u32[]{:S(2)}, u32[]{:S(2)}) collective-permute-start(f32[456,128]{1,0:T(8,128)S(1)} %get-tuple-element.20.order), channel_id=1, source_target_pairs={{0,15},{1,0},{2,1},{3,2},{4,3},{5,4},{6,5},{7,6},{8,7},{9,8},{10,9... | collective-permute-start | bytes 700424 | tf_op jit(solution)/shard_map/ppermute | solution.py:509
  19.7 0.0 collective-permute-start.4
  19.8 0.0 collective-permute-done.before
  19.8 0.0 collective-permute-done.1.after
  19.8 2.7 %collective-permute-start.6 = (f32[48,8,128]{2,1,0:T(8,128)S(1)}, f32[48,8,128]{2,1,0:T(8,128)S(1)}, u32[]{:S(2)}, u32[]{:S(2)}) collective-permute-start(f32[48,8,128]{2,1,0:T(8,128)S(1)} %get-tuple-element.21.order), channel_id=1, source_target_pairs={{0,15},{1,0},{2,1},{3,2},{4,3},{5,4},{6,5},{7,6},{8,7},{9,8},{10,9... | collective-permute-start | bytes 589832 | tf_op jit(solution)/shard_map/ppermute | solution.py:509
  22.5 0.7 collective-permute-start.7
  23.2 0.1 collective-permute-done.5.above
  23.3 0.1 collective-permute-done.4.below
  23.4 7.0 %shard_map.53 = (f32[42,96,128]{2,1,0:T(8,128)S(1)}, f32[32,64,128]{2,1,0:T(8,128)}, f32[256,128]{1,0:T(8,128)S(1)}) custom-call(f32[32,64,128]{2,1,0:T(8,128)S(1)} %select_multiply_fusion.source, f32[9,64,128]{2,1,0:T(8,128)S(1)} %collective-permute-done.2.before, f32[9,64,128]{2,1,0:T(8,128)S(1)} %collective-permute-done.3.after, ...), custom_call_target="tpu_custom_call" | custom-call | tf_op jit(solution)/shard_map/pallas_call | solution.py:491
  30.4 0.0 collective-permute-done.6.above
  30.5 0.0 collective-permute-done.7.below
  30.5 27.0 %all_to_all.5 = f32[256,1,128]{2,1,0:T(1,128)S(1)} all-to-all(f32[256,1,128]{2,1,0:T(1,128)S(1)} %bitcast.5), channel_id=1, replica_groups=mesh['gx'=16,'gy'=16] {'gx','gy'}, dimensions={0} | all-to-all | bytes 262144 | tf_op jit(solution)/shard_map/all_to_all | solution.py:549
  57.4 22.6 %shard_map.54 = f32[32,64,128]{2,1,0:T(8,128)} custom-call(f32[32,64,128]{2,1,0:T(8,128)S(1)} %copy-done, f32[8,64,128]{2,1,0:T(8,128)S(1)} %collective-permute-done.before, f32[8,64,128]{2,1,0:T(8,128)S(1)} %collective-permute-done.1.after, f32[48,8,128]{2,1,0:T(8,128)S(1)} %collective-permute-done.7.below, f32[48,8,128]{2,1,0:T(8,128)S(1)} %collective-permute-done.6.above, ...), custom_call_target="tpu_custom_call" | custom-call | tf_op jit(solution)/shard_map/pallas_call | solution.py:491
  (7 shorter events, 0.1 us)
Async XLA Ops:
  0.6 7.5 %copy-start = (f32[32,64,128]{2,1,0:T(8,128)S(1)}, f32[32,64,128]{2,1,0:T(8,128)}, u32[]{:S(2)}) copy-start(f32[32,64,128]{2,1,0:T(8,128)} %own_level.1) | copy-start | bytes 3145732
  0.6 15.5 %copy-start.1 = (f32[32,64,128]{2,1,0:T(8,128)S(1)}, f32[32,64,128]{2,1,0:T(8,128)}, u32[]{:S(2)}) copy-start(f32[32,64,128]{2,1,0:T(8,128)} %param.4) | copy-start | bytes 3145732
  0.6 15.5 %copy-start.2 = (s32[32,64,128]{2,1,0:T(8,128)S(1)}, s32[32,64,128]{2,1,0:T(8,128)}, u32[]{:S(2)}) copy-start(s32[32,64,128]{2,1,0:T(8,128)} %param.5) | copy-start | bytes 3145732
  2.2 14.2 %collective-permute-start.2 = (f32[9,64,128]{2,1,0:T(8,128)S(1)}, f32[9,64,128]{2,1,0:T(8,128)S(1)}, u32[]{:S(2)}, u32[]{:S(2)}) collective-permute-start(f32[9,64,128]{2,1,0:T(8,128)S(1)} %get-tuple-element.30), channel_id=1, source_target_pairs={{0,16},{16,32},{32,48},{48,64},{64,80},{80,96},{96,112},{112,128},... | collective-permute-start | bytes 884744 | tf_op jit(solution)/shard_map/ppermute | solution.py:509
  4.4 12.0 %collective-permute-start.3 = (f32[9,64,128]{2,1,0:T(8,128)S(1)}, f32[9,64,128]{2,1,0:T(8,128)S(1)}, u32[]{:S(2)}, u32[]{:S(2)}) collective-permute-start(f32[9,64,128]{2,1,0:T(8,128)S(1)} %get-tuple-element.31), channel_id=1, source_target_pairs={{0,240},{16,0},{32,16},{48,32},{64,48},{80,64},{96,80},{112,96},{1... | collective-permute-start | bytes 884744 | tf_op jit(solution)/shard_map/ppermute | solution.py:509
  8.1 11.6 %collective-permute-start = (f32[8,64,128]{2,1,0:T(8,128)S(1)}, f32[8,64,128]{2,1,0:T(8,128)S(1)}, u32[]{:S(2)}, u32[]{:S(2)}) collective-permute-start(f32[8,64,128]{2,1,0:T(8,128)S(1)} %get-tuple-element.16.high), channel_id=1, source_target_pairs={{0,16},{16,32},{32,48},{48,64},{64,80},{80,96},{96,112},{112,128},... | collective-permute-start | bytes 786440 | tf_op jit(solution)/shard_map/ppermute | solution.py:509
  8.2 11.5 %collective-permute-start.1 = (f32[8,64,128]{2,1,0:T(8,128)S(1)}, f32[8,64,128]{2,1,0:T(8,128)S(1)}, u32[]{:S(2)}, u32[]{:S(2)}) collective-permute-start(f32[8,64,128]{2,1,0:T(8,128)S(1)} %get-tuple-element.17.low), channel_id=1, source_target_pairs={{0,240},{16,0},{32,16},{48,32},{64,48},{80,64},{96,80},{112,96},{1... | collective-permute-start | bytes 786440 | tf_op jit(solution)/shard_map/ppermute | solution.py:509
  16.4 6.8 %collective-permute-start.5 = (f32[456,128]{1,0:T(8,128)S(1)}, f32[456,128]{1,0:T(8,128)S(1)}, u32[]{:S(2)}, u32[]{:S(2)}) collective-permute-start(f32[456,128]{1,0:T(8,128)S(1)} %get-tuple-element.20.order), channel_id=1, source_target_pairs={{0,15},{1,0},{2,1},{3,2},{4,3},{5,4},{6,5},{7,6},{8,7},{9,8},{10,9... | collective-permute-start | bytes 700424 | tf_op jit(solution)/shard_map/ppermute | solution.py:509
  19.7 3.7 %collective-permute-start.4 = (f32[456,128]{1,0:T(8,128)S(1)}, f32[456,128]{1,0:T(8,128)S(1)}, u32[]{:S(2)}, u32[]{:S(2)}) collective-permute-start(f32[456,128]{1,0:T(8,128)S(1)} %get-tuple-element.19), channel_id=1, source_target_pairs={{0,1},{1,2},{2,3},{3,4},{4,5},{5,6},{6,7},{7,8},{8,9},{9,10},{10,1... | collective-permute-start | bytes 700424 | tf_op jit(solution)/shard_map/ppermute | solution.py:509
  19.8 10.7 %collective-permute-start.6 = (f32[48,8,128]{2,1,0:T(8,128)S(1)}, f32[48,8,128]{2,1,0:T(8,128)S(1)}, u32[]{:S(2)}, u32[]{:S(2)}) collective-permute-start(f32[48,8,128]{2,1,0:T(8,128)S(1)} %get-tuple-element.21.order), channel_id=1, source_target_pairs={{0,15},{1,0},{2,1},{3,2},{4,3},{5,4},{6,5},{7,6},{8,7},{9,8},{10,9... | collective-permute-start | bytes 589832 | tf_op jit(solution)/shard_map/ppermute | solution.py:509
  22.5 8.0 %collective-permute-start.7 = (f32[48,8,128]{2,1,0:T(8,128)S(1)}, f32[48,8,128]{2,1,0:T(8,128)S(1)}, u32[]{:S(2)}, u32[]{:S(2)}) collective-permute-start(f32[48,8,128]{2,1,0:T(8,128)S(1)} %get-tuple-element.23), channel_id=1, source_target_pairs={{0,1},{1,2},{2,3},{3,4},{4,5},{5,6},{6,7},{7,8},{8,9},{9,10},{10,1... | collective-permute-start | bytes 589832 | tf_op jit(solution)/shard_map/ppermute | solution.py:509

commit v11 on v10

--- a/solution.py
+++ b/solution.py
@@ -181,7 +181,8 @@
             acc[i, t] = upwind_square(left, right, sign)
         return _
 
-    lax.fori_loop(0, step, along_x, 0)
+    if lanes is None:
+        lax.fori_loop(0, step, along_x, 0)
 
     def finish(x, t, total):
         velocity = strided(speed, sx + x, start + t, step)
@@ -197,11 +198,8 @@
 
         for t, left, right in weno_line(f, step):
             sign = sign_of(strided(speed, sx + x, start + t, step))
-            total = acc[x, t] + upwind_square(left, right, sign)
-            if lanes is None:
-                acc[x, t] = total
-            else:
-                finish(x, t, total + strided(lanes, x, start + t, step))
+            total = upwind_square(left, right, sign)
+            finish(x, t, total + strided(lanes, x, start + t, step))
         return _
 
     def along_yz(p, _):
@@ -252,16 +250,18 @@
             centre = f(t)
             base = strided(origin, ox + x, row, step)
             sign_field = base * lax.rsqrt(base * base + 1.0)
-            sign = sign_of(sign_field)
-            total = upwind_square(
-                centre - strided(field, fx + x - 1, row, step),
-                centre - strided(field, fx + x + 1, row, step),
-                sign,
+            sign = sign_of(base)
+            signed = sign * centre
+
+            def climb(low, high):
+                lowest = jnp.minimum(sign * low, sign * high)
+                return jnp.square(jnp.maximum(signed - lowest, 0.0))
+
+            total = climb(
+                strided(field, fx + x - 1, row, step), strided(field, fx + x + 1, row, step)
             )
-            total = total + upwind_square(centre - f(t - 1), centre - f(t + 1), sign)
-            total = total + upwind_square(
-                centre - along_lanes(centre, -1), centre - along_lanes(centre, 1), sign
-            )
+            total = total + climb(f(t - 1), f(t + 1))
+            total = total + climb(along_lanes(centre, -1), along_lanes(centre, 1))
             emit(x, t, centre - pseudo_step * sign_field * (root(total) - 1.0))
         return _
 
@@ -315,6 +315,17 @@
 
     piped(nx * rows // GROUP, GROUP, lambda g, j: level[tile(g, j)], compute, buffers)
 
+    def inner(n, _):
+        at = pl.ds(pl.multiple_of(n * 8, 8), 8)
+        for i, left, right in weno_line(lambda j: level[3 + j, at], nx - 6):
+            high = jnp.square(jnp.maximum(jnp.maximum(left, right), 0.0))
+            low_square = jnp.square(jnp.minimum(jnp.minimum(left, right), 0.0))
+            upper[3 + i, at] = upper[3 + i, at] + high
+            lower[3 + i, at] = lower[3 + i, at] + low_square
+        return _
+
+    lax.fori_loop(0, rows, inner, 0)
+
 
 def other_lanes(level, speed, upper, lower, lanes, buffers):
     nx, ny, _ = upper.shape
@@ -346,6 +357,25 @@
         return _
 
     lax.fori_loop(0, nx, own, 0, unroll=2)
+
+    def add_x(first, count, at):
+        for i, left, right in weno_line(lambda j: level[LEV - SPD + first + j, at], count):
+            x = first + i
+            lanes[x, at] = lanes[x, at] + upwind_square(left, right, sign_of(speed[x, at]))
+
+    def edges(n, _):
+        at = pl.ds(pl.multiple_of(OWN - 8 + n * (ny + 8), 8), 8)
+        add_x(0, planes, at)
+        return _
+
+    def sides(n, _):
+        at = pl.ds(pl.multiple_of(OWN + n * 8, 8), 8)
+        add_x(0, SPD + 3, at)
+        add_x(SPD + nx - 3, SPD + 3, at)
+        return _
+
+    lax.fori_loop(0, 2, edges, 0)
+    lax.fori_loop(0, rows, sides, 0)
 
 
 def velocity(

time: 80.2 us -> 78.7 us (0.981)
  blocking collectives: 27 us -> 25.4 us
    all_to_all x1, blocking collectives: 27 us -> 25.4 us  [local(): peaks = lax.all_to_all(peaks.reshape(devices, 1, nz), ('gx', 'gy'), 0, 0)]
  transfers between devices with their start and end apart: 8 -> 8, of which waited for: 2 -> 2; matrix products, arithmetic and copies ran while one was open for 0% -> 0% of each run, Pallas kernels for 13% -> 15%
where the time goes in v11:
time: 78.7 us; the launch traced here: 78.5 us
  Pallas kernels  32.9 us (42%)
  blocking collectives  25.4 us (32%)
  starting transfers between devices  16.8 us (21%)
  other arithmetic  1.73 us (2%)
  waiting for transfers between devices  0.94 us (1%)
    pallas_call x5, Pallas kernels, call(): pl.pallas_call(kernel, out_shape=[jax.ShapeDtypeStruct(shape, jnp.float32...  32.9 us
    all_to_all x1, blocking collectives, local(): peaks = lax.all_to_all(peaks.reshape(devices, 1, nz), ('gx', 'gy'), 0, 0)  25.4 us
    ppermute x8, starting transfers between devices, shift(): lax.ppermute(value, axis, [(i, (i + by) % size) for i in range(size)])  16.8 us
    mul x2, other arithmetic, weigh(): return weight.astype(jnp.float32) * stress  1.73 us
  transfers between devices with their start and end apart: 8, of which 2 were waited for; matrix products, arithmetic and copies ran while one was open for 0% of the time, Pallas kernels for 15%

profile of v11, /device:TPU:1, one launch (start us, length us, event | category | flops | bytes accessed | tf_op | source)
XLA Modules:
  0.0 78.5 jit_solution(18177425558126702555)
XLA Ops:
  0.6 0.0 copy-start
  0.7 1.5 %slice_multiply_fusion = (f32[9,64,128]{2,1,0:T(8,128)S(1)}, f32[9,64,128]{2,1,0:T(8,128)S(1)}) fusion(f32[32,64,128]{2,1,0:T(8,128)} %param.4, s32[32,64,128]{2,1,0:T(8,128)} %param.5), kind=kLoop, calls=%fused_computation.1 | loop fusion | flops 737280 | bytes 1769472 | tf_op jit(solution)/shard_map/mul | solution.py:273
  2.2 2.2 %collective-permute-start.2 = (f32[9,64,128]{2,1,0:T(8,128)S(1)}, f32[9,64,128]{2,1,0:T(8,128)S(1)}, u32[]{:S(2)}, u32[]{:S(2)}) collective-permute-start(f32[9,64,128]{2,1,0:T(8,128)S(1)} %get-tuple-element.30), channel_id=1, source_target_pairs={{0,16},{16,32},{32,48},{48,64},{64,80},{80,96},{96,112},{112,128},... | collective-permute-start | bytes 884744 | tf_op jit(solution)/shard_map/ppermute | solution.py:539
  4.4 3.7 %collective-permute-start.3 = (f32[9,64,128]{2,1,0:T(8,128)S(1)}, f32[9,64,128]{2,1,0:T(8,128)S(1)}, u32[]{:S(2)}, u32[]{:S(2)}) collective-permute-start(f32[9,64,128]{2,1,0:T(8,128)S(1)} %get-tuple-element.31), channel_id=1, source_target_pairs={{0,240},{16,0},{32,16},{48,32},{64,48},{80,64},{96,80},{112,96},{1... | collective-permute-start | bytes 884744 | tf_op jit(solution)/shard_map/ppermute | solution.py:539
  8.1 0.1 collective-permute-start
  8.2 4.8 %collective-permute-start.1 = (f32[8,64,128]{2,1,0:T(8,128)S(1)}, f32[8,64,128]{2,1,0:T(8,128)S(1)}, u32[]{:S(2)}, u32[]{:S(2)}) collective-permute-start(f32[8,64,128]{2,1,0:T(8,128)S(1)} %get-tuple-element.17.low), channel_id=1, source_target_pairs={{0,240},{16,0},{32,16},{48,32},{64,48},{80,64},{96,80},{112,96},{1... | collective-permute-start | bytes 786440 | tf_op jit(solution)/shard_map/ppermute | solution.py:539
  13.0 4.6 %shard_map.50 = (f32[32,64,128]{2,1,0:T(8,128)S(1)}, f32[32,64,128]{2,1,0:T(8,128)S(1)}) custom-call(f32[32,64,128]{2,1,0:T(8,128)S(1)} %copy-done, f32[8,64,128]{2,1,0:T(8,128)S(1)} %get-tuple-element.17.low, f32[8,64,128]{2,1,0:T(8,128)S(1)} %get-tuple-element.16.high), custom_call_target="tpu_custom_call" | custom-call | tf_op jit(solution)/shard_map/pallas_call | solution.py:521
  17.7 0.2 select_multiply_fusion.source
  17.9 0.0 collective-permute-done.2.before
  17.9 0.0 collective-permute-done.3.after
  17.9 0.1 shard_map.51
  18.0 3.3 %collective-permute-start.5 = (f32[456,128]{1,0:T(8,128)S(1)}, f32[456,128]{1,0:T(8,128)S(1)}, u32[]{:S(2)}, u32[]{:S(2)}) collective-permute-start(f32[456,128]{1,0:T(8,128)S(1)} %get-tuple-element.20.order), channel_id=1, source_target_pairs={{0,15},{1,0},{2,1},{3,2},{4,3},{5,4},{6,5},{7,6},{8,7},{9,8},{10,9... | collective-permute-start | bytes 700424 | tf_op jit(solution)/shard_map/ppermute | solution.py:539
  21.3 0.0 collective-permute-start.4
  21.3 0.0 collective-permute-done.before
  21.3 0.0 collective-permute-done.1.after
  21.3 2.7 %collective-permute-start.6 = (f32[48,8,128]{2,1,0:T(8,128)S(1)}, f32[48,8,128]{2,1,0:T(8,128)S(1)}, u32[]{:S(2)}, u32[]{:S(2)}) collective-permute-start(f32[48,8,128]{2,1,0:T(8,128)S(1)} %get-tuple-element.21.order), channel_id=1, source_target_pairs={{0,15},{1,0},{2,1},{3,2},{4,3},{5,4},{6,5},{7,6},{8,7},{9,8},{10,9... | collective-permute-start | bytes 589832 | tf_op jit(solution)/shard_map/ppermute | solution.py:539
  24.0 0.0 collective-permute-start.7
  24.0 0.8 %collective-permute-done.5.above = f32[456,128]{1,0:T(8,128)S(1)} collective-permute-done((f32[456,128]{1,0:T(8,128)S(1)}, f32[456,128]{1,0:T(8,128)S(1)}, u32[]{:S(2)}, u32[]{:S(2)}) %collective-permute-start.5) | collective-permute-done | bytes 233504 | tf_op jit(solution)/shard_map/ppermute | solution.py:539
  24.8 0.1 collective-permute-done.4.below
  24.9 7.0 %shard_map.53 = (f32[42,96,128]{2,1,0:T(8,128)S(1)}, f32[32,64,128]{2,1,0:T(8,128)}, f32[256,128]{1,0:T(8,128)S(1)}) custom-call(f32[32,64,128]{2,1,0:T(8,128)S(1)} %select_multiply_fusion.source, f32[9,64,128]{2,1,0:T(8,128)S(1)} %collective-permute-done.2.before, f32[9,64,128]{2,1,0:T(8,128)S(1)} %collective-permute-done.3.after, ...), custom_call_target="tpu_custom_call" | custom-call | tf_op jit(solution)/shard_map/pallas_call | solution.py:521
  32.0 0.0 collective-permute-done.6.above
  32.0 0.0 collective-permute-done.7.below
  32.0 25.4 %all_to_all.5 = f32[256,1,128]{2,1,0:T(1,128)S(1)} all-to-all(f32[256,1,128]{2,1,0:T(1,128)S(1)} %bitcast.5), channel_id=1, replica_groups=mesh['gx'=16,'gy'=16] {'gx','gy'}, dimensions={0} | all-to-all | bytes 262144 | tf_op jit(solution)/shard_map/all_to_all | solution.py:579
  57.4 21.1 %shard_map.54 = f32[32,64,128]{2,1,0:T(8,128)} custom-call(f32[32,64,128]{2,1,0:T(8,128)S(1)} %copy-done, f32[8,64,128]{2,1,0:T(8,128)S(1)} %collective-permute-done.before, f32[8,64,128]{2,1,0:T(8,128)S(1)} %collective-permute-done.1.after, f32[48,8,128]{2,1,0:T(8,128)S(1)} %collective-permute-done.7.below, f32[48,8,128]{2,1,0:T(8,128)S(1)} %collective-permute-done.6.above, ...), custom_call_target="tpu_custom_call" | custom-call | tf_op jit(solution)/shard_map/pallas_call | solution.py:521
  (7 shorter events, 0.1 us)
Async XLA Ops:
  0.6 7.5 %copy-start = (f32[32,64,128]{2,1,0:T(8,128)S(1)}, f32[32,64,128]{2,1,0:T(8,128)}, u32[]{:S(2)}) copy-start(f32[32,64,128]{2,1,0:T(8,128)} %own_level.1) | copy-start | bytes 3145732
  0.6 17.0 %copy-start.1 = (f32[32,64,128]{2,1,0:T(8,128)S(1)}, f32[32,64,128]{2,1,0:T(8,128)}, u32[]{:S(2)}) copy-start(f32[32,64,128]{2,1,0:T(8,128)} %param.4) | copy-start | bytes 3145732
  0.6 17.0 %copy-start.2 = (s32[32,64,128]{2,1,0:T(8,128)S(1)}, s32[32,64,128]{2,1,0:T(8,128)}, u32[]{:S(2)}) copy-start(s32[32,64,128]{2,1,0:T(8,128)} %param.5) | copy-start | bytes 3145732
  2.2 15.7 %collective-permute-start.2 = (f32[9,64,128]{2,1,0:T(8,128)S(1)}, f32[9,64,128]{2,1,0:T(8,128)S(1)}, u32[]{:S(2)}, u32[]{:S(2)}) collective-permute-start(f32[9,64,128]{2,1,0:T(8,128)S(1)} %get-tuple-element.30), channel_id=1, source_target_pairs={{0,16},{16,32},{32,48},{48,64},{64,80},{80,96},{96,112},{112,128},... | collective-permute-start | bytes 884744 | tf_op jit(solution)/shard_map/ppermute | solution.py:539
  4.4 13.5 %collective-permute-start.3 = (f32[9,64,128]{2,1,0:T(8,128)S(1)}, f32[9,64,128]{2,1,0:T(8,128)S(1)}, u32[]{:S(2)}, u32[]{:S(2)}) collective-permute-start(f32[9,64,128]{2,1,0:T(8,128)S(1)} %get-tuple-element.31), channel_id=1, source_target_pairs={{0,240},{16,0},{32,16},{48,32},{64,48},{80,64},{96,80},{112,96},{1... | collective-permute-start | bytes 884744 | tf_op jit(solution)/shard_map/ppermute | solution.py:539
  8.1 13.1 %collective-permute-start = (f32[8,64,128]{2,1,0:T(8,128)S(1)}, f32[8,64,128]{2,1,0:T(8,128)S(1)}, u32[]{:S(2)}, u32[]{:S(2)}) collective-permute-start(f32[8,64,128]{2,1,0:T(8,128)S(1)} %get-tuple-element.16.high), channel_id=1, source_target_pairs={{0,16},{16,32},{32,48},{48,64},{64,80},{80,96},{96,112},{112,128},... | collective-permute-start | bytes 786440 | tf_op jit(solution)/shard_map/ppermute | solution.py:539
  8.2 13.1 %collective-permute-start.1 = (f32[8,64,128]{2,1,0:T(8,128)S(1)}, f32[8,64,128]{2,1,0:T(8,128)S(1)}, u32[]{:S(2)}, u32[]{:S(2)}) collective-permute-start(f32[8,64,128]{2,1,0:T(8,128)S(1)} %get-tuple-element.17.low), channel_id=1, source_target_pairs={{0,240},{16,0},{32,16},{48,32},{64,48},{80,64},{96,80},{112,96},{1... | collective-permute-start | bytes 786440 | tf_op jit(solution)/shard_map/ppermute | solution.py:539
  18.0 6.8 %collective-permute-start.5 = (f32[456,128]{1,0:T(8,128)S(1)}, f32[456,128]{1,0:T(8,128)S(1)}, u32[]{:S(2)}, u32[]{:S(2)}) collective-permute-start(f32[456,128]{1,0:T(8,128)S(1)} %get-tuple-element.20.order), channel_id=1, source_target_pairs={{0,15},{1,0},{2,1},{3,2},{4,3},{5,4},{6,5},{7,6},{8,7},{9,8},{10,9... | collective-permute-start | bytes 700424 | tf_op jit(solution)/shard_map/ppermute | solution.py:539
  21.3 3.7 %collective-permute-start.4 = (f32[456,128]{1,0:T(8,128)S(1)}, f32[456,128]{1,0:T(8,128)S(1)}, u32[]{:S(2)}, u32[]{:S(2)}) collective-permute-start(f32[456,128]{1,0:T(8,128)S(1)} %get-tuple-element.19), channel_id=1, source_target_pairs={{0,1},{1,2},{2,3},{3,4},{4,5},{5,6},{6,7},{7,8},{8,9},{9,10},{10,1... | collective-permute-start | bytes 700424 | tf_op jit(solution)/shard_map/ppermute | solution.py:539
  21.3 10.7 %collective-permute-start.6 = (f32[48,8,128]{2,1,0:T(8,128)S(1)}, f32[48,8,128]{2,1,0:T(8,128)S(1)}, u32[]{:S(2)}, u32[]{:S(2)}) collective-permute-start(f32[48,8,128]{2,1,0:T(8,128)S(1)} %get-tuple-element.21.order), channel_id=1, source_target_pairs={{0,15},{1,0},{2,1},{3,2},{4,3},{5,4},{6,5},{7,6},{8,7},{9,8},{10,9... | collective-permute-start | bytes 589832 | tf_op jit(solution)/shard_map/ppermute | solution.py:539
  24.0 8.0 %collective-permute-start.7 = (f32[48,8,128]{2,1,0:T(8,128)S(1)}, f32[48,8,128]{2,1,0:T(8,128)S(1)}, u32[]{:S(2)}, u32[]{:S(2)}) collective-permute-start(f32[48,8,128]{2,1,0:T(8,128)S(1)} %get-tuple-element.23), channel_id=1, source_target_pairs={{0,1},{1,2},{2,3},{3,4},{4,5},{5,6},{6,7},{7,8},{8,9},{9,10},{10,1... | collective-permute-start | bytes 589832 | tf_op jit(solution)/shard_map/ppermute | solution.py:539

commit v12 on v11

--- a/solution.py
+++ b/solution.py
@@ -419,7 +419,8 @@
                 new[x - shift, pl.ds(start + t, 8, stride=step), :] = beside + constant * own
             return _
 
-        lax.fori_loop(lo, hi, body, 0, unroll=11)
+        unroll = min(range(14, 8, -1), key=lambda u: (hi - lo) % u)
+        lax.fori_loop(lo, hi, body, 0, unroll=unroll)
 
     sweep(src, one, 0, 1, wide - 1, coefficients[4], coefficients[3])
     sweep(one, two, 0, 2, wide - 2, None, coefficients[2])

time: 78.7 us -> 77.7 us (0.987)
  Pallas kernels: 32.9 us -> 31.9 us
    pallas_call x5, Pallas kernels: 32.9 us -> 31.9 us  [call(): pl.pallas_call(kernel, out_shape=[jax.ShapeDtypeStruct(shape, jnp.float32...]
  transfers between devices with their start and end apart: 8 -> 8, of which waited for: 2 -> 2; matrix products, arithmetic and copies ran while one was open for 0% -> 0% of each run, Pallas kernels for 15% -> 14%
where the time goes in v12:
time: 77.7 us; the launch traced here: 77.6 us
  Pallas kernels  31.9 us (41%)
  blocking collectives  25.4 us (33%)
  starting transfers between devices  16.8 us (22%)
  other arithmetic  1.73 us (2%)
  waiting for transfers between devices  0.94 us (1%)
    pallas_call x5, Pallas kernels, call(): pl.pallas_call(kernel, out_shape=[jax.ShapeDtypeStruct(shape, jnp.float32...  31.9 us
    all_to_all x1, blocking collectives, local(): peaks = lax.all_to_all(peaks.reshape(devices, 1, nz), ('gx', 'gy'), 0, 0)  25.4 us
    ppermute x8, starting transfers between devices, shift(): lax.ppermute(value, axis, [(i, (i + by) % size) for i in range(size)])  16.8 us
    mul x2, other arithmetic, weigh(): return weight.astype(jnp.float32) * stress  1.73 us
  transfers between devices with their start and end apart: 8, of which 2 were waited for; matrix products, arithmetic and copies ran while one was open for 0% of the time, Pallas kernels for 14%

profile of v12, /device:TPU:1, one launch (start us, length us, event | category | flops | bytes accessed | tf_op | source)
XLA Modules:
  0.0 77.6 jit_solution(16080850085314693250)
XLA Ops:
  0.6 0.0 copy-start
  0.7 1.5 %slice_multiply_fusion = (f32[9,64,128]{2,1,0:T(8,128)S(1)}, f32[9,64,128]{2,1,0:T(8,128)S(1)}) fusion(f32[32,64,128]{2,1,0:T(8,128)} %param.4, s32[32,64,128]{2,1,0:T(8,128)} %param.5), kind=kLoop, calls=%fused_computation.1 | loop fusion | flops 737280 | bytes 1769472 | tf_op jit(solution)/shard_map/mul | solution.py:273
  2.2 2.2 %collective-permute-start.2 = (f32[9,64,128]{2,1,0:T(8,128)S(1)}, f32[9,64,128]{2,1,0:T(8,128)S(1)}, u32[]{:S(2)}, u32[]{:S(2)}) collective-permute-start(f32[9,64,128]{2,1,0:T(8,128)S(1)} %get-tuple-element.30), channel_id=1, source_target_pairs={{0,16},{16,32},{32,48},{48,64},{64,80},{80,96},{96,112},{112,128},... | collective-permute-start | bytes 884744 | tf_op jit(solution)/shard_map/ppermute | solution.py:540
  4.4 3.7 %collective-permute-start.3 = (f32[9,64,128]{2,1,0:T(8,128)S(1)}, f32[9,64,128]{2,1,0:T(8,128)S(1)}, u32[]{:S(2)}, u32[]{:S(2)}) collective-permute-start(f32[9,64,128]{2,1,0:T(8,128)S(1)} %get-tuple-element.31), channel_id=1, source_target_pairs={{0,240},{16,0},{32,16},{48,32},{64,48},{80,64},{96,80},{112,96},{1... | collective-permute-start | bytes 884744 | tf_op jit(solution)/shard_map/ppermute | solution.py:540
  8.1 0.1 collective-permute-start
  8.2 4.8 %collective-permute-start.1 = (f32[8,64,128]{2,1,0:T(8,128)S(1)}, f32[8,64,128]{2,1,0:T(8,128)S(1)}, u32[]{:S(2)}, u32[]{:S(2)}) collective-permute-start(f32[8,64,128]{2,1,0:T(8,128)S(1)} %get-tuple-element.17.low), channel_id=1, source_target_pairs={{0,240},{16,0},{32,16},{48,32},{64,48},{80,64},{96,80},{112,96},{1... | collective-permute-start | bytes 786440 | tf_op jit(solution)/shard_map/ppermute | solution.py:540
  13.0 4.6 %shard_map.50 = (f32[32,64,128]{2,1,0:T(8,128)S(1)}, f32[32,64,128]{2,1,0:T(8,128)S(1)}) custom-call(f32[32,64,128]{2,1,0:T(8,128)S(1)} %copy-done, f32[8,64,128]{2,1,0:T(8,128)S(1)} %get-tuple-element.17.low, f32[8,64,128]{2,1,0:T(8,128)S(1)} %get-tuple-element.16.high), custom_call_target="tpu_custom_call" | custom-call | tf_op jit(solution)/shard_map/pallas_call | solution.py:522
  17.7 0.2 select_multiply_fusion.source
  17.9 0.0 collective-permute-done.2.before
  17.9 0.0 collective-permute-done.3.after
  17.9 0.1 shard_map.51
  18.0 3.3 %collective-permute-start.5 = (f32[456,128]{1,0:T(8,128)S(1)}, f32[456,128]{1,0:T(8,128)S(1)}, u32[]{:S(2)}, u32[]{:S(2)}) collective-permute-start(f32[456,128]{1,0:T(8,128)S(1)} %get-tuple-element.20.order), channel_id=1, source_target_pairs={{0,15},{1,0},{2,1},{3,2},{4,3},{5,4},{6,5},{7,6},{8,7},{9,8},{10,9... | collective-permute-start | bytes 700424 | tf_op jit(solution)/shard_map/ppermute | solution.py:540
  21.3 0.0 collective-permute-start.4
  21.3 0.0 collective-permute-done.before
  21.3 0.0 collective-permute-done.1.after
  21.3 2.7 %collective-permute-start.6 = (f32[48,8,128]{2,1,0:T(8,128)S(1)}, f32[48,8,128]{2,1,0:T(8,128)S(1)}, u32[]{:S(2)}, u32[]{:S(2)}) collective-permute-start(f32[48,8,128]{2,1,0:T(8,128)S(1)} %get-tuple-element.21.order), channel_id=1, source_target_pairs={{0,15},{1,0},{2,1},{3,2},{4,3},{5,4},{6,5},{7,6},{8,7},{9,8},{10,9... | collective-permute-start | bytes 589832 | tf_op jit(solution)/shard_map/ppermute | solution.py:540
  24.0 0.0 collective-permute-start.7
  24.0 0.8 %collective-permute-done.5.above = f32[456,128]{1,0:T(8,128)S(1)} collective-permute-done((f32[456,128]{1,0:T(8,128)S(1)}, f32[456,128]{1,0:T(8,128)S(1)}, u32[]{:S(2)}, u32[]{:S(2)}) %collective-permute-start.5) | collective-permute-done | bytes 233504 | tf_op jit(solution)/shard_map/ppermute | solution.py:540
  24.8 0.1 collective-permute-done.4.below
  24.9 6.1 %shard_map.53 = (f32[42,96,128]{2,1,0:T(8,128)S(1)}, f32[32,64,128]{2,1,0:T(8,128)}, f32[256,128]{1,0:T(8,128)S(1)}) custom-call(f32[32,64,128]{2,1,0:T(8,128)S(1)} %select_multiply_fusion.source, f32[9,64,128]{2,1,0:T(8,128)S(1)} %collective-permute-done.2.before, f32[9,64,128]{2,1,0:T(8,128)S(1)} %collective-permute-done.3.after, ...), custom_call_target="tpu_custom_call" | custom-call | tf_op jit(solution)/shard_map/pallas_call | solution.py:522
  31.1 0.0 collective-permute-done.6.above
  31.1 0.0 collective-permute-done.7.below
  31.1 25.4 %all_to_all.5 = f32[256,1,128]{2,1,0:T(1,128)S(1)} all-to-all(f32[256,1,128]{2,1,0:T(1,128)S(1)} %bitcast.5), channel_id=1, replica_groups=mesh['gx'=16,'gy'=16] {'gx','gy'}, dimensions={0} | all-to-all | bytes 262144 | tf_op jit(solution)/shard_map/all_to_all | solution.py:580
  56.5 21.1 %shard_map.54 = f32[32,64,128]{2,1,0:T(8,128)} custom-call(f32[32,64,128]{2,1,0:T(8,128)S(1)} %copy-done, f32[8,64,128]{2,1,0:T(8,128)S(1)} %collective-permute-done.before, f32[8,64,128]{2,1,0:T(8,128)S(1)} %collective-permute-done.1.after, f32[48,8,128]{2,1,0:T(8,128)S(1)} %collective-permute-done.7.below, f32[48,8,128]{2,1,0:T(8,128)S(1)} %collective-permute-done.6.above, ...), custom_call_target="tpu_custom_call" | custom-call | tf_op jit(solution)/shard_map/pallas_call | solution.py:522
  (7 shorter events, 0.1 us)
Async XLA Ops:
  0.6 7.5 %copy-start = (f32[32,64,128]{2,1,0:T(8,128)S(1)}, f32[32,64,128]{2,1,0:T(8,128)}, u32[]{:S(2)}) copy-start(f32[32,64,128]{2,1,0:T(8,128)} %own_level.1) | copy-start | bytes 3145732
  0.6 17.0 %copy-start.1 = (f32[32,64,128]{2,1,0:T(8,128)S(1)}, f32[32,64,128]{2,1,0:T(8,128)}, u32[]{:S(2)}) copy-start(f32[32,64,128]{2,1,0:T(8,128)} %param.4) | copy-start | bytes 3145732
  0.6 17.0 %copy-start.2 = (s32[32,64,128]{2,1,0:T(8,128)S(1)}, s32[32,64,128]{2,1,0:T(8,128)}, u32[]{:S(2)}) copy-start(s32[32,64,128]{2,1,0:T(8,128)} %param.5) | copy-start | bytes 3145732
  2.2 15.7 %collective-permute-start.2 = (f32[9,64,128]{2,1,0:T(8,128)S(1)}, f32[9,64,128]{2,1,0:T(8,128)S(1)}, u32[]{:S(2)}, u32[]{:S(2)}) collective-permute-start(f32[9,64,128]{2,1,0:T(8,128)S(1)} %get-tuple-element.30), channel_id=1, source_target_pairs={{0,16},{16,32},{32,48},{48,64},{64,80},{80,96},{96,112},{112,128},... | collective-permute-start | bytes 884744 | tf_op jit(solution)/shard_map/ppermute | solution.py:540
  4.4 13.5 %collective-permute-start.3 = (f32[9,64,128]{2,1,0:T(8,128)S(1)}, f32[9,64,128]{2,1,0:T(8,128)S(1)}, u32[]{:S(2)}, u32[]{:S(2)}) collective-permute-start(f32[9,64,128]{2,1,0:T(8,128)S(1)} %get-tuple-element.31), channel_id=1, source_target_pairs={{0,240},{16,0},{32,16},{48,32},{64,48},{80,64},{96,80},{112,96},{1... | collective-permute-start | bytes 884744 | tf_op jit(solution)/shard_map/ppermute | solution.py:540
  8.1 13.1 %collective-permute-start = (f32[8,64,128]{2,1,0:T(8,128)S(1)}, f32[8,64,128]{2,1,0:T(8,128)S(1)}, u32[]{:S(2)}, u32[]{:S(2)}) collective-permute-start(f32[8,64,128]{2,1,0:T(8,128)S(1)} %get-tuple-element.16.high), channel_id=1, source_target_pairs={{0,16},{16,32},{32,48},{48,64},{64,80},{80,96},{96,112},{112,128},... | collective-permute-start | bytes 786440 | tf_op jit(solution)/shard_map/ppermute | solution.py:540
  8.2 13.1 %collective-permute-start.1 = (f32[8,64,128]{2,1,0:T(8,128)S(1)}, f32[8,64,128]{2,1,0:T(8,128)S(1)}, u32[]{:S(2)}, u32[]{:S(2)}) collective-permute-start(f32[8,64,128]{2,1,0:T(8,128)S(1)} %get-tuple-element.17.low), channel_id=1, source_target_pairs={{0,240},{16,0},{32,16},{48,32},{64,48},{80,64},{96,80},{112,96},{1... | collective-permute-start | bytes 786440 | tf_op jit(solution)/shard_map/ppermute | solution.py:540
  18.0 6.8 %collective-permute-start.5 = (f32[456,128]{1,0:T(8,128)S(1)}, f32[456,128]{1,0:T(8,128)S(1)}, u32[]{:S(2)}, u32[]{:S(2)}) collective-permute-start(f32[456,128]{1,0:T(8,128)S(1)} %get-tuple-element.20.order), channel_id=1, source_target_pairs={{0,15},{1,0},{2,1},{3,2},{4,3},{5,4},{6,5},{7,6},{8,7},{9,8},{10,9... | collective-permute-start | bytes 700424 | tf_op jit(solution)/shard_map/ppermute | solution.py:540
  21.3 3.7 %collective-permute-start.4 = (f32[456,128]{1,0:T(8,128)S(1)}, f32[456,128]{1,0:T(8,128)S(1)}, u32[]{:S(2)}, u32[]{:S(2)}) collective-permute-start(f32[456,128]{1,0:T(8,128)S(1)} %get-tuple-element.19), channel_id=1, source_target_pairs={{0,1},{1,2},{2,3},{3,4},{4,5},{5,6},{6,7},{7,8},{8,9},{9,10},{10,1... | collective-permute-start | bytes 700424 | tf_op jit(solution)/shard_map/ppermute | solution.py:540
  21.3 9.7 %collective-permute-start.6 = (f32[48,8,128]{2,1,0:T(8,128)S(1)}, f32[48,8,128]{2,1,0:T(8,128)S(1)}, u32[]{:S(2)}, u32[]{:S(2)}) collective-permute-start(f32[48,8,128]{2,1,0:T(8,128)S(1)} %get-tuple-element.21.order), channel_id=1, source_target_pairs={{0,15},{1,0},{2,1},{3,2},{4,3},{5,4},{6,5},{7,6},{8,7},{9,8},{10,9... | collective-permute-start | bytes 589832 | tf_op jit(solution)/shard_map/ppermute | solution.py:540
  24.0 7.1 %collective-permute-start.7 = (f32[48,8,128]{2,1,0:T(8,128)S(1)}, f32[48,8,128]{2,1,0:T(8,128)S(1)}, u32[]{:S(2)}, u32[]{:S(2)}) collective-permute-start(f32[48,8,128]{2,1,0:T(8,128)S(1)} %get-tuple-element.23), channel_id=1, source_target_pairs={{0,1},{1,2},{2,3},{3,4},{4,5},{5,6},{6,7},{7,8},{8,9},{9,10},{10,1... | collective-permute-start | bytes 589832 | tf_op jit(solution)/shard_map/ppermute | solution.py:540
